TPU v7x, 128 devices: a whole 4x4x4 slice. The times are simulated.
128 devices in a mesh: ctx: 8 (over z, x_lo), exp: 16 (over y, x_hi, core).
Axes of the slice: x: 4 (x_hi: 2, x_lo: 2; x = x_hi * 2 + x_lo), y: 4, z: 4, core: 2. Of those that a mesh axis runs over, the one named last changes fastest.
Arguments:
- tokens: bfloat16 [16, 1024, 1024], P('exp', 'ctx'), may hold values from -6 to 6
- cotangent: bfloat16 [16, 1024, 1024], P('exp', 'ctx'), may hold values from -6 to 6
- routes: int32 [16, 1024, 8], P('exp', 'ctx'), may hold values from 0 to 31, all different within a row; in each aligned block of 128 rows (0 to 127, 128 to 255, ..., all dimensions but the last counted through in order) at most 48 rows name the same one
- query_weight: bfloat16 [1024, 1024], P(None, 'exp'), may hold values from -0.25 to 0.25
- kv_weight: bfloat16 [1024, 1024], P(None, 'exp'), may hold values from -0.25 to 0.25
- output_weight: bfloat16 [1024, 1024], P(None, 'exp'), may hold values from -1 to 1
- router: float32 [1024, 32], P(None, 'exp'), may hold values from -0.09375 to 0.09375
- gains: float32 [2, 1024], P(None, 'exp'), may hold values from 0.5 to 1.5
- gate_weight: bfloat16 [32, 1024, 512], P('exp', 'ctx'), may hold values from -0.1875 to 0.1875
- up_weight: bfloat16 [32, 1024, 512], P('exp', 'ctx'), may hold values from -0.1875 to 0.1875
- down_weight: bfloat16 [32, 1024, 512], P('exp', 'ctx'), may hold values from -0.75 to 0.75
- query_momentum: float32 [1024, 1024], P(None, 'exp'), may hold values from -224 to 224
- kv_momentum: float32 [1024, 1024], P(None, 'exp'), may hold values from -224 to 224
- output_momentum: float32 [1024, 1024], P(None, 'exp'), may hold values from -112 to 112
- gate_momentum: float32 [32, 1024, 512], P('exp', 'ctx'), may hold values from -112 to 112
- up_momentum: float32 [32, 1024, 512], P('exp', 'ctx'), may hold values from -112 to 112
- down_momentum: float32 [32, 1024, 512], P('exp', 'ctx'), may hold values from -32 to 32
- router_first: float32 [1024, 32], P(None, 'exp'), may hold values from -320 to 320
- router_second: float32 [1024, 32], P(None, 'exp'), may hold values from 10240 to 40960
- gains_first: float32 [2, 1024], P(None, 'exp'), may hold values from -160 to 160
- gains_second: float32 [2, 1024], P(None, 'exp'), may hold values from 3276.8 to 13107.2
Outputs:
- block_out: bfloat16 [16, 1024, 1024], P('exp', 'ctx')
- input_grad: float32 [16, 1024, 1024], P('exp', 'ctx')
- query_momentum_new: float32 [1024, 1024], P(None, 'exp')
- query_new: float32 [1024, 1024], P(None, 'exp')
- kv_momentum_new: float32 [1024, 1024], P(None, 'exp')
- kv_new: float32 [1024, 1024], P(None, 'exp')
- output_momentum_new: float32 [1024, 1024], P(None, 'exp')
- output_new: float32 [1024, 1024], P(None, 'exp')
- gate_momentum_new: float32 [32, 1024, 512], P('exp', 'ctx')
- gate_new: float32 [32, 1024, 512], P('exp', 'ctx')
- up_momentum_new: float32 [32, 1024, 512], P('exp', 'ctx')
- up_new: float32 [32, 1024, 512], P('exp', 'ctx')
- down_momentum_new: float32 [32, 1024, 512], P('exp', 'ctx')
- down_new: float32 [32, 1024, 512], P('exp', 'ctx')
- router_first_new: float32 [1024, 32], P(None, 'exp')
- router_second_new: float32 [1024, 32], P(None, 'exp')
- router_new: float32 [1024, 32], P(None, 'exp')
- gains_first_new: float32 [2, 1024], P(None, 'exp')
- gains_second_new: float32 [2, 1024], P(None, 'exp')
- gains_new: float32 [2, 1024], P(None, 'exp')
Inputs may be any that keep to these rules, and one draw needn't show every extreme that they name: `routes`: each token names 8 different experts. Among the tokens of one device, in sequence order, no expert is named by more than 48 tokens, a bound that some block reaches.
All inputs are finite; a program needn't handle non-finite values.
Results may differ from a plain program's by a relative error of at most 0.015.
The roundings to bfloat16 on the way count: a program that leaves them out, or rounds other values in their place, can miss the bound.
Values may be sent and summed in bfloat16 or wider, within the bound.
No kernel may reach another device: no remote copies, remote signals or barrier semaphores. Data moves between devices by JAX's collectives and lax.ppermute only.
A program may use at most 192 MiB of HBM per device.

v0:
```python
import math

import jax
import jax.numpy as jnp
from jax import lax
from jax.sharding import PartitionSpec as P

D = 1024
HEADS = 16
KV = 8
HD = 64
TOP = 8
STEP = 10


eps_norm = 1e-05
rope_base = 10000.0
mom_rate = 0.95
muon_rate = 0.15
decay_rate = 0.1
adam_one = 0.9
adam_two = 0.95
adam_eps = 1e-08
router_rate = 0.015
gain_rate = 0.2
coef_one = 3.4445
coef_two = -4.775
coef_three = 2.0315
highest = lax.Precision.HIGHEST


def rope_tables(first_row, token_count):
    half_width = HD // 2
    frequency = rope_base ** (-jnp.arange(half_width, dtype=jnp.float32) * 2.0 / HD)
    position = (first_row + jnp.arange(token_count, dtype=jnp.int32)).astype(jnp.float32)
    angle_grid = position[:, None] * frequency[None, :]
    return (jnp.cos(angle_grid), jnp.sin(angle_grid))


def rotate(vector, cosine, sine):
    half_width = vector.shape[-1] // 2
    front_half = vector[..., :half_width]
    back_half = vector[..., half_width:]
    cos_rows = cosine[:, None, :]
    sin_rows = sine[:, None, :]
    return jnp.concatenate(
        [
            front_half * cos_rows - back_half * sin_rows,
            back_half * cos_rows + front_half * sin_rows,
        ],
        axis=-1,
    )


def orthogonalize(matrices):
    magnitude = jnp.sqrt(jnp.sum(matrices * matrices, axis=(-2, -1), keepdims=True))
    matrices = matrices / (magnitude + 1e-07)
    for iteration in range(5):
        gram_mat = jnp.einsum("bij,bkj->bik", matrices, matrices, precision=highest)
        poly_term = coef_two * gram_mat + coef_three * jnp.einsum(
            "bij,bjk->bik", gram_mat, gram_mat, precision=highest
        )
        matrices = coef_one * matrices + jnp.einsum(
            "bij,bjk->bik", poly_term, matrices, precision=highest
        )
    return matrices


def owner_orthogonal(stacked):
    return jnp.swapaxes(orthogonalize(jnp.swapaxes(stacked, 1, 2)), 1, 2)


def step_weight(weight, ortho):
    return (
        weight.astype(jnp.float32) * (1.0 - muon_rate * decay_rate)
        - muon_rate * 0.2 * math.sqrt(D) * ortho
    )


def head_update(weight, momentum, grad):
    fresh = mom_rate * momentum + grad
    row_count, col_count = fresh.shape
    blocks = jnp.transpose(fresh.reshape(row_count, col_count // HD, HD), (1, 2, 0))
    ortho = jnp.transpose(orthogonalize(blocks), (2, 0, 1)).reshape(row_count, col_count)
    return (fresh, step_weight(weight, ortho))


def adam_update(param, first, second, grad, rate, decay):
    first = adam_one * first + (1.0 - adam_one) * grad
    second = adam_two * second + (1.0 - adam_two) * grad * grad
    fixed_one = first / (1.0 - adam_one**STEP)
    fixed_two = second / (1.0 - adam_two**STEP)
    return (
        first,
        second,
        param * (1.0 - rate * decay) - rate * fixed_one / (jnp.sqrt(fixed_two) + adam_eps),
    )


def dispatch(row_buffer):
    return lax.all_to_all(row_buffer, "exp", split_axis=0, concat_axis=0, tiled=True)


def combine(row_buffer):
    return lax.all_to_all(row_buffer, "exp", split_axis=0, concat_axis=0, tiled=True)


def to_owners(stacked):
    return lax.all_to_all(stacked, "ctx", split_axis=0, concat_axis=1, tiled=True)


def pad_slots(stacked, slot_total):
    extra = slot_total - stacked.shape[0]
    return jnp.concatenate(
        [stacked, jnp.zeros((extra,) + stacked.shape[1:], stacked.dtype)], axis=0
    )


def contract_rows(left, right):
    return lax.dot_general(
        left, right, (((0,), (0,)), ((), ())), preferred_element_type=jnp.float32
    )


def contract_cols(left, right):
    return lax.dot_general(
        left, right, (((1,), (1,)), ((), ())), preferred_element_type=jnp.float32
    )


def body(
    tokens,
    cotangent,
    routes,
    query_weight,
    kv_weight,
    output_weight,
    router,
    gains,
    gate_weight,
    up_weight,
    down_weight,
    query_momentum,
    kv_momentum,
    output_momentum,
    gate_momentum,
    up_momentum,
    down_momentum,
    router_first,
    router_second,
    gains_first,
    gains_second,
):
    ctx_count = lax.axis_size("ctx")
    exp_count = lax.axis_size("exp")
    row_count = tokens.shape[1]
    model_width = tokens.shape[2]
    inputs = tokens[0].astype(jnp.float32)
    grad_out = cotangent[0].astype(jnp.float32)
    route_ids = routes[0]
    full_query, full_kv, full_output, full_router, full_gains = (
        lax.all_gather(query_weight, "exp", axis=1, tiled=True),
        lax.all_gather(kv_weight, "exp", axis=1, tiled=True),
        lax.all_gather(output_weight, "exp", axis=1, tiled=True),
        lax.all_gather(router.astype(jnp.bfloat16), "exp", axis=1, tiled=True),
        lax.all_gather(gains.astype(jnp.bfloat16), "exp", axis=1, tiled=True),
    )
    full_gate, full_up, full_down = (
        lax.all_gather(gate_weight, "ctx", axis=1, tiled=True),
        lax.all_gather(up_weight, "ctx", axis=1, tiled=True),
        lax.all_gather(down_weight, "ctx", axis=1, tiled=True),
    )
    gain_one = full_gains[0].astype(jnp.float32)
    gain_two = full_gains[1].astype(jnp.float32)
    inv_one = lax.rsqrt(jnp.mean(inputs * inputs, axis=-1, keepdims=True) + eps_norm)
    normed_one = (inputs * inv_one * gain_one).astype(jnp.bfloat16)
    query_raw = jnp.dot(normed_one, full_query, preferred_element_type=jnp.float32)
    kv_raw = jnp.dot(normed_one, full_kv, preferred_element_type=jnp.float32)
    first_row = lax.axis_index("ctx") * row_count
    cosine, sine = rope_tables(first_row, row_count)
    queries = rotate(query_raw.reshape(row_count, HEADS, HD), cosine, sine).astype(jnp.bfloat16)
    keys = (
        rotate(kv_raw[:, : KV * HD].reshape(row_count, KV, HD), cosine, sine)
        .astype(jnp.bfloat16)
        .reshape(row_count, KV * HD)
    )
    values = kv_raw[:, KV * HD :].astype(jnp.bfloat16)
    all_keys, all_values = (
        lax.all_gather(keys, "ctx", axis=0, tiled=True),
        lax.all_gather(values, "ctx", axis=0, tiled=True),
    )
    key_count = all_keys.shape[0]
    group_size = HEADS // KV
    score_scale = HD ** (-0.5)
    query_groups = queries.reshape(row_count, KV, group_size, HD)
    key_heads = all_keys.reshape(key_count, KV, HD)
    value_heads = all_values.reshape(key_count, KV, HD)
    scores = (
        jnp.einsum("ikgd,jkd->kgij", query_groups, key_heads, preferred_element_type=jnp.float32)
        * score_scale
    )
    causal = jnp.arange(key_count)[None, :] <= (first_row + jnp.arange(row_count))[:, None]
    scores = jnp.where(causal, scores, -1e30)
    running_max = jnp.max(scores, axis=-1, keepdims=True)
    log_total = running_max + jnp.log(
        jnp.sum(jnp.exp(scores - running_max), axis=-1, keepdims=True)
    )
    weights_full = jnp.exp(scores - log_total)
    weights_low = weights_full.astype(jnp.bfloat16)
    mixed = jnp.einsum(
        "kgij,jkd->ikgd", weights_low, value_heads, preferred_element_type=jnp.float32
    )
    mixed_low = mixed.reshape(row_count, HEADS * HD).astype(jnp.bfloat16)
    attended = contract_cols(mixed_low, full_output)
    residual = inputs + attended
    inv_two = lax.rsqrt(jnp.mean(residual * residual, axis=-1, keepdims=True) + eps_norm)
    normed_two = (residual * inv_two * gain_two).astype(jnp.bfloat16)
    logits = jnp.dot(normed_two, full_router, preferred_element_type=jnp.float32)
    expert_count = full_router.shape[1]
    per_group = expert_count // exp_count
    capacity = max(2, 3 * row_count * TOP // (2 * expert_count))
    expert_ids = jnp.arange(expert_count, dtype=jnp.int32)
    route_match = route_ids[:, :, None] == expert_ids[None, None, :]
    chosen = jnp.sum(jnp.where(route_match, logits[:, None, :], 0.0), axis=-1)
    gate_weights = jax.nn.softmax(chosen, axis=-1)
    flat_ids = route_ids.reshape(-1)
    route_hits = route_match.reshape(row_count * TOP, expert_count).astype(jnp.int32)
    route_rank = jnp.sum((jnp.cumsum(route_hits, axis=0) - route_hits) * route_hits, axis=1)
    slot_table = (
        jnp.full((expert_count, capacity), row_count * TOP, jnp.int32)
        .at[flat_ids, route_rank]
        .set(jnp.arange(row_count * TOP, dtype=jnp.int32))
    )
    token_table = slot_table // TOP
    padded_inputs = jnp.concatenate([normed_two, jnp.zeros((1, model_width), jnp.bfloat16)], axis=0)
    arrived = dispatch(
        padded_inputs[token_table].reshape(exp_count, per_group, capacity, model_width)
    )
    gate_pre = jnp.einsum("sekd,edf->sekf", arrived, full_gate, preferred_element_type=jnp.float32)
    up_pre = jnp.einsum("sekd,edf->sekf", arrived, full_up, preferred_element_type=jnp.float32)
    sigma = jax.nn.sigmoid(gate_pre)
    activated = gate_pre * sigma
    hidden = (activated * up_pre).astype(jnp.bfloat16)
    produced = jnp.einsum(
        "sekf,edf->sekd", hidden, full_down, preferred_element_type=jnp.float32
    ).astype(jnp.bfloat16)
    returned = combine(produced).reshape(expert_count, capacity, model_width)
    route_values = (
        returned[flat_ids, route_rank].reshape(row_count, TOP, model_width).astype(jnp.float32)
    )
    block_value = residual + jnp.sum(gate_weights[:, :, None] * route_values, axis=1)
    grad_routes = (gate_weights[:, :, None] * grad_out[:, None, :]).astype(jnp.bfloat16)
    grad_gates = jnp.sum(route_values * grad_out[:, None, :], axis=-1)
    grad_chosen = gate_weights * (
        grad_gates - jnp.sum(gate_weights * grad_gates, axis=-1, keepdims=True)
    )
    grad_logits = jnp.sum(jnp.where(route_match, grad_chosen[:, :, None], 0.0), axis=1).astype(
        jnp.bfloat16
    )
    padded_grads = jnp.concatenate(
        [
            grad_routes.reshape(row_count * TOP, model_width),
            jnp.zeros((1, model_width), jnp.bfloat16),
        ],
        axis=0,
    )
    grad_arrived = dispatch(
        padded_grads[slot_table].reshape(exp_count, per_group, capacity, model_width)
    )
    grad_hidden = jnp.einsum(
        "sekd,edf->sekf", grad_arrived, full_down, preferred_element_type=jnp.float32
    )
    grad_gate_pre = (grad_hidden * up_pre * sigma * (1.0 + gate_pre * (1.0 - sigma))).astype(
        jnp.bfloat16
    )
    grad_up_pre = (grad_hidden * activated).astype(jnp.bfloat16)
    grad_down = jnp.einsum(
        "sekd,sekf->edf", grad_arrived, hidden, preferred_element_type=jnp.float32
    )
    grad_gate = jnp.einsum(
        "sekd,sekf->edf", arrived, grad_gate_pre, preferred_element_type=jnp.float32
    )
    grad_up = jnp.einsum("sekd,sekf->edf", arrived, grad_up_pre, preferred_element_type=jnp.float32)
    grad_inputs = jnp.einsum(
        "sekf,edf->sekd", grad_gate_pre, full_gate, preferred_element_type=jnp.float32
    ) + jnp.einsum("sekf,edf->sekd", grad_up_pre, full_up, preferred_element_type=jnp.float32)
    grad_back = combine(grad_inputs.astype(jnp.bfloat16)).reshape(
        expert_count, capacity, model_width
    )
    grad_normed_two = jnp.sum(
        grad_back[flat_ids, route_rank].reshape(row_count, TOP, model_width).astype(jnp.float32),
        axis=1,
    ) + contract_cols(grad_logits, full_router)
    scaled_two = grad_normed_two * gain_two
    grad_gain_two = jnp.sum(grad_normed_two * residual * inv_two, axis=0)
    grad_residual = (
        grad_out
        + inv_two * scaled_two
        - residual * inv_two**3 * jnp.mean(scaled_two * residual, axis=-1, keepdims=True)
    )
    grad_attended = grad_residual.astype(jnp.bfloat16)
    grad_mixed = jnp.dot(grad_attended, full_output, preferred_element_type=jnp.float32).astype(
        jnp.bfloat16
    )
    grad_output = contract_rows(grad_attended, mixed_low)
    grad_mixed_heads = grad_mixed.reshape(row_count, KV, group_size, HD)
    grad_weights = jnp.einsum(
        "ikgd,jkd->kgij", grad_mixed_heads, value_heads, preferred_element_type=jnp.float32
    )
    row_inner = jnp.sum(weights_full * grad_weights, axis=-1, keepdims=True)
    grad_scores = (weights_full * (grad_weights - row_inner)).astype(jnp.bfloat16)
    grad_queries = (
        jnp.einsum("kgij,jkd->ikgd", grad_scores, key_heads, preferred_element_type=jnp.float32)
        * score_scale
    )
    key_terms = (
        jnp.einsum("kgij,ikgd->jkd", grad_scores, query_groups, preferred_element_type=jnp.float32)
        * score_scale
    )
    value_terms = jnp.einsum(
        "kgij,ikgd->jkd", weights_low, grad_mixed_heads, preferred_element_type=jnp.float32
    )
    grad_keys, grad_values = (
        lax.psum_scatter(
            key_terms.reshape(key_count, KV * HD), "ctx", scatter_dimension=0, tiled=True
        ),
        lax.psum_scatter(
            value_terms.reshape(key_count, KV * HD), "ctx", scatter_dimension=0, tiled=True
        ),
    )
    grad_query_raw = (
        rotate(grad_queries.reshape(row_count, HEADS, HD), cosine, -sine)
        .astype(jnp.bfloat16)
        .reshape(row_count, HEADS * HD)
    )
    grad_key_raw = (
        rotate(grad_keys.reshape(row_count, KV, HD), cosine, -sine)
        .astype(jnp.bfloat16)
        .reshape(row_count, KV * HD)
    )
    grad_kv_raw = jnp.concatenate([grad_key_raw, grad_values.astype(jnp.bfloat16)], axis=1)
    grad_normed_one = contract_cols(grad_query_raw, full_query) + contract_cols(
        grad_kv_raw, full_kv
    )
    grad_query = contract_rows(normed_one, grad_query_raw)
    grad_kv = contract_rows(normed_one, grad_kv_raw)
    scaled_one = grad_normed_one * gain_one
    grad_gain_one = jnp.sum(grad_normed_one * inputs * inv_one, axis=0)
    input_grad = (
        grad_residual
        + inv_one * scaled_one
        - inputs * inv_one**3 * jnp.mean(scaled_one * inputs, axis=-1, keepdims=True)
    )
    grad_router = contract_rows(normed_two, grad_logits)
    grad_gains = jnp.stack([grad_gain_one, grad_gain_two])
    part_query, part_kv, part_output, part_router, part_gains = (
        lax.psum_scatter(grad_query, "exp", scatter_dimension=1, tiled=True),
        lax.psum_scatter(grad_kv, "exp", scatter_dimension=1, tiled=True),
        lax.psum_scatter(grad_output, "exp", scatter_dimension=1, tiled=True),
        lax.psum_scatter(grad_router, "exp", scatter_dimension=1, tiled=True),
        lax.psum_scatter(grad_gains, "exp", scatter_dimension=1, tiled=True),
    )
    sum_query, sum_kv, sum_output, sum_router, sum_gains = lax.psum(
        (part_query, part_kv, part_output, part_router, part_gains), "ctx"
    )
    query_fresh, query_new = head_update(query_weight, query_momentum, sum_query)
    kv_fresh, kv_new = head_update(kv_weight, kv_momentum, sum_kv)
    output_fresh, output_new = head_update(output_weight, output_momentum, sum_output)
    router_one, router_two, router_new = adam_update(
        router, router_first, router_second, sum_router, router_rate, decay_rate
    )
    gains_one, gains_two, gains_new = adam_update(
        gains, gains_first, gains_second, sum_gains, gain_rate, 0.0
    )
    matrix_count = 3 * per_group
    slots_each = -(-matrix_count // ctx_count)
    slot_total = slots_each * ctx_count
    summed = lax.psum_scatter(
        pad_slots(jnp.concatenate([grad_gate, grad_up, grad_down], axis=0), slot_total),
        "ctx",
        scatter_dimension=0,
        tiled=True,
    )
    previous = to_owners(
        pad_slots(jnp.concatenate([gate_momentum, up_momentum, down_momentum], axis=0), slot_total)
    )
    fresh_owned = mom_rate * previous + summed
    ortho_owned = owner_orthogonal(fresh_owned)
    fresh_back, ortho_back = (
        lax.all_to_all(fresh_owned, "ctx", split_axis=1, concat_axis=0, tiled=True),
        lax.all_to_all(ortho_owned, "ctx", split_axis=1, concat_axis=0, tiled=True),
    )
    fresh_rows = fresh_back[:matrix_count]
    ortho_rows = ortho_back[:matrix_count]
    new_rows = step_weight(
        jnp.concatenate([gate_weight, up_weight, down_weight], axis=0), ortho_rows
    )
    return (
        block_value.astype(jnp.bfloat16)[None],
        input_grad[None],
        query_fresh,
        query_new,
        kv_fresh,
        kv_new,
        output_fresh,
        output_new,
        fresh_rows[:per_group],
        new_rows[:per_group],
        fresh_rows[per_group : 2 * per_group],
        new_rows[per_group : 2 * per_group],
        fresh_rows[2 * per_group :],
        new_rows[2 * per_group :],
        router_one,
        router_two,
        router_new,
        gains_one,
        gains_two,
        gains_new,
    )


def solution(mesh):
    return jax.shard_map(
        body,
        mesh=mesh,
        in_specs=(
            P("exp", "ctx", None),
            P("exp", "ctx", None),
            P("exp", "ctx", None),
            P(None, "exp"),
            P(None, "exp"),
            P(None, "exp"),
            P(None, "exp"),
            P(None, "exp"),
            P("exp", "ctx", None),
            P("exp", "ctx", None),
            P("exp", "ctx", None),
            P(None, "exp"),
            P(None, "exp"),
            P(None, "exp"),
            P("exp", "ctx", None),
            P("exp", "ctx", None),
            P("exp", "ctx", None),
            P(None, "exp"),
            P(None, "exp"),
            P(None, "exp"),
            P(None, "exp"),
        ),
        out_specs=(
            P("exp", "ctx", None),
            P("exp", "ctx", None),
            P(None, "exp"),
            P(None, "exp"),
            P(None, "exp"),
            P(None, "exp"),
            P(None, "exp"),
            P(None, "exp"),
            P("exp", "ctx", None),
            P("exp", "ctx", None),
            P("exp", "ctx", None),
            P("exp", "ctx", None),
            P("exp", "ctx", None),
            P("exp", "ctx", None),
            P(None, "exp"),
            P(None, "exp"),
            P(None, "exp"),
            P(None, "exp"),
            P(None, "exp"),
            P(None, "exp"),
        ),
        check_vma=False,
    )
```

profile of v0, /device:TPU:0, one launch (start us, length us, event | category | flops | bytes accessed | tf_op | source)
XLA Modules:
  0.0 1669.5 jit_solution(10904300134345542519)
XLA Ops:
  9.4 24.4 %all-gather = bf16[16,64,2]{1,2,0:T(2,128)(2,1)S(1)} all-gather(bf16[1,64,2]{1,2,0:T(2,128)(2,1)S(1)} %convert_bitcast_fusion.3), channel_id=1, replica_groups=mesh['ctx'=8,'exp'=16] {'exp'}, dimensions={0}, use_global_device_ids=true | all-gather | bytes 4352 | tf_op jit(solution)/shard_map/all_gather | solution.py:166
  36.3 24.1 %all-gather.11.cloned.1.call-done = bf16[1024,1024]{0,1:T(8,128)(2,1)} async-done(((bf16[1024,64]{0,1:T(8,128)(2,1)}), bf16[1024,1024]{0,1:T(8,128)(2,1)}) %all-gather.11.cloned.1.call-update) | async-done | bytes 2097168 | tf_op jit(solution)/shard_map/all_gather | solution.py:163
  67.0 9.0 reduce-window.6
  81.3 27.9 %all-gather.17.cloned.1.call-done = bf16[1024,1024]{0,1:T(8,128)(2,1)} async-done(((bf16[1024,64]{0,1:T(8,128)(2,1)}), bf16[1024,1024]{0,1:T(8,128)(2,1)}) %all-gather.17.cloned.1.call-update) | async-done | bytes 2097168 | tf_op jit(solution)/shard_map/all_gather | solution.py:162
  111.7 39.0 %all-gather.15.cloned.1.call-done = bf16[1024,512]{0,1:T(8,128)(2,1)} async-done(((bf16[128,512]{0,1:T(8,128)(2,1)}), bf16[1024,512]{0,1:T(8,128)(2,1)}) %all-gather.15.cloned.1.call-update) | async-done | bytes 1048592 | tf_op jit(solution)/shard_map/all_gather | solution.py:189
  156.7 37.2 %all-gather.13.cloned.1.call-done = bf16[1024,512]{1,0:T(8,128)(2,1)} async-done(((bf16[128,512]{1,0:T(8,128)(2,1)}), bf16[1024,512]{1,0:T(8,128)(2,1)}) %all-gather.13.cloned.1.call-update) | async-done | bytes 1048592 | tf_op jit(solution)/shard_map/all_gather | solution.py:190
  203.4 39.6 %all-gather.19.cloned.1.call-done = bf16[1024,1024]{0,1:T(8,128)(2,1)} async-done(((bf16[1024,64]{0,1:T(8,128)(2,1)}), bf16[1024,1024]{0,1:T(8,128)(2,1)}) %all-gather.19.cloned.1.call-update) | async-done | bytes 2097168 | tf_op jit(solution)/shard_map/all_gather | solution.py:164
  257.4 85.1 %all-gather.1 = bf16[16,2,1024]{2,1,0:T(2,128)(2,1)S(1)} all-gather(bf16[1,2,1024]{2,1,0:T(2,128)(2,1)S(1)} %convert_bitcast_fusion.2), channel_id=1, replica_groups=mesh['ctx'=8,'exp'=16] {'exp'}, dimensions={0}, use_global_device_ids=true | all-gather | bytes 69632 | tf_op jit(solution)/shard_map/all_gather | solution.py:165
  361.6 42.9 %all-gather.21.cloned.1.call-done = bf16[2,1024,512]{2,1,0:T(8,128)(2,1)} async-done(((bf16[2,128,512]{2,1,0:T(8,128)(2,1)}), bf16[2,1024,512]{2,1,0:T(8,128)(2,1)}) %all-gather.21.cloned.1.call-update) | async-done | bytes 2097168 | tf_op jit(solution)/shard_map/all_gather | solution.py:169
  410.4 46.6 %all-gather.25.cloned.1.call-done = bf16[2,1024,512]{2,1,0:T(8,128)(2,1)} async-done(((bf16[2,128,512]{2,1,0:T(8,128)(2,1)}), bf16[2,1024,512]{2,1,0:T(8,128)(2,1)}) %all-gather.25.cloned.1.call-update) | async-done | bytes 2097168 | tf_op jit(solution)/shard_map/all_gather | solution.py:171
  457.1 8.0 fusion.12
  468.9 6.5 all-to-all-start.1
  483.4 32.7 %all-to-all-done.1 = bf16[16,2,48,1024]{3,2,1,0:T(8,128)(2,1)S(1)} async-done(((bf16[16,2,48,1024]{3,2,1,0:T(8,128)(2,1)}), bf16[16,2,48,1024]{3,2,1,0:T(8,128)(2,1)S(1)}, u32[]{:S(2)}, u32[]{:S(2)}) %all-to-all-start.1) | async-done | bytes 3145760 | tf_op jit(solution)/shard_map/all_to_all | solution.py:105
  522.0 20.6 %gather_fusion.1 = bf16[1024,1024]{1,0:T(8,128)(2,1)} fusion(bf16[32,48,1024]{2,1,0:T(8,128)(2,1)} %bitcast.594, s32[1024]{0:T(1024)S(1)} %bitcast.591), kind=kCustom, calls=%fused_computation.1 | custom fusion | bytes 4202496 | tf_op jit(solution)/shard_map/gather | solution.py:249
  549.9 12.1 all-to-all-done.3
  562.0 15.4 gather_fusion.3
  583.5 6.7 fusion.191
  614.9 23.9 %reduce-scatter.12.cloned.1.call-done = f32[128,512]{0,1:T(8,128)} async-done(((f32[1024,512]{0,1:T(8,128)}), f32[128,512]{0,1:T(8,128)}) %reduce-scatter.12.cloned.1.call-update) | async-done | bytes 262160 | tf_op jit(solution)/shard_map/reduce_scatter | solution.py:327
  639.8 53.1 %reduce-scatter.10.cloned.1.call-done = f32[128,512]{0,1:T(8,128)} async-done(((f32[1024,512]{0,1:T(8,128)}), f32[128,512]{0,1:T(8,128)}) %reduce-scatter.10.cloned.1.call-update) | async-done | bytes 262160 | tf_op jit(solution)/shard_map/reduce_scatter | solution.py:324
  716.2 6.5 convolution_bitcast_fusion.2
  722.7 53.9 %reduce-scatter.14.cloned.1.call-done = f32[1024,64]{0,1:T(8,128)} async-done(((f32[1024,1024]{0,1:T(8,128)}), f32[1024,64]{0,1:T(8,128)}) %reduce-scatter.14.cloned.1.call-update) | async-done | bytes 262160 | tf_op jit(solution)/shard_map/reduce_scatter | solution.py:357
  776.6 83.7 %reduce-scatter.18.cloned.1.call-done = f32[1024,64]{0,1:T(8,128)} async-done(((f32[1024,1024]{0,1:T(8,128)}), f32[1024,64]{0,1:T(8,128)}) %reduce-scatter.18.cloned.1.call-update) | async-done | bytes 262160 | tf_op jit(solution)/shard_map/reduce_scatter | solution.py:359
  860.3 83.3 %reduce-scatter.16.cloned.1.call-done = f32[1024,64]{0,1:T(8,128)} async-done(((f32[1024,1024]{0,1:T(8,128)}), f32[1024,64]{0,1:T(8,128)}) %reduce-scatter.16.cloned.1.call-update) | async-done | bytes 262160 | tf_op jit(solution)/shard_map/reduce_scatter | solution.py:358
  943.7 11.3 maximum_maximum_fusion
  963.9 24.9 %all-to-all-done.4 = f32[8,128,512]{2,1,0:T(8,128)} async-done(((f32[8,128,512]{2,1,0:T(8,128)}), f32[8,128,512]{2,1,0:T(8,128)}, u32[]{:S(2)}, u32[]{:S(2)}) %all-to-all-start.4) | async-done | bytes 2097184 | tf_op jit(solution)/shard_map/all_to_all | solution.py:109
  990.7 91.8 %all-reduce.8.cloned.1.call-done = f32[1024,32]{0,1:T(8,128)} async-done(((f32[1024,32]{0,1:T(8,128)}), f32[1024,32]{0,1:T(8,128)}) %all-reduce.8.cloned.1.call-update) | async-done | bytes 131088
  1084.3 68.8 %reduce-scatter.22.cloned.1.call-done = f32[64,2]{1,0:T(8,128)} async-done(((f32[1024,2]{1,0:T(8,128)}), f32[64,2]{1,0:T(8,128)}) %reduce-scatter.22.cloned.1.call-update) | async-done | bytes 528
  1153.9 19.9 %all-reduce.3 = (f32[1024,2]{0,1:T(2,128)S(1)}, f32[2,64]{1,0:T(2,128)S(1)}) all-reduce(f32[1024,2]{0,1:T(2,128)S(1)} %constant_dynamic-slice_fusion, f32[2,64]{1,0:T(2,128)S(1)} %copy.207), channel_id=1, replica_groups=mesh['ctx'=8,'exp'=16] {'ctx'}, use_global_device_ids=true, to_apply=%region_33.34 | all-reduce | flops 2176 | bytes 17408 | tf_op jit(solution)/shard_map/psum | solution.py:363
  1175.1 58.3 %all-reduce.10.cloned.1.call-done = (f32[1024,64]{0,1:T(8,128)}, f32[1024,64]{0,1:T(8,128)}, f32[1024,64]{0,1:T(8,128)}) async-done(((f32[1024,64]{0,1:T(8,128)}, f32[1024,64]{0,1:T(8,128)}, f32[1024,64]{0,1:T(8,128)}), (f32[1024,64]{0,1:T(8,128)}, f32[1024,64]{0,1:T(8,128)}, f32[1024,64]{0,1:T(8,128)})) %all-reduce.10.cloned.1.call-update) | async-done | bytes 786448 | tf_op jit(solution)/shard_map/psum | solution.py:363
  1250.7 310.9 %reduce-scatter.20.cloned.1.call-done = f32[1,1024,512]{2,1,0:T(8,128)} async-done(((f32[8,1024,512]{2,1,0:T(8,128)}), f32[1,1024,512]{2,1,0:T(8,128)}) %reduce-scatter.20.cloned.1.call-update) | async-done | bytes 2097168 | tf_op jit(solution)/shard_map/reduce_scatter | solution.py:378
  1625.7 6.1 all-to-all-start.6
  1639.3 18.9 %all-to-all-done.6 = f32[1,1024,512]{2,0,1:T(1,128)S(1)} async-done(((f32[1,1024,512]{2,0,1:T(1,128)}), f32[1,1024,512]{2,0,1:T(1,128)S(1)}, u32[]{:S(2)}, u32[]{:S(2)}) %all-to-all-start.6) | async-done | bytes 2097184 | tf_op jit(solution)/shard_map/all_to_all | solution.py:391
  (382 shorter events, 257.2 us)
Async XLA Ops:
  7.2 53.2 %all-gather.11.cloned.1.call-start = ((), (), s32[]{:S(2)}) async-start(), calls=%async_computation.14 | async-start | bytes 2228224 | tf_op jit(solution)/shard_map/all_gather | solution.py:163
  7.9 101.3 %all-gather.17.cloned.1.call-start = ((), (), s32[]{:S(2)}) async-start(), calls=%async_computation.17 | async-start | bytes 2228224 | tf_op jit(solution)/shard_map/all_gather | solution.py:162
  8.7 142.0 %all-gather.15.cloned.1.call-start = ((), (), s32[]{:S(2)}) async-start(), calls=%async_computation.16 | async-start | bytes 1179648 | tf_op jit(solution)/shard_map/all_gather | solution.py:189
  35.5 210.2 %copy-start.51 = (f32[1,1024]{1,0:T(1,128)}, f32[1,1024]{1,0:T(1,128)S(1)}, u32[]{:S(2)}) copy-start(f32[1,1024]{1,0:T(1,128)S(1)} %get-tuple-element.69) | copy-start | bytes 12292
  63.9 130.0 %all-gather.13.cloned.1.call-start = ((), (), s32[]{:S(2)}) async-start(), calls=%async_computation.15 | async-start | bytes 1179648 | tf_op jit(solution)/shard_map/all_gather | solution.py:190
  64.6 178.4 %all-gather.19.cloned.1.call-start = ((), (), s32[]{:S(2)}) async-start(), calls=%async_computation.18 | async-start | bytes 2228224 | tf_op jit(solution)/shard_map/all_gather | solution.py:164
  65.2 290.3 %all-gather.23.cloned.1.call-start = ((), (), s32[]{:S(2)}) async-start(), calls=%async_computation.20 | async-start | bytes 2359296 | tf_op jit(solution)/shard_map/all_gather | solution.py:170
  65.8 338.7 %all-gather.21.cloned.1.call-start = ((), (), s32[]{:S(2)}) async-start(), calls=%async_computation.19 | async-start | bytes 2359296 | tf_op jit(solution)/shard_map/all_gather | solution.py:169
  252.0 99.1 %all-to-all-start = ((bf16[16,2,48,1024]{3,2,1,0:T(8,128)(2,1)}), bf16[16,2,48,1024]{3,2,1,0:T(8,128)(2,1)}, u32[]{:S(2)}, u32[]{:S(2)}) async-start(bf16[16,2,48,1024]{3,2,1,0:T(8,128)(2,1)} %bitcast.595), calls=%async_computation | async-start | bytes 6291456 | tf_op jit(solution)/shard_map/all_to_all | solution.py:101
  256.6 200.5 %all-gather.25.cloned.1.call-start = ((), (), s32[]{:S(2)}) async-start(), calls=%async_computation.21 | async-start | bytes 2359296 | tf_op jit(solution)/shard_map/all_gather | solution.py:171
  351.0 106.0 %all-to-all-start.2 = ((bf16[16,2,48,1024]{3,2,1,0:T(8,128)(2,1)}), bf16[16,2,48,1024]{3,2,1,0:T(8,128)(2,1)S(1)}, u32[]{:S(2)}, u32[]{:S(2)}) async-start(bf16[16,2,48,1024]{3,2,1,0:T(8,128)(2,1)} %bitcast.596), calls=%async_computation.2 | async-start | bytes 6291456 | tf_op jit(solution)/shard_map/all_to_all | solution.py:101
  468.9 47.1 %all-to-all-start.1 = ((bf16[16,2,48,1024]{3,2,1,0:T(8,128)(2,1)}), bf16[16,2,48,1024]{3,2,1,0:T(8,128)(2,1)S(1)}, u32[]{:S(2)}, u32[]{:S(2)}) async-start(bf16[16,2,48,1024]{3,2,1,0:T(8,128)(2,1)} %copy.166), calls=%async_computation.1 | async-start | bytes 6291456 | tf_op jit(solution)/shard_map/all_to_all | solution.py:105
  517.7 44.3 %all-to-all-start.3 = ((bf16[16,2,48,1024]{3,2,1,0:T(8,128)(2,1)}), bf16[16,2,48,1024]{3,2,1,0:T(8,128)(2,1)S(1)}, u32[]{:S(2)}, u32[]{:S(2)}) async-start(bf16[16,2,48,1024]{3,2,1,0:T(8,128)(2,1)} %copy.169), calls=%async_computation.3 | async-start | bytes 6291456 | tf_op jit(solution)/shard_map/all_to_all | solution.py:105
  521.4 117.4 %reduce-scatter.12.cloned.1.call-start = ((), (), s32[]{:S(2)}) async-start(), calls=%async_computation.23 | async-start | bytes 2359296 | tf_op jit(solution)/shard_map/reduce_scatter | solution.py:327
  590.2 102.7 %reduce-scatter.10.cloned.1.call-start = ((), (), s32[]{:S(2)}) async-start(), calls=%async_computation.22 | async-start | bytes 2359296 | tf_op jit(solution)/shard_map/reduce_scatter | solution.py:324
  604.1 172.5 %reduce-scatter.14.cloned.1.call-start = ((), (), s32[]{:S(2)}) async-start(), calls=%async_computation.24 | async-start | bytes 4456448 | tf_op jit(solution)/shard_map/reduce_scatter | solution.py:357
  611.2 249.1 %reduce-scatter.18.cloned.1.call-start = ((), (), s32[]{:S(2)}) async-start(), calls=%async_computation.26 | async-start | bytes 4456448 | tf_op jit(solution)/shard_map/reduce_scatter | solution.py:359
  614.9 328.8 %reduce-scatter.16.cloned.1.call-start = ((), (), s32[]{:S(2)}) async-start(), calls=%async_computation.25 | async-start | bytes 4456448 | tf_op jit(solution)/shard_map/reduce_scatter | solution.py:358
  696.9 385.6 %all-reduce.8.cloned.1.call-start = ((), (), s32[]{:S(2)}) async-start(), calls=%async_computation.29 | async-start | bytes 262144
  710.8 442.2 %reduce-scatter.22.cloned.1.call-start = ((), (), s32[]{:S(2)}) async-start(), calls=%async_computation.28 | async-start | bytes 557056
  715.7 228.0 %copy-start.65 = (f32[8]{0:T(128)S(1)}, f32[8]{0:T(128)}, u32[]{:S(2)}) copy-start(f32[8]{0:T(128)} %pad.14.clone) | copy-start | bytes 100
  715.7 517.7 %all-reduce.10.cloned.1.call-start = ((), (), s32[]{:S(2)}) async-start(), calls=%async_computation.30 | async-start | bytes 1572864 | tf_op jit(solution)/shard_map/psum | solution.py:363
  943.7 617.9 %reduce-scatter.20.cloned.1.call-start = ((), (), s32[]{:S(2)}) async-start(), calls=%async_computation.27 | async-start | bytes 18874368 | tf_op jit(solution)/shard_map/reduce_scatter | solution.py:378
  958.0 30.8 %all-to-all-start.4 = ((f32[8,128,512]{2,1,0:T(8,128)}), f32[8,128,512]{2,1,0:T(8,128)}, u32[]{:S(2)}, u32[]{:S(2)}) async-start(f32[8,128,512]{2,1,0:T(8,128)} %maximum_maximum_fusion.1), calls=%async_computation.9 | async-start | bytes 4194304 | tf_op jit(solution)/shard_map/all_to_all | solution.py:109
  963.9 210.0 %copy-start.66 = (f32[2,64]{1,0:T(2,128)S(1)}, f32[2,64]{1,0:T(2,128)}, u32[]{:S(2)}) copy-start(f32[2,64]{1,0:T(2,128)} %param.28) | copy-start | bytes 1540
  963.9 210.0 %copy-start.67 = (f32[2,64]{1,0:T(2,128)S(1)}, f32[2,64]{1,0:T(2,128)}, u32[]{:S(2)}) copy-start(f32[2,64]{1,0:T(2,128)} %param.41) | copy-start | bytes 1540
  963.9 210.0 %copy-start.68 = (f32[2,64]{1,0:T(2,128)S(1)}, f32[2,64]{1,0:T(2,128)}, u32[]{:S(2)}) copy-start(f32[2,64]{1,0:T(2,128)} %param.40) | copy-start | bytes 1540
  963.9 210.6 %copy-start.55 = (f32[1024,2]{0,1:T(2,128)S(1)}, f32[1024,2]{0,1:T(2,128)}, u32[]{:S(2)}) copy-start(f32[1024,2]{0,1:T(2,128)} %param.27) | copy-start | bytes 24580
  963.9 210.6 %copy-start.61 = (f32[1024,2]{0,1:T(2,128)S(1)}, f32[1024,2]{0,1:T(2,128)}, u32[]{:S(2)}) copy-start(f32[1024,2]{0,1:T(2,128)} %param.39) | copy-start | bytes 24580
  963.9 210.6 %copy-start.62 = (f32[1024,2]{0,1:T(2,128)S(1)}, f32[1024,2]{0,1:T(2,128)}, u32[]{:S(2)}) copy-start(f32[1024,2]{0,1:T(2,128)} %param.38) | copy-start | bytes 24580
  1569.2 56.5 %all-to-all-start.5 = ((f32[1,1024,512]{2,0,1:T(1,128)}), f32[1,1024,512]{2,0,1:T(1,128)}, u32[]{:S(2)}, u32[]{:S(2)}) async-start(f32[1,1024,512]{2,0,1:T(1,128)} %copy.179), calls=%async_computation.11 | async-start | bytes 4194304 | tf_op jit(solution)/shard_map/all_to_all | solution.py:390
  1625.7 32.6 %all-to-all-start.6 = ((f32[1,1024,512]{2,0,1:T(1,128)}), f32[1,1024,512]{2,0,1:T(1,128)S(1)}, u32[]{:S(2)}, u32[]{:S(2)}) async-start(f32[1,1024,512]{2,0,1:T(1,128)} %copy.186), calls=%async_computation.12 | async-start | bytes 4194304 | tf_op jit(solution)/shard_map/all_to_all | solution.py:391
  (69 other events, 883.4 us)
Sparse Core Ops, SparseCore 0:
  10.5 49.8 all-gather.10
  62.9 46.3 all-gather.16
  111.4 39.2 all-gather.14
  152.8 41.0 all-gather.12
  196.2 46.8 all-gather.18
  244.5 84.9 all-gather.22
  331.2 73.2 all-gather.20
  406.1 50.8 all-gather.24
  590.4 48.4 reduce-scatter.11
  641.1 51.8 reduce-scatter.9
  697.0 79.5 reduce-scatter.13
  781.0 79.2 reduce-scatter.17
  864.3 79.2 reduce-scatter.15
  946.7 135.7 all-reduce.7
  1086.6 66.4 reduce-scatter.21
  1155.9 77.5 all-reduce.9
  1235.7 325.7 reduce-scatter.19
where the time goes:
time: 1680 us; the launch traced here: 1670 us
  waiting for transfers between devices  1180 us (70%)
  matrix products  155 us (9%)
  blocking collectives  129 us (8%)
  local copies, waits for them, and re-layouts  89.6 us (5%)
  other arithmetic  61.2 us (4%)
  starting transfers between devices  37.3 us (2%)
  between operations  19.2 us (1%)
    reduce_scatter x1, waiting for transfers between devices, body(): lax.psum_scatter(pad_slots(jnp.concatenate([grad_gate, grad_up, grad_down...  311 us
    unnamed x19, waiting for transfers between devices  165 us
    all_gather x1, blocking collectives, body(): lax.all_gather(router.astype(jnp.bfloat16), 'exp', axis=1, tiled=True)  85.1 us
    reduce_scatter x1, waiting for transfers between devices, body(): lax.psum_scatter(grad_output, 'exp', scatter_dimension=1, tiled=True)  83.7 us
    reduce_scatter x1, waiting for transfers between devices, body(): lax.psum_scatter(grad_kv, 'exp', scatter_dimension=1, tiled=True)  83.3 us
    psum x1, waiting for transfers between devices, body(): lax.psum((part_query, part_kv, part_output, part_router, part_gains), 'ctx')  58.3 us
    reduce_scatter x1, waiting for transfers between devices, body(): lax.psum_scatter(grad_query, 'exp', scatter_dimension=1, tiled=True)  53.9 us
    reduce_scatter x1, waiting for transfers between devices, body(): lax.psum_scatter(key_terms.reshape(key_count, KV * HD), 'ctx', scatter_di...  53.1 us
  transfers between devices with their start and end apart: 24, of which 20 were waited for; matrix products, arithmetic and copies ran while one was open for 15% of the time, Pallas kernels for 0%

commit v1 on v0

v1 whole, which is shorter than its diff:
```python
import math

import jax
import jax.numpy as jnp
from jax import lax
from jax.experimental import pallas as pl
from jax.experimental.pallas import tpu as pltpu
from jax.sharding import PartitionSpec as P

D = 1024
HEADS = 16
KV = 8
HD = 64
TOP = 8
STEP = 10


eps_norm = 1e-05
rope_base = 10000.0
mom_rate = 0.95
muon_rate = 0.15
decay_rate = 0.1
adam_one = 0.9
adam_two = 0.95
adam_eps = 1e-08
router_rate = 0.015
gain_rate = 0.2
coef_one = 3.4445
coef_two = -4.775
coef_three = 2.0315
highest = lax.Precision.HIGHEST


def rope_tables(first_row, token_count):
    half_width = HD // 2
    frequency = rope_base ** (-jnp.arange(half_width, dtype=jnp.float32) * 2.0 / HD)
    position = (first_row + jnp.arange(token_count, dtype=jnp.int32)).astype(jnp.float32)
    angle_grid = position[:, None] * frequency[None, :]
    return (jnp.cos(angle_grid), jnp.sin(angle_grid))


def rotate(vector, cosine, sine):
    half_width = vector.shape[-1] // 2
    front_half = vector[..., :half_width]
    back_half = vector[..., half_width:]
    cos_rows = cosine[:, None, :]
    sin_rows = sine[:, None, :]
    return jnp.concatenate(
        [
            front_half * cos_rows - back_half * sin_rows,
            back_half * cos_rows + front_half * sin_rows,
        ],
        axis=-1,
    )


EXPERTS = 32
CAP = 48
WIDE = 128
FF = 512
ROWS = 16 * CAP
CHUNKS = 2


def exchange(blocks, axis, groups=None):
    return lax.all_to_all(
        blocks, axis, split_axis=0, concat_axis=0, tiled=True, axis_index_groups=groups
    )


def spread(block, axis, groups=None, count=8):
    return exchange(jnp.broadcast_to(block[None], (count,) + block.shape), axis, groups)


def parity_groups(count):
    return [list(range(core, count, 2)) for core in range(2)]


def core_swap(block, count):
    return lax.ppermute(block, "exp", [(i, i ^ 1) for i in range(count)])


def three_parts(value):
    high = value.astype(jnp.bfloat16)
    rest = value - high.astype(jnp.float32)
    middle = rest.astype(jnp.bfloat16)
    low = (rest - middle.astype(jnp.float32)).astype(jnp.bfloat16)
    return high, middle, low


def polynomial(gram, steps, precision):
    total = None
    for step in range(steps):
        square = jnp.matmul(gram, gram, precision=precision)
        eye = jnp.eye(gram.shape[-1], dtype=jnp.float32)
        factor = coef_one * eye + coef_two * gram + coef_three * square
        total = factor if total is None else jnp.matmul(factor, total, precision=precision)
        if step < steps - 1:
            gram = jnp.matmul(
                jnp.matmul(factor, gram, precision=precision), factor, precision=precision
            )
    return total


def step_weight(weight, ortho):
    return (
        weight.astype(jnp.float32) * (1.0 - muon_rate * decay_rate)
        - muon_rate * 0.2 * math.sqrt(D) * ortho
    )


def adam_update(param, first, second, grad, rate, decay):
    first = adam_one * first + (1.0 - adam_one) * grad
    second = adam_two * second + (1.0 - adam_two) * grad * grad
    fixed_one = first / (1.0 - adam_one**STEP)
    fixed_two = second / (1.0 - adam_two**STEP)
    return (
        first,
        second,
        param * (1.0 - rate * decay) - rate * fixed_one / (jnp.sqrt(fixed_two) + adam_eps),
    )


def contract_rows(left, right, precision=None):
    return lax.dot_general(
        left,
        right,
        (((0,), (0,)), ((), ())),
        preferred_element_type=jnp.float32,
        precision=precision,
    )


def contract_cols(left, right):
    return lax.dot_general(
        left, right, (((1,), (1,)), ((), ())), preferred_element_type=jnp.float32
    )


def mat(left, right):
    return jnp.dot(left, right, preferred_element_type=jnp.float32)


def head_blocks(sums, momenta, weights):
    fresh = mom_rate * momenta + sums
    width = fresh.shape[1]
    block = jnp.arange(width) // HD
    same = block[:, None] == block[None, :]
    gram = jnp.where(same, contract_rows(fresh, fresh, highest), 0.0)
    square = jnp.sum(jnp.where(jnp.eye(width, dtype=bool), gram, 0.0), axis=0, keepdims=True)
    total = jnp.sum(jnp.where(same, square.T, 0.0), axis=0, keepdims=True)
    scale = 1.0 / (jnp.sqrt(total) + 1e-07)
    poly = polynomial(gram * scale * scale.T, 5, highest)
    ortho = jnp.dot(fresh * scale, poly, precision=highest)
    return fresh, step_weight(weights, ortho)


def expert_kernel(own_ref, arrived_ref, grads_ref, weight_ref, made_ref, back_ref, sums_ref,
                  rows_ref, hidden_ref, dgate_ref, dup_ref, dy_ref):
    expert = own_ref[0] + pl.program_id(0)
    full_gate = weight_ref[:, 0, 0].reshape(D, FF)
    full_up = weight_ref[:, 1, 0].reshape(D, FF)
    full_down = weight_ref[:, 2, 0].reshape(D, FF)
    chunk = ROWS // CHUNKS
    seqs = chunk // CAP

    def forward(step, carry):
        first = pl.multiple_of(step * seqs, seqs)
        where = pl.ds(pl.multiple_of(step * chunk, chunk), chunk)
        both = arrived_ref[pl.ds(first, seqs), 0].reshape(chunk, D + WIDE)
        rows = both[:, :D]
        lane = lax.broadcasted_iota(jnp.int32, (chunk, WIDE), 1)
        pick = (lane % EXPERTS == expert) & (lane < 3 * EXPERTS)
        gate = jnp.sum(
            jnp.where(pick, both[:, D:].astype(jnp.float32), 0.0), axis=1, keepdims=True
        )
        gate_pre = mat(rows, full_gate)
        up_pre = mat(rows, full_up)
        sigma = jax.nn.sigmoid(gate_pre)
        activated = gate_pre * sigma
        hidden = (activated * up_pre).astype(jnp.bfloat16)
        made = contract_cols(hidden, full_down).astype(jnp.bfloat16)
        made_ref[pl.ds(first, seqs), 0] = made.reshape(seqs, CAP, D)
        grad_f32 = grads_ref[pl.ds(first, seqs), 0].reshape(chunk, D).astype(jnp.float32)
        grad_made = (gate * grad_f32).astype(jnp.bfloat16)
        grad_gate_value = jnp.sum(made.astype(jnp.float32) * grad_f32, axis=1, keepdims=True)
        grad_hidden = mat(grad_made, full_down)
        grad_gate_pre = (
            grad_hidden * up_pre * sigma * (1.0 + gate_pre * (1.0 - sigma))
        ).astype(jnp.bfloat16)
        grad_up_pre = (grad_hidden * activated).astype(jnp.bfloat16)
        back = contract_cols(grad_gate_pre, full_gate) + contract_cols(grad_up_pre, full_up)
        back_ref[pl.ds(first, seqs), 0, :, :D] = back.astype(jnp.bfloat16).reshape(seqs, CAP, D)
        high, middle, low = [
            part.astype(jnp.float32) for part in three_parts(grad_gate_value)
        ]
        slot = jnp.where(
            lane < EXPERTS, high, jnp.where(lane < 2 * EXPERTS, middle, low)
        )
        back_ref[pl.ds(first, seqs), 0, :, D:] = (
            jnp.where(pick, slot, 0.0).astype(jnp.bfloat16).reshape(seqs, CAP, WIDE)
        )
        rows_ref[where] = rows
        hidden_ref[where] = hidden
        dgate_ref[where] = grad_gate_pre
        dup_ref[where] = grad_up_pre
        dy_ref[where] = grad_made
        return carry

    lax.fori_loop(0, CHUNKS, forward, 0)
    parts = sums_ref.shape[0]
    width = D // parts

    def gradients(part, carry):
        columns = pl.ds(pl.multiple_of(part * width, width), width)
        rows = rows_ref[:, columns]
        sums_ref[part, 0, 0] = contract_rows(rows, dgate_ref[...]).astype(jnp.bfloat16)
        sums_ref[part, 1, 0] = contract_rows(rows, dup_ref[...]).astype(jnp.bfloat16)
        sums_ref[part, 2, 0] = contract_rows(dy_ref[:, columns], hidden_ref[...]).astype(
            jnp.bfloat16
        )
        return carry

    lax.fori_loop(0, parts, gradients, 0)


def expert_math(arrived, grad_rows, weights):
    seqs, per_group = arrived.shape[:2]
    own = (lax.axis_index("exp") * per_group).astype(jnp.int32).reshape(1)
    count = weights.shape[0]

    def rows_spec(width):
        return pl.BlockSpec((seqs, 1, CAP, width), lambda e, own: (0, e, 0, 0))

    weight_spec = pl.BlockSpec(
        (count, 3, 1, D // count, FF), lambda e, own: (0, 0, e, 0, 0)
    )
    return pl.pallas_call(
        expert_kernel,
        grid_spec=pltpu.PrefetchScalarGridSpec(
            num_scalar_prefetch=1,
            grid=(per_group,),
            in_specs=[rows_spec(D + WIDE), rows_spec(D), weight_spec],
            out_specs=[rows_spec(D), rows_spec(D + WIDE), weight_spec],
            scratch_shapes=[
                pltpu.VMEM((ROWS, D), jnp.bfloat16),
                pltpu.VMEM((ROWS, FF), jnp.bfloat16),
                pltpu.VMEM((ROWS, FF), jnp.bfloat16),
                pltpu.VMEM((ROWS, FF), jnp.bfloat16),
                pltpu.VMEM((ROWS, D), jnp.bfloat16),
            ],
        ),
        out_shape=[
            jax.ShapeDtypeStruct((seqs, per_group, CAP, D), jnp.bfloat16),
            jax.ShapeDtypeStruct((seqs, per_group, CAP, D + WIDE), jnp.bfloat16),
            jax.ShapeDtypeStruct(weights.shape, jnp.bfloat16),
        ],
        compiler_params=pltpu.CompilerParams(vmem_limit_bytes=56 * 2**20),
        cost_estimate=pl.CostEstimate(
            flops=18 * ROWS * per_group * D * FF,
            bytes_accessed=30 * 2**20,
            transcendentals=ROWS * per_group * FF,
        ),
        name="experts",
    )(own, arrived, grad_rows, weights)


def split_two(value):
    high = value.astype(jnp.bfloat16)
    return high, (value - high.astype(jnp.float32)).astype(jnp.bfloat16)


def mat_three(left, right):
    return mat(left[0], right[0]) + (mat(left[0], right[1]) + mat(left[1], right[0]))


def owner_kernel(matrix_ref, out_ref, gram_ref, total_ref):
    gram = contract_rows(matrix_ref[...], matrix_ref[...])
    width = gram_ref.shape[0]
    row = lax.broadcasted_iota(jnp.int32, (width, width), 0)
    column = lax.broadcasted_iota(jnp.int32, (width, width), 1)
    eye = (row == column).astype(jnp.float32)
    square = jnp.sum(jnp.sum(eye * gram, axis=1, keepdims=True), axis=0, keepdims=True)
    scale = 1.0 / (jnp.sqrt(square) + 1e-07)
    gram_ref[...] = gram * scale * scale
    total_ref[...] = eye

    def step(index, carry):
        gram = gram_ref[...]
        gram_two = split_two(gram)
        factor = coef_one * eye + coef_two * gram + coef_three * mat_three(gram_two, gram_two)
        factor_two = split_two(factor)
        total_ref[...] = mat_three(factor_two, split_two(total_ref[...]))
        gram_ref[...] = mat_three(split_two(mat_three(factor_two, gram_two)), factor_two)
        return carry

    lax.fori_loop(0, 5, step, 0)
    high, low = split_two(total_ref[...])
    matrix = matrix_ref[...]
    out_ref[...] = ((mat(matrix, high) + mat(matrix, low)) * scale).astype(out_ref.dtype)


def owner_orthogonal(stacked):
    rows, width = stacked.shape
    return pl.pallas_call(
        owner_kernel,
        out_shape=jax.ShapeDtypeStruct(stacked.shape, jnp.bfloat16),
        in_specs=[pl.BlockSpec(memory_space=pltpu.VMEM)],
        out_specs=pl.BlockSpec(memory_space=pltpu.VMEM),
        scratch_shapes=[
            pltpu.VMEM((width, width), jnp.float32),
            pltpu.VMEM((width, width), jnp.float32),
        ],
        compiler_params=pltpu.CompilerParams(vmem_limit_bytes=48 * 2**20),
        cost_estimate=pl.CostEstimate(
            flops=6 * (22 * width**3 + 2 * rows * width**2),
            bytes_accessed=4 * rows * width,
            transcendentals=0,
        ),
        name="owner",
    )(stacked)


def probabilities(queries, keys, first):
    scores = contract_cols(queries, keys) * HD ** (-0.5)
    token = lax.broadcasted_iota(jnp.int32, scores.shape, 0) % (scores.shape[0] // 2)
    key = lax.broadcasted_iota(jnp.int32, scores.shape, 1)
    scores = jnp.where(key <= first + token, scores, -1e30)
    running_max = jnp.max(scores, axis=1, keepdims=True)
    raised = jnp.exp(scores - running_max)
    return raised * (1.0 / jnp.sum(raised, axis=1, keepdims=True))


def two_heads(block, group):
    left = block[:, 2 * group * HD : (2 * group + 1) * HD]
    right = block[:, (2 * group + 1) * HD : (2 * group + 2) * HD]
    return jnp.concatenate([left, right], axis=0)


def side_by_side(stacked):
    half = stacked.shape[0] // 2
    return jnp.concatenate([stacked[:half], stacked[half:]], axis=1)


def attend_kernel(first_ref, query_ref, key_ref, value_ref, mixed_ref):
    queries, keys, values = query_ref[...], key_ref[...], value_ref[...]
    mixed = []
    for group in range(2):
        columns = slice(group * HD, (group + 1) * HD)
        weights = probabilities(two_heads(queries, group), keys[:, columns], first_ref[0])
        mixed.append(side_by_side(mat(weights.astype(jnp.bfloat16), values[:, columns])))
    mixed_ref[...] = jnp.concatenate(mixed, axis=1).astype(mixed_ref.dtype)


def attend_back_kernel(
    first_ref, query_ref, key_ref, value_ref, grad_ref, dquery_ref, dkey_ref, dvalue_ref
):
    queries, keys, values, grads = query_ref[...], key_ref[...], value_ref[...], grad_ref[...]
    dquery, dkey, dvalue = [], [], []
    for group in range(2):
        columns = slice(group * HD, (group + 1) * HD)
        query, grad = two_heads(queries, group), two_heads(grads, group)
        weights = probabilities(query, keys[:, columns], first_ref[0])
        grad_weights = contract_cols(grad, values[:, columns])
        inner = jnp.sum(weights * grad_weights, axis=1, keepdims=True)
        grad_scores = (weights * (grad_weights - inner)).astype(jnp.bfloat16)
        dquery.append(side_by_side(mat(grad_scores, keys[:, columns]) * HD ** (-0.5)))
        dkey.append(contract_rows(grad_scores, query) * HD ** (-0.5))
        dvalue.append(contract_rows(weights.astype(jnp.bfloat16), grad))
    dquery_ref[...] = jnp.concatenate(dquery, axis=1)
    dkey_ref[...] = jnp.concatenate(dkey, axis=1).astype(dkey_ref.dtype)
    dvalue_ref[...] = jnp.concatenate(dvalue, axis=1).astype(dvalue_ref.dtype)


def attention_call(kernel, operands, grads, first, name):
    queries, all_kv = operands
    rows, keys = queries.shape[0], all_kv.shape[0]
    steps = KV // 2
    wide = pl.BlockSpec((rows, 4 * HD), lambda g, first: (0, g))
    key_spec = pl.BlockSpec((keys, 2 * HD), lambda g, first: (0, g))
    value_spec = pl.BlockSpec((keys, 2 * HD), lambda g, first: (0, g + steps))
    if grads is None:
        arrays, specs = (queries, all_kv, all_kv), [wide, key_spec, value_spec]
        out_shape = jax.ShapeDtypeStruct(queries.shape, jnp.bfloat16)
        out_specs = wide
    else:
        arrays, specs = (queries, all_kv, all_kv, grads), [wide, key_spec, value_spec, wide]
        out_shape = [
            jax.ShapeDtypeStruct(queries.shape, jnp.float32),
            jax.ShapeDtypeStruct((keys, KV * HD), jnp.bfloat16),
            jax.ShapeDtypeStruct((keys, KV * HD), jnp.bfloat16),
        ]
        out_specs = [wide, key_spec, key_spec]
    factor = 4 if grads is None else 10
    return pl.pallas_call(
        kernel,
        grid_spec=pltpu.PrefetchScalarGridSpec(
            num_scalar_prefetch=1, grid=(steps,), in_specs=specs, out_specs=out_specs
        ),
        out_shape=out_shape,
        compiler_params=pltpu.CompilerParams(vmem_limit_bytes=48 * 2**20),
        cost_estimate=pl.CostEstimate(
            flops=factor * rows * keys * HEADS * HD,
            bytes_accessed=4 * 2**20,
            transcendentals=rows * keys * HEADS,
        ),
        name=name,
    )(first.astype(jnp.int32).reshape(1), *arrays)


def body(
    tokens,
    cotangent,
    routes,
    query_weight,
    kv_weight,
    output_weight,
    router,
    gains,
    gate_weight,
    up_weight,
    down_weight,
    query_momentum,
    kv_momentum,
    output_momentum,
    gate_momentum,
    up_momentum,
    down_momentum,
    router_first,
    router_second,
    gains_first,
    gains_second,
):
    bf16 = jnp.bfloat16
    ctx_count = lax.axis_size("ctx")
    exp_count = lax.axis_size("exp")
    exp_index = lax.axis_index("exp")
    row_count = tokens.shape[1]
    per_group = EXPERTS // exp_count
    inputs = tokens[0].astype(jnp.float32)
    grad_out = cotangent[0].astype(jnp.float32)
    route_ids = routes[0]

    packed = jnp.concatenate(
        [
            jnp.concatenate([query_weight, kv_weight], axis=1).T,
            router.astype(bf16).T,
            jnp.pad(gains.astype(bf16).reshape(1, -1), ((0, 0), (0, D - 2 * HD))),
            jnp.zeros((5, D), bf16),
        ],
        axis=0,
    )
    mine = spread(packed, "exp", parity_groups(exp_count), exp_count // 2)
    other = core_swap(mine, exp_count)
    even = (exp_index % 2 == 0)

    def ordered(first, last):
        left, right = mine[:, first:last], other[:, first:last]
        return jnp.stack(
            [jnp.where(even, left, right), jnp.where(even, right, left)], axis=1
        ).reshape((exp_count, last - first, D))

    full_qkv = ordered(0, 2 * HD).reshape(exp_count * 2 * HD, D)
    full_router = ordered(2 * HD, 2 * HD + per_group).reshape(EXPERTS, D)
    full_gains = ordered(2 * HD + per_group, 2 * HD + per_group + 1)[:, 0, : 2 * HD]
    full_gains = full_gains.reshape(exp_count, 2, HD).transpose(1, 0, 2).reshape(2, D)
    gain_one = full_gains[0].astype(jnp.float32)
    gain_two = full_gains[1].astype(jnp.float32)

    full_experts = lax.all_gather(
        jnp.stack([gate_weight, up_weight, down_weight]), "ctx", axis=0, tiled=False
    )
    full_output = lax.all_gather(output_weight.T, "exp", axis=0, tiled=True)

    expert_ids = jnp.arange(EXPERTS, dtype=jnp.int32)
    named = jnp.any(route_ids[:, :, None] == expert_ids[None, None, :], axis=1)
    named_low = named.astype(bf16)
    token_ids = jnp.arange(row_count)
    earlier = (token_ids[None, :] < token_ids[:, None]).astype(bf16)
    rank = mat(earlier, named_low)
    place = jnp.where(named, rank + 1.0, 0.0).astype(bf16)
    slot_ids = jnp.arange(EXPERTS * CAP, dtype=jnp.int32)
    widen = (slot_ids[None, :] // CAP == expert_ids[:, None]).astype(bf16)
    chosen_slot = mat(place, widen) == (slot_ids % CAP + 1).astype(jnp.float32)[None, :]
    select = chosen_slot.astype(bf16)

    sent_grads = contract_rows(select, cotangent[0]).astype(bf16)
    grad_rows = exchange(sent_grads.reshape(exp_count, per_group * CAP, D), "exp")

    inv_one = lax.rsqrt(jnp.mean(inputs * inputs, axis=-1, keepdims=True) + eps_norm)
    normed_one = (inputs * inv_one * gain_one).astype(bf16)
    all_normed = lax.all_gather(normed_one, "exp", axis=0, tiled=True)
    projected = contract_cols(normed_one, full_qkv).reshape(row_count, exp_count, 2 * HD)
    query_raw = projected[:, :, :HD]
    kv_raw = projected[:, :, HD:]
    first_row = lax.axis_index("ctx") * row_count
    cosine, sine = rope_tables(first_row, row_count)
    queries = rotate(query_raw, cosine, sine).astype(bf16)
    keys = rotate(kv_raw[:, :KV], cosine, sine).astype(bf16)
    values = kv_raw[:, KV:].astype(bf16)
    sent_kv = jnp.concatenate([keys, values], axis=1).reshape(row_count, 2 * KV * HD)
    all_kv = spread(sent_kv, "ctx", None, ctx_count).reshape(ctx_count * row_count, 2 * KV * HD)
    flat_queries = queries.reshape(row_count, HEADS * HD)
    mixed_low = attention_call(attend_kernel, (flat_queries, all_kv), None, first_row, "attend")
    head_mixed = exchange(
        mixed_low.reshape(row_count, exp_count, HD).transpose(1, 0, 2), "exp"
    ).reshape(exp_count * row_count, HD)
    attended = mat(mixed_low, full_output)
    residual = inputs + attended
    inv_two = lax.rsqrt(jnp.mean(residual * residual, axis=-1, keepdims=True) + eps_norm)
    normed_two = (residual * inv_two * gain_two).astype(bf16)
    logits = contract_cols(normed_two, full_router)
    gates = jax.nn.softmax(jnp.where(named, logits, -1e30), axis=-1)
    gates = jnp.where(named, gates, 0.0)
    gate_parts = three_parts(gates)
    extended = jnp.concatenate(
        [normed_two, *gate_parts, jnp.zeros((row_count, WIDE - 3 * EXPERTS), bf16)], axis=1
    )
    sent_rows = contract_rows(select, extended).astype(bf16)
    arrived = exchange(sent_rows.reshape(exp_count, per_group * CAP, D + WIDE), "exp")
    produced, back, expert_grads = expert_math(
        arrived.reshape(exp_count, per_group, CAP, D + WIDE),
        grad_rows.reshape(exp_count, per_group, CAP, D),
        full_experts,
    )
    returned = exchange(back.reshape(exp_count, per_group * CAP, D + WIDE), "exp")
    returned = returned.reshape(EXPERTS * CAP, D + WIDE)
    route_values = exchange(produced.reshape(exp_count, per_group * CAP, D), "exp")
    route_values = route_values.reshape(EXPERTS * CAP, D)
    expert_sums = exchange(expert_grads, "ctx")

    summed_back = mat(select, returned)
    tail = summed_back[:, D:]
    grad_gates = (
        tail[:, :EXPERTS] + tail[:, EXPERTS : 2 * EXPERTS] + tail[:, 2 * EXPERTS : 3 * EXPERTS]
    )
    grad_logits = (
        gates * (grad_gates - jnp.sum(gates * grad_gates, axis=-1, keepdims=True))
    ).astype(bf16)
    grad_normed_two = summed_back[:, :D] + mat(grad_logits, full_router)
    scaled_two = grad_normed_two * gain_two
    grad_gain_two = jnp.sum(grad_normed_two * residual * inv_two, axis=0)
    grad_residual = (
        grad_out
        + inv_two * scaled_two
        - residual * inv_two**3 * jnp.mean(scaled_two * residual, axis=-1, keepdims=True)
    )
    grad_attended = grad_residual.astype(bf16)
    all_attended = lax.all_gather(grad_attended, "exp", axis=0, tiled=True)
    grad_mixed = contract_cols(grad_attended, full_output).astype(bf16)
    grad_queries, key_terms, value_terms = attention_call(
        attend_back_kernel, (flat_queries, all_kv), grad_mixed, first_row, "attend_back"
    )
    kv_terms = jnp.concatenate([key_terms, value_terms], axis=1)
    kv_terms = exchange(kv_terms.reshape(ctx_count, row_count, 2 * KV * HD), "ctx")
    grad_query_raw = rotate(
        grad_queries.reshape(row_count, HEADS, HD), cosine, -sine
    ).astype(bf16)
    kv_sums = jnp.sum(kv_terms.astype(jnp.float32), axis=0).reshape(row_count, 2 * KV, HD)
    grad_key_raw = rotate(kv_sums[:, :KV], cosine, -sine).astype(bf16)
    grad_kv_raw = jnp.concatenate([grad_key_raw, kv_sums[:, KV:].astype(bf16)], axis=1)
    grad_projected = jnp.concatenate([grad_query_raw, grad_kv_raw], axis=2)
    head_grads = exchange(jnp.transpose(grad_projected, (1, 0, 2)), "exp")
    head_grads = head_grads.reshape(exp_count * row_count, 2 * HD)
    grad_normed_one = mat(grad_projected.reshape(row_count, exp_count * 2 * HD), full_qkv)
    scaled_one = grad_normed_one * gain_one
    grad_gain_one = jnp.sum(grad_normed_one * inputs * inv_one, axis=0)
    input_grad = (
        grad_residual
        + inv_one * scaled_one
        - inputs * inv_one**3 * jnp.mean(scaled_one * inputs, axis=-1, keepdims=True)
    )

    small = jnp.concatenate(
        [
            contract_rows(grad_logits, normed_two),
            grad_gain_one[None],
            grad_gain_two[None],
            jnp.zeros((6, D), jnp.float32),
        ],
        axis=0,
    )
    small = lax.psum(small, ("exp", "ctx"))
    sum_router = lax.dynamic_slice(small, (exp_index * per_group, 0), (per_group, D)).T
    sum_gains = lax.dynamic_slice(small, (EXPERTS, exp_index * HD), (2, HD))
    router_one, router_two, router_new = adam_update(
        router, router_first, router_second, sum_router, router_rate, decay_rate
    )
    gains_one, gains_two, gains_new = adam_update(
        gains, gains_first, gains_second, sum_gains, gain_rate, 0.0
    )

    part = jnp.concatenate(
        [contract_rows(all_normed, head_grads), contract_rows(all_attended, head_mixed)], axis=1
    )
    part = exchange(part.astype(bf16).reshape(ctx_count, D // ctx_count, 3 * HD), "ctx")
    part = jnp.sum(part.astype(jnp.float32), axis=0)
    sums = spread(part, "ctx", None, ctx_count).reshape(D, 3 * HD)
    head_fresh, head_new = head_blocks(
        sums,
        jnp.concatenate([query_momentum, kv_momentum, output_momentum], axis=1),
        jnp.concatenate([query_weight, kv_weight, output_weight], axis=1),
    )

    expert_sums = jnp.sum(expert_sums.astype(jnp.float32), axis=0)
    momenta = jnp.stack([gate_momentum, up_momentum, down_momentum])
    fresh = mom_rate * momenta + expert_sums
    matrix_count = 3 * per_group
    rows_each = fresh.shape[2]
    sent_fresh = jnp.pad(
        fresh.astype(bf16).reshape(matrix_count, rows_each, -1),
        ((0, ctx_count - matrix_count), (0, 0), (0, 0)),
    )
    owned = exchange(sent_fresh, "ctx").reshape(ctx_count * rows_each, -1)
    ortho = owner_orthogonal(owned).astype(bf16)
    ortho = exchange(ortho.reshape(ctx_count, rows_each, -1), "ctx")
    ortho = ortho[:matrix_count].reshape(fresh.shape).astype(jnp.float32)
    new = step_weight(jnp.stack([gate_weight, up_weight, down_weight]), ortho)

    gates_wide = [mat(part, widen) for part in gate_parts]
    block_value = residual
    for wide in gates_wide:
        weighted = jnp.where(chosen_slot, wide, 0.0).astype(bf16)
        block_value = block_value + mat(weighted, route_values)
    return (
        block_value.astype(bf16)[None],
        input_grad[None],
        head_fresh[:, :HD],
        head_new[:, :HD],
        head_fresh[:, HD : 2 * HD],
        head_new[:, HD : 2 * HD],
        head_fresh[:, 2 * HD :],
        head_new[:, 2 * HD :],
        fresh[0],
        new[0],
        fresh[1],
        new[1],
        fresh[2],
        new[2],
        router_one,
        router_two,
        router_new,
        gains_one,
        gains_two,
        gains_new,
    )


def solution(mesh):
    return jax.shard_map(
        body,
        mesh=mesh,
        in_specs=(
            P("exp", "ctx", None),
            P("exp", "ctx", None),
            P("exp", "ctx", None),
            P(None, "exp"),
            P(None, "exp"),
            P(None, "exp"),
            P(None, "exp"),
            P(None, "exp"),
            P("exp", "ctx", None),
            P("exp", "ctx", None),
            P("exp", "ctx", None),
            P(None, "exp"),
            P(None, "exp"),
            P(None, "exp"),
            P("exp", "ctx", None),
            P("exp", "ctx", None),
            P("exp", "ctx", None),
            P(None, "exp"),
            P(None, "exp"),
            P(None, "exp"),
            P(None, "exp"),
        ),
        out_specs=(
            P("exp", "ctx", None),
            P("exp", "ctx", None),
            P(None, "exp"),
            P(None, "exp"),
            P(None, "exp"),
            P(None, "exp"),
            P(None, "exp"),
            P(None, "exp"),
            P("exp", "ctx", None),
            P("exp", "ctx", None),
            P("exp", "ctx", None),
            P("exp", "ctx", None),
            P("exp", "ctx", None),
            P("exp", "ctx", None),
            P(None, "exp"),
            P(None, "exp"),
            P(None, "exp"),
            P(None, "exp"),
            P(None, "exp"),
            P(None, "exp"),
        ),
        check_vma=False,
    )
```

time: 1680 us -> 785 us (0.47)
  waiting for transfers between devices: 1180 us -> 426 us
  matrix products: 155 us -> 43 us
  Pallas kernels: 0 us -> 65.5 us
  local copies, waits for them, and re-layouts: 89.6 us -> 46 us
  blocking collectives: 129 us -> 87.3 us
  other arithmetic: 61.2 us -> 33.9 us
  starting transfers between devices: 37.3 us -> 58.6 us
    reduce_scatter x6 -> x0, waiting for transfers between devices: 609 us -> none  [the longest x1 311 us: body(): lax.psum_scatter(pad_slots(jnp.concatenate([grad_gate, grad_up, grad_down...]
    all_gather x8 -> x4, waiting for transfers between devices: 257 us -> 1.98 us  [the longest x1 1.92 us: body(): lax.all_gather(jnp.stack([gate_weight, up_weight, down_weight]), 'ctx', a...]
    all_to_all x7 -> x12, waiting for transfers between devices: 88.6 us -> 334 us  [exchange(): lax.all_to_all(blocks, axis, split_axis=0, concat_axis=0, tiled=True, axi...]
    unnamed x19 -> x5, waiting for transfers between devices: 165 us -> 0.75 us
    dot_general x79 -> x26, matrix products: 139 us -> 22.2 us  [the longest x8 15.6 us: mat(): return jnp.dot(left, right, preferred_element_type=jnp.float32)]
    all_gather x2 -> x0, blocking collectives: 109 us -> none  [the longest x1 85.1 us: body(): lax.all_gather(router.astype(jnp.bfloat16), 'exp', axis=1, tiled=True)]
    all_to_all x0 -> x2, blocking collectives: none -> 87.3 us  [exchange(): lax.all_to_all(blocks, axis, split_axis=0, concat_axis=0, tiled=True, axi...]
    pallas_call x0 -> x4, Pallas kernels: none -> 65.5 us  [the longest x1 26.6 us: expert_math(): pl.pallas_call(expert_kernel, grid_spec=pltpu.PrefetchScalarGridSpec(num_...]
  transfers between devices with their start and end apart: 24 -> 18, of which waited for: 20 -> 11; matrix products, arithmetic and copies ran while one was open for 15% -> 14% of each run, Pallas kernels for 0% -> 5%
where the time goes in v1:
time: 785 us; the launch traced here: 775 us
  waiting for transfers between devices  426 us (54%)
  blocking collectives  87.3 us (11%)
  Pallas kernels  65.5 us (8%)
  starting transfers between devices  58.6 us (7%)
  local copies, waits for them, and re-layouts  46 us (6%)
  matrix products  43 us (5%)
  other arithmetic  33.9 us (4%)
  between operations  15.6 us (2%)
    all_to_all x12, waiting for transfers between devices, exchange(): lax.all_to_all(blocks, axis, split_axis=0, concat_axis=0, tiled=True, axi...  334 us
    all_to_all x2, blocking collectives, exchange(): lax.all_to_all(blocks, axis, split_axis=0, concat_axis=0, tiled=True, axi...  87.3 us
    psum x1, waiting for transfers between devices, body(): small = lax.psum(small, ('exp', 'ctx'))  87.2 us
    all_to_all x12, starting transfers between devices, exchange(): lax.all_to_all(blocks, axis, split_axis=0, concat_axis=0, tiled=True, axi...  58.1 us
    pallas_call x1, Pallas kernels, expert_math(): pl.pallas_call(expert_kernel, grid_spec=pltpu.PrefetchScalarGridSpec(num_...  26.6 us
    pallas_call x1, Pallas kernels, owner_orthogonal(): pl.pallas_call(owner_kernel, out_shape=jax.ShapeDtypeStruct(stacked.shape...  20.5 us
    pallas_call x2, Pallas kernels, attention_call(): pl.pallas_call(kernel, grid_spec=pltpu.PrefetchScalarGridSpec(num_scalar_...  18.4 us
    dot_general x6, matrix products, contract_rows(): lax.dot_general(left, right, (((0,), (0,)), ((), ())), preferred_element_...  16.6 us
  transfers between devices with their start and end apart: 18, of which 11 were waited for; matrix products, arithmetic and copies ran while one was open for 14% of the time, Pallas kernels for 5%

profile of v1, /device:TPU:0, one launch (start us, length us, event | category | flops | bytes accessed | tf_op | source)
XLA Modules:
  0.0 775.5 jit_solution(3631088918134001517)
XLA Ops:
  10.9 38.2 %all_to_all.70 = bf16[8,136,1024]{2,1,0:T(8,128)(2,1)S(1)} all-to-all(bf16[8,136,1024]{2,1,0:T(8,128)(2,1)S(1)} %broadcast_in_dim.46), channel_id=1, replica_groups={{0,2,4,6,8,10,12,14},{1,3,5,7,9,11,13,15},{16,18,20,22,24,26,28,30},{17..., dimensions={0} | all-to-all | bytes 4456448 | tf_op jit(solution)/shard_map/all_to_all | solution.py:66
  65.4 5.7 all-to-all-start.1
  74.3 43.4 %all-to-all-done.1 = bf16[8,128,1024]{2,1,0:T(8,128)(2,1)S(1)} async-done(((bf16[8,128,1024]{2,1,0:T(8,128)(2,1)}), bf16[8,128,1024]{2,1,0:T(8,128)(2,1)S(1)}, u32[]{:S(2)}, u32[]{:S(2)}) %all-to-all-start.1) | async-done | bytes 2097184 | tf_op jit(solution)/shard_map/all_to_all | solution.py:66
  117.6 4.8 all-to-all-start.3
  124.3 7.2 attend.1
  138.2 3.9 convolution_convert_fusion
  142.0 54.9 %all-to-all-done.3 = bf16[16,96,1024]{2,1,0:T(8,128)(2,1)} async-done(((bf16[16,96,1024]{2,1,0:T(8,128)(2,1)}), bf16[16,96,1024]{2,1,0:T(8,128)(2,1)}, u32[]{:S(2)}, u32[]{:S(2)}) %all-to-all-start.3) | async-done | bytes 3145760 | tf_op jit(solution)/shard_map/all_to_all | solution.py:66
  196.9 4.5 all-to-all-start.2
  201.5 82.9 %all-to-all-done.2 = bf16[16,96,1152]{2,1,0:T(8,128)(2,1)} async-done(((bf16[16,96,1152]{2,1,0:T(8,128)(2,1)}), bf16[16,96,1152]{2,1,0:T(8,128)(2,1)}, u32[]{:S(2)}, u32[]{:S(2)}) %all-to-all-start.2) | async-done | bytes 3538976 | tf_op jit(solution)/shard_map/all_to_all | solution.py:66
  286.3 26.6 %experts.1 = (bf16[16,2,48,1024]{3,2,1,0:T(8,128)(2,1)}, bf16[16,2,48,1152]{3,2,1,0:T(8,128)(2,1)}, bf16[8,3,2,128,512]{4,3,2,1,0:T(8,128)(2,1)}) custom-call(s32[1]{0:T(128)} %bitcast.19.own_ref, bf16[16,2,48,1152]{3,2,1,0:T(8,128)(2,1)} %bitcast.21.arrived_ref, bf16[16,2,48,1024]{3,2,1,0:T(8,128)(2,1)} %bitcast.24.grads_ref, ...), custom_call_target="tpu_custom_call" | custom-call | flops 14495514624 | bytes 31457280 | tf_op jit(solution)/shard_map/experts/pallas_call | solution.py:238
  312.9 49.1 %all_to_all.71 = bf16[16,96,1152]{2,1,0:T(8,128)(2,1)S(1)} all-to-all(bf16[16,96,1152]{2,1,0:T(8,128)(2,1)} %bitcast.235), channel_id=1, replica_groups=mesh['ctx'=8,'exp'=16] {'exp'}, dimensions={0} | all-to-all | bytes 7077888 | tf_op jit(solution)/shard_map/all_to_all | solution.py:66
  365.9 3.7 all-to-all-start.8
  372.2 11.2 %attend_back.1 = (f32[128,1024]{1,0:T(8,128)S(1)}, bf16[1024,512]{1,0:T(8,128)(2,1)S(1)}, bf16[1024,512]{1,0:T(8,128)(2,1)S(1)}) custom-call(s32[1]{0:T(128)} %bitcast.1.first_ref, bf16[128,1024]{1,0:T(8,128)(2,1)S(1)} %copy.131.query_ref, bf16[1024,1024]{1,0:T(8,128)(2,1)S(1)} %bitcast.218, bf16[1024,1024]{1,0:T(8,128)(2,1)S(1)} %bitcast.219, ...), custom_call_target="tpu_custom_call" | custom-call | flops 1342177280 | bytes 4194304 | tf_op jit(solution)/shard_map/attend_back/pallas_call | solution.py:395
  385.1 4.3 all-to-all-start.6
  390.4 37.8 %all-to-all-done.6 = bf16[8,128,1024]{2,1,0:T(8,128)(2,1)S(1)} async-done(((bf16[8,128,1024]{2,1,0:T(8,128)(2,1)}), bf16[8,128,1024]{2,1,0:T(8,128)(2,1)S(1)}, u32[]{:S(2)}, u32[]{:S(2)}) %all-to-all-start.6) | async-done | bytes 2097184 | tf_op jit(solution)/shard_map/all_to_all | solution.py:66
  429.5 7.6 all-to-all-start.4
  451.4 29.2 %all-to-all-done.4 = bf16[16,96,1024]{2,1,0:T(8,128)(2,1)S(1)} async-done(((bf16[16,96,1024]{2,1,0:T(8,128)(2,1)}), bf16[16,96,1024]{2,1,0:T(8,128)(2,1)S(1)}, u32[]{:S(2)}, u32[]{:S(2)}) %all-to-all-start.4) | async-done | bytes 3145760 | tf_op jit(solution)/shard_map/all_to_all | solution.py:66
  480.6 4.8 all-to-all-start.11
  502.0 66.5 %all-to-all-done.11 = bf16[8,3,2,128,512]{4,3,2,1,0:T(8,128)(2,1)} async-done(((bf16[8,3,2,128,512]{4,3,2,1,0:T(8,128)(2,1)}), bf16[8,3,2,128,512]{4,3,2,1,0:T(8,128)(2,1)}, u32[]{:S(2)}, u32[]{:S(2)}) %all-to-all-start.11) | async-done | bytes 6291488 | tf_op jit(solution)/shard_map/all_to_all | solution.py:66
  568.5 3.6 all-to-all-start.7
  572.2 4.1 convert_reduce_fusion
  577.8 6.7 all-to-all-done.7
  590.5 6.5 copy.158
  597.0 3.6 convolution_convert_fusion.4
  600.6 6.5 copy.156
  607.1 3.7 convolution_convert_fusion.3
  611.6 5.6 all-to-all-start.9
  617.2 20.5 %owner.1 = bf16[1024,512]{1,0:T(8,128)(2,1)} custom-call(bf16[1024,512]{1,0:T(8,128)(2,1)S(1)} %bitcast.220), custom_call_target="tpu_custom_call" | custom-call | flops 20937965568 | bytes 2097152 | tf_op jit(solution)/shard_map/owner/pallas_call | solution.py:305
  637.7 5.8 all-to-all-start.13
  646.9 87.2 %all-reduce.4.cloned.1.call-done = f32[40,1024]{1,0:T(8,128)} async-done(((f32[40,1024]{1,0:T(8,128)}), f32[40,1024]{1,0:T(8,128)}) %all-reduce.4.cloned.1.call-update) | async-done | bytes 163856 | tf_op jit(solution)/shard_map/psum | solution.py:583
  740.1 4.2 all-to-all-start.10
  746.1 12.4 %all-to-all-done.10 = f32[8,128,192]{1,2,0:T(8,128)S(1)} async-done(((f32[8,128,192]{1,2,0:T(8,128)}), f32[8,128,192]{1,2,0:T(8,128)S(1)}, u32[]{:S(2)}, u32[]{:S(2)}) %all-to-all-start.10) | async-done | bytes 786464 | tf_op jit(solution)/shard_map/all_to_all | solution.py:66
  (271 shorter events, 103.5 us)
Async XLA Ops:
  7.2 124.4 %all-gather.6.cloned.1.call-start = ((), (), s32[]{:S(2)}) async-start(), calls=%async_computation.14 | async-start | bytes 2228224 | tf_op jit(solution)/shard_map/all_gather | solution.py:473
  7.9 278.4 %all-gather.12.cloned.1.call-start = ((), (), s32[]{:S(2)}) async-start(), calls=%async_computation.18 | async-start | bytes 7077888 | tf_op jit(solution)/shard_map/all_gather | solution.py:470
  50.3 4.6 collective-permute-start
  65.4 52.3 %all-to-all-start.1 = ((bf16[8,128,1024]{2,1,0:T(8,128)(2,1)}), bf16[8,128,1024]{2,1,0:T(8,128)(2,1)S(1)}, u32[]{:S(2)}, u32[]{:S(2)}) async-start(bf16[8,128,1024]{2,1,0:T(8,128)(2,1)} %broadcast_in_dim.49), calls=%async_computation.1 | async-start | bytes 4194304 | tf_op jit(solution)/shard_map/all_to_all | solution.py:66
  117.6 79.3 %all-to-all-start.3 = ((bf16[16,96,1024]{2,1,0:T(8,128)(2,1)}), bf16[16,96,1024]{2,1,0:T(8,128)(2,1)}, u32[]{:S(2)}, u32[]{:S(2)}) async-start(bf16[16,96,1024]{2,1,0:T(8,128)(2,1)} %bitcast.230), calls=%async_computation.3 | async-start | bytes 6291456 | tf_op jit(solution)/shard_map/all_to_all | solution.py:66
  133.7 230.2 %copy-start.2 = (f32[128,1024]{1,0:T(8,128)}, f32[128,1024]{1,0:T(8,128)S(1)}, u32[]{:S(2)}) copy-start(f32[128,1024]{1,0:T(8,128)S(1)} %get-tuple-element.88) | copy-start | bytes 1572868
  196.9 87.5 %all-to-all-start.2 = ((bf16[16,96,1152]{2,1,0:T(8,128)(2,1)}), bf16[16,96,1152]{2,1,0:T(8,128)(2,1)}, u32[]{:S(2)}, u32[]{:S(2)}) async-start(bf16[16,96,1152]{2,1,0:T(8,128)(2,1)} %bitcast.228), calls=%async_computation.2 | async-start | bytes 7077888 | tf_op jit(solution)/shard_map/all_to_all | solution.py:66
  201.5 389.0 %all-gather.10.cloned.1.call-start = ((), (), s32[]{:S(2)}) async-start(), calls=%async_computation.16 | async-start | bytes 4456448 | tf_op jit(solution)/shard_map/all_gather | solution.py:549
  365.9 19.2 %all-to-all-start.8 = ((bf16[16,128,64]{1,2,0:T(8,128)(2,1)}), bf16[16,128,64]{1,2,0:T(8,128)(2,1)S(1)}, u32[]{:S(2)}, u32[]{:S(2)}) async-start(bf16[16,128,64]{1,2,0:T(8,128)(2,1)} %bitcast.48), calls=%async_computation.8 | async-start | bytes 524288 | tf_op jit(solution)/shard_map/all_to_all | solution.py:66
  385.1 43.0 %all-to-all-start.6 = ((bf16[8,128,1024]{2,1,0:T(8,128)(2,1)}), bf16[8,128,1024]{2,1,0:T(8,128)(2,1)S(1)}, u32[]{:S(2)}, u32[]{:S(2)}) async-start(bf16[8,128,1024]{2,1,0:T(8,128)(2,1)} %bitcast.231), calls=%async_computation.6 | async-start | bytes 4194304 | tf_op jit(solution)/shard_map/all_to_all | solution.py:66
  429.5 51.1 %all-to-all-start.4 = ((bf16[16,96,1024]{2,1,0:T(8,128)(2,1)}), bf16[16,96,1024]{2,1,0:T(8,128)(2,1)S(1)}, u32[]{:S(2)}, u32[]{:S(2)}) async-start(bf16[16,96,1024]{2,1,0:T(8,128)(2,1)} %bitcast.236), calls=%async_computation.4 | async-start | bytes 6291456 | tf_op jit(solution)/shard_map/all_to_all | solution.py:66
  437.1 163.5 %all-gather.8.cloned.1.call-start = ((), (), s32[]{:S(2)}) async-start(), calls=%async_computation.15 | async-start | bytes 4456448 | tf_op jit(solution)/shard_map/all_gather | solution.py:492
  480.6 15.2 %copy-start = (bf16[16,96,1024]{2,1,0:T(8,128)(2,1)}, bf16[16,96,1024]{2,1,0:T(8,128)(2,1)S(1)}, u32[]{:S(2)}) copy-start(bf16[16,96,1024]{2,1,0:T(8,128)(2,1)S(1)} %all-to-all-done.4) | copy-start | bytes 9437188
  480.6 87.9 %all-to-all-start.11 = ((bf16[8,3,2,128,512]{4,3,2,1,0:T(8,128)(2,1)}), bf16[8,3,2,128,512]{4,3,2,1,0:T(8,128)(2,1)}, u32[]{:S(2)}, u32[]{:S(2)}) async-start(bf16[8,3,2,128,512]{4,3,2,1,0:T(8,128)(2,1)} %get-tuple-element.31), calls=%async_computation.11 | async-start | bytes 12582912 | tf_op jit(solution)/shard_map/all_to_all | solution.py:66
  568.5 15.9 %all-to-all-start.7 = ((bf16[16,128,128]{1,2,0:T(8,128)(2,1)}), bf16[16,128,128]{1,2,0:T(8,128)(2,1)S(1)}, u32[]{:S(2)}, u32[]{:S(2)}) async-start(bf16[16,128,128]{1,2,0:T(8,128)(2,1)} %fusion.178), calls=%async_computation.7 | async-start | bytes 1048576 | tf_op jit(solution)/shard_map/all_to_all | solution.py:66
  576.7 11.7 %copy-start.28 = (f32[32,1024]{1,0:T(8,128)S(1)}, f32[32,1024]{1,0:T(8,128)}, u32[]{:S(2)}) copy-start(f32[32,1024]{1,0:T(8,128)} %fusion.118) | copy-start | bytes 393220
  576.7 11.7 %copy-start.50 = (f32[1024]{0:T(1024)S(1)}, f32[1024]{0:T(1024)}, u32[]{:S(2)}) copy-start(f32[1024]{0:T(1024)} %get-tuple-element.32) | copy-start | bytes 12292
  584.5 27.1 %all-to-all-start.12 = ((bf16[8,128,512]{2,1,0:T(8,128)(2,1)}), bf16[8,128,512]{2,1,0:T(8,128)(2,1)S(1)}, u32[]{:S(2)}, u32[]{:S(2)}) async-start(bf16[8,128,512]{2,1,0:T(8,128)(2,1)} %pad.9), calls=%async_computation.12 | async-start | bytes 2097152 | tf_op jit(solution)/shard_map/all_to_all | solution.py:66
  588.0 146.0 %all-reduce.4.cloned.1.call-start = ((), (), s32[]{:S(2)}) async-start(), calls=%async_computation.17 | async-start | bytes 327680 | tf_op jit(solution)/shard_map/psum | solution.py:583
  611.6 26.1 %all-to-all-start.9 = ((bf16[8,128,192]{1,2,0:T(8,128)(2,1)}), bf16[8,128,192]{1,2,0:T(8,128)(2,1)}, u32[]{:S(2)}, u32[]{:S(2)}) async-start(bf16[8,128,192]{1,2,0:T(8,128)(2,1)} %pad_maximum_fusion.3), calls=%async_computation.9 | async-start | bytes 786432 | tf_op jit(solution)/shard_map/all_to_all | solution.py:66
  617.2 26.3 %copy-start.36 = (bf16[128,32]{1,0:T(8,128)(2,1)S(1)}, bf16[128,32]{1,0:T(8,128)(2,1)}, u32[]{:S(2)}) copy-start(bf16[128,32]{1,0:T(8,128)(2,1)} %copy-done.35) | copy-start | bytes 24580
  637.7 101.4 %all-to-all-start.13 = ((bf16[8,128,512]{2,1,0:T(8,128)(2,1)}), bf16[8,128,512]{2,1,0:T(8,128)(2,1)S(1)}, u32[]{:S(2)}, u32[]{:S(2)}) async-start(bf16[8,128,512]{2,1,0:T(8,128)(2,1)} %bitcast.56), calls=%async_computation.13 | async-start | bytes 2097152 | tf_op jit(solution)/shard_map/all_to_all | solution.py:66
  643.5 90.5 %copy-start.58 = (f32[2,64]{1,0:T(2,128)S(1)}, f32[2,64]{1,0:T(2,128)}, u32[]{:S(2)}) copy-start(f32[2,64]{1,0:T(2,128)} %param.28) | copy-start | bytes 1540
  643.5 90.5 %copy-start.59 = (f32[2,64]{1,0:T(2,128)S(1)}, f32[2,64]{1,0:T(2,128)}, u32[]{:S(2)}) copy-start(f32[2,64]{1,0:T(2,128)} %param.41) | copy-start | bytes 1540
  643.5 90.5 %copy-start.60 = (f32[2,64]{1,0:T(2,128)S(1)}, f32[2,64]{1,0:T(2,128)}, u32[]{:S(2)}) copy-start(f32[2,64]{1,0:T(2,128)} %param.40) | copy-start | bytes 1540
  643.6 91.8 %copy-start.49 = (f32[1024,2]{0,1:T(2,128)S(1)}, f32[1024,2]{0,1:T(2,128)}, u32[]{:S(2)}) copy-start(f32[1024,2]{0,1:T(2,128)} %param.27) | copy-start | bytes 24580
  643.6 91.8 %copy-start.51 = (f32[1024,2]{0,1:T(2,128)S(1)}, f32[1024,2]{0,1:T(2,128)}, u32[]{:S(2)}) copy-start(f32[1024,2]{0,1:T(2,128)} %param.39) | copy-start | bytes 24580
  643.6 91.8 %copy-start.52 = (f32[1024,2]{0,1:T(2,128)S(1)}, f32[1024,2]{0,1:T(2,128)}, u32[]{:S(2)}) copy-start(f32[1024,2]{0,1:T(2,128)} %param.38) | copy-start | bytes 24580
  740.1 18.5 %all-to-all-start.10 = ((f32[8,128,192]{1,2,0:T(8,128)}), f32[8,128,192]{1,2,0:T(8,128)S(1)}, u32[]{:S(2)}, u32[]{:S(2)}) async-start(f32[8,128,192]{1,2,0:T(8,128)} %broadcast_in_dim.61), calls=%async_computation.10 | async-start | bytes 1572864 | tf_op jit(solution)/shard_map/all_to_all | solution.py:66
  744.9 13.6 %copy-start.38 = (f32[8,128,64]{1,2,0:T(8,128)S(1)}, f32[8,128,64]{1,2,0:T(8,128)}, u32[]{:S(2)}) copy-start(f32[8,128,64]{1,2,0:T(8,128)} %copy_bitcast_fusion.2) | copy-start | bytes 786436
  744.9 13.6 %copy-start.39 = (f32[8,128,64]{1,2,0:T(8,128)S(1)}, f32[8,128,64]{1,2,0:T(8,128)}, u32[]{:S(2)}) copy-start(f32[8,128,64]{1,2,0:T(8,128)} %get-tuple-element.97) | copy-start | bytes 786436
  744.9 13.6 %copy-start.40 = (f32[8,128,64]{1,2,0:T(8,128)S(1)}, f32[8,128,64]{1,2,0:T(8,128)}, u32[]{:S(2)}) copy-start(f32[8,128,64]{1,2,0:T(8,128)} %get-tuple-element.98) | copy-start | bytes 786436
  (50 other events, 174.3 us)
Sparse Core Ops, SparseCore 0:
  10.5 55.9 all-gather.5
  68.2 218.1 all-gather.11
  365.2 63.4 all-gather.9
  451.5 71.2 all-gather.7
  593.9 140.1 all-reduce.3

commit v2 on v1

--- a/solution.py
+++ b/solution.py
@@ -60,6 +60,7 @@
 FF = 512
 ROWS = 16 * CAP
 CHUNKS = 2
+LOCAL = 128
 
 
 def exchange(blocks, axis, groups=None):
@@ -78,6 +79,27 @@
 
 def core_swap(block, count):
     return lax.ppermute(block, "exp", [(i, i ^ 1) for i in range(count)])
+
+
+def ctx_move(block, up, other):
+    pairs = [
+        (2 * z + x, 2 * ((z + up) % 4) + (x ^ other)) for z in range(4) for x in range(2)
+    ]
+    return lax.ppermute(block, "ctx", pairs)
+
+
+def gather_rows(block):
+    same = jnp.stack([block, ctx_move(block, 0, 1)])
+    below = ctx_move(same, 1, 0)
+    above = ctx_move(same, 3, 0)
+    return same, below, above, ctx_move(below[0], 1, 0), ctx_move(above[1], 3, 0)
+
+
+def reduce_rows(same, up, down, far):
+    total = same.astype(jnp.float32) + ctx_move(up, 1, 0).astype(jnp.float32)
+    total = total + ctx_move(down, 3, 0).astype(jnp.float32)
+    total = total + ctx_move(far, 2, 0).astype(jnp.float32)
+    return total[0] + ctx_move(total[1].astype(jnp.bfloat16), 0, 1).astype(jnp.float32)
 
 
 def three_parts(value):
@@ -155,12 +177,25 @@
     return fresh, step_weight(weights, ortho)
 
 
-def expert_kernel(own_ref, arrived_ref, grads_ref, weight_ref, made_ref, back_ref, sums_ref,
-                  rows_ref, hidden_ref, dgate_ref, dup_ref, dy_ref):
+def expert_kernel(own_ref, arrived_ref, grads_ref, same_ref, below_ref, above_ref, far_ref, far_two_ref,
+                  made_ref, back_ref, sums_ref, sums_up_ref, sums_down_ref, sums_far_ref,
+                  weight_ref, rows_ref, hidden_ref, dgate_ref, dup_ref, dy_ref):
     expert = own_ref[0] + pl.program_id(0)
-    full_gate = weight_ref[:, 0, 0].reshape(D, FF)
-    full_up = weight_ref[:, 1, 0].reshape(D, FF)
-    full_down = weight_ref[:, 2, 0].reshape(D, FF)
+    level, side = own_ref[1], own_ref[2]
+    width = D // 8
+
+    def part(up, other):
+        index = 2 * lax.rem(level + up, 4) + (1 - side if other else side)
+        return pl.ds(pl.multiple_of(index * width, width), width)
+
+    for up, ref in ((0, same_ref), (3, below_ref), (1, above_ref)):
+        for other in range(2):
+            for kind in range(3):
+                weight_ref[kind, part(up, other)] = ref[other, kind, 0]
+    for kind in range(3):
+        weight_ref[kind, part(2, 0)] = far_ref[kind, 0]
+        weight_ref[kind, part(2, 1)] = far_two_ref[kind, 0]
+    full_gate, full_up, full_down = weight_ref[0], weight_ref[1], weight_ref[2]
     chunk = ROWS // CHUNKS
     seqs = chunk // CAP
 
@@ -181,7 +216,15 @@
         hidden = (activated * up_pre).astype(jnp.bfloat16)
         made = contract_cols(hidden, full_down).astype(jnp.bfloat16)
         made_ref[pl.ds(first, seqs), 0] = made.reshape(seqs, CAP, D)
-        grad_f32 = grads_ref[pl.ds(first, seqs), 0].reshape(chunk, D).astype(jnp.float32)
+        slot_ids = lax.broadcasted_iota(jnp.int32, (LOCAL, CAP), 1).astype(jnp.float32) + 1.0
+        token_lane = lax.broadcasted_iota(jnp.int32, (LOCAL, WIDE), 1)
+        taken = []
+        for seq in range(seqs):
+            source = grads_ref[first + seq]
+            places = jnp.where(token_lane == expert, source[:, D:].astype(jnp.float32), 0.0)
+            chosen = jnp.sum(places, axis=1, keepdims=True) == slot_ids
+            taken.append(contract_rows(chosen.astype(jnp.bfloat16), source[:, :D]))
+        grad_f32 = jnp.concatenate(taken, axis=0)
         grad_made = (gate * grad_f32).astype(jnp.bfloat16)
         grad_gate_value = jnp.sum(made.astype(jnp.float32) * grad_f32, axis=1, keepdims=True)
         grad_hidden = mat(grad_made, full_down)
@@ -208,41 +251,38 @@
         return carry
 
     lax.fori_loop(0, CHUNKS, forward, 0)
-    parts = sums_ref.shape[0]
-    width = D // parts
-
-    def gradients(part, carry):
-        columns = pl.ds(pl.multiple_of(part * width, width), width)
-        rows = rows_ref[:, columns]
-        sums_ref[part, 0, 0] = contract_rows(rows, dgate_ref[...]).astype(jnp.bfloat16)
-        sums_ref[part, 1, 0] = contract_rows(rows, dup_ref[...]).astype(jnp.bfloat16)
-        sums_ref[part, 2, 0] = contract_rows(dy_ref[:, columns], hidden_ref[...]).astype(
-            jnp.bfloat16
-        )
-        return carry
-
-    lax.fori_loop(0, parts, gradients, 0)
-
-
-def expert_math(arrived, grad_rows, weights):
+    for up, ref in ((0, sums_ref), (1, sums_up_ref), (3, sums_down_ref), (2, sums_far_ref)):
+        for other in range(2):
+            columns = part(up, other)
+            rows = rows_ref[:, columns]
+            ref[other, 0, 0] = contract_rows(rows, dgate_ref[...]).astype(jnp.bfloat16)
+            ref[other, 1, 0] = contract_rows(rows, dup_ref[...]).astype(jnp.bfloat16)
+            ref[other, 2, 0] = contract_rows(dy_ref[:, columns], hidden_ref[...]).astype(
+                jnp.bfloat16
+            )
+
+
+def expert_math(arrived, all_grads, weights):
     seqs, per_group = arrived.shape[:2]
-    own = (lax.axis_index("exp") * per_group).astype(jnp.int32).reshape(1)
-    count = weights.shape[0]
+    place = lax.axis_index("ctx")
+    own = jnp.stack([lax.axis_index("exp") * per_group, place // 2, place % 2]).astype(jnp.int32)
+    rows_each = D // 8
 
     def rows_spec(width):
         return pl.BlockSpec((seqs, 1, CAP, width), lambda e, own: (0, e, 0, 0))
 
-    weight_spec = pl.BlockSpec(
-        (count, 3, 1, D // count, FF), lambda e, own: (0, 0, e, 0, 0)
-    )
+    two = pl.BlockSpec((2, 3, 1, rows_each, FF), lambda e, own: (0, 0, e, 0, 0))
+    one = pl.BlockSpec((3, 1, rows_each, FF), lambda e, own: (0, e, 0, 0))
+    whole = pl.BlockSpec(all_grads.shape, lambda e, own: (0, 0, 0))
     return pl.pallas_call(
         expert_kernel,
         grid_spec=pltpu.PrefetchScalarGridSpec(
             num_scalar_prefetch=1,
             grid=(per_group,),
-            in_specs=[rows_spec(D + WIDE), rows_spec(D), weight_spec],
-            out_specs=[rows_spec(D), rows_spec(D + WIDE), weight_spec],
+            in_specs=[rows_spec(D + WIDE), whole, two, two, two, one, one],
+            out_specs=[rows_spec(D), rows_spec(D + WIDE), two, two, two, two],
             scratch_shapes=[
+                pltpu.VMEM((3, D, FF), jnp.bfloat16),
                 pltpu.VMEM((ROWS, D), jnp.bfloat16),
                 pltpu.VMEM((ROWS, FF), jnp.bfloat16),
                 pltpu.VMEM((ROWS, FF), jnp.bfloat16),
@@ -253,8 +293,8 @@
         out_shape=[
             jax.ShapeDtypeStruct((seqs, per_group, CAP, D), jnp.bfloat16),
             jax.ShapeDtypeStruct((seqs, per_group, CAP, D + WIDE), jnp.bfloat16),
-            jax.ShapeDtypeStruct(weights.shape, jnp.bfloat16),
-        ],
+        ]
+        + [jax.ShapeDtypeStruct((2, 3, per_group, rows_each, FF), jnp.bfloat16)] * 4,
         compiler_params=pltpu.CompilerParams(vmem_limit_bytes=56 * 2**20),
         cost_estimate=pl.CostEstimate(
             flops=18 * ROWS * per_group * D * FF,
@@ -262,7 +302,7 @@
             transcendentals=ROWS * per_group * FF,
         ),
         name="experts",
-    )(own, arrived, grad_rows, weights)
+    )(own, arrived, all_grads, *weights)
 
 
 def split_two(value):
@@ -467,9 +507,7 @@
     gain_one = full_gains[0].astype(jnp.float32)
     gain_two = full_gains[1].astype(jnp.float32)
 
-    full_experts = lax.all_gather(
-        jnp.stack([gate_weight, up_weight, down_weight]), "ctx", axis=0, tiled=False
-    )
+    full_experts = gather_rows(jnp.stack([gate_weight, up_weight, down_weight]))
     full_output = lax.all_gather(output_weight.T, "exp", axis=0, tiled=True)
 
     expert_ids = jnp.arange(EXPERTS, dtype=jnp.int32)
@@ -484,12 +522,13 @@
     chosen_slot = mat(place, widen) == (slot_ids % CAP + 1).astype(jnp.float32)[None, :]
     select = chosen_slot.astype(bf16)
 
-    sent_grads = contract_rows(select, cotangent[0]).astype(bf16)
-    grad_rows = exchange(sent_grads.reshape(exp_count, per_group * CAP, D), "exp")
+    sent_grads = jnp.concatenate(
+        [cotangent[0], place, jnp.zeros((row_count, WIDE - EXPERTS), bf16)], axis=1
+    )
+    all_grads = lax.all_gather(sent_grads, "exp", axis=0, tiled=False)
 
     inv_one = lax.rsqrt(jnp.mean(inputs * inputs, axis=-1, keepdims=True) + eps_norm)
     normed_one = (inputs * inv_one * gain_one).astype(bf16)
-    all_normed = lax.all_gather(normed_one, "exp", axis=0, tiled=True)
     projected = contract_cols(normed_one, full_qkv).reshape(row_count, exp_count, 2 * HD)
     query_raw = projected[:, :, :HD]
     kv_raw = projected[:, :, HD:]
@@ -502,9 +541,8 @@
     all_kv = spread(sent_kv, "ctx", None, ctx_count).reshape(ctx_count * row_count, 2 * KV * HD)
     flat_queries = queries.reshape(row_count, HEADS * HD)
     mixed_low = attention_call(attend_kernel, (flat_queries, all_kv), None, first_row, "attend")
-    head_mixed = exchange(
-        mixed_low.reshape(row_count, exp_count, HD).transpose(1, 0, 2), "exp"
-    ).reshape(exp_count * row_count, HD)
+    sent_mixed = mixed_low.reshape(row_count, exp_count, HD).transpose(1, 0, 2)
+    sent_mixed = sent_mixed.reshape(exp_count, row_count * HD // D, D)
     attended = mat(mixed_low, full_output)
     residual = inputs + attended
     inv_two = lax.rsqrt(jnp.mean(residual * residual, axis=-1, keepdims=True) + eps_norm)
@@ -518,16 +556,20 @@
     )
     sent_rows = contract_rows(select, extended).astype(bf16)
     arrived = exchange(sent_rows.reshape(exp_count, per_group * CAP, D + WIDE), "exp")
-    produced, back, expert_grads = expert_math(
-        arrived.reshape(exp_count, per_group, CAP, D + WIDE),
-        grad_rows.reshape(exp_count, per_group, CAP, D),
-        full_experts,
+    later_normed, arrived = lax.optimization_barrier((normed_one, arrived))
+    all_normed = lax.all_gather(later_normed, "exp", axis=0, tiled=True)
+    produced, back, *expert_grads = expert_math(
+        arrived.reshape(exp_count, per_group, CAP, D + WIDE), all_grads, full_experts
     )
     returned = exchange(back.reshape(exp_count, per_group * CAP, D + WIDE), "exp")
     returned = returned.reshape(EXPERTS * CAP, D + WIDE)
-    route_values = exchange(produced.reshape(exp_count, per_group * CAP, D), "exp")
-    route_values = route_values.reshape(EXPERTS * CAP, D)
-    expert_sums = exchange(expert_grads, "ctx")
+    route_values = exchange(
+        jnp.concatenate([produced.reshape(exp_count, per_group * CAP, D), sent_mixed], axis=1),
+        "exp",
+    )
+    head_mixed = route_values[:, per_group * CAP :].reshape(exp_count * row_count, HD)
+    route_values = route_values[:, : per_group * CAP].reshape(EXPERTS * CAP, D)
+    expert_sums = reduce_rows(*expert_grads)
 
     summed_back = mat(select, returned)
     tail = summed_back[:, D:]
@@ -560,8 +602,6 @@
     grad_key_raw = rotate(kv_sums[:, :KV], cosine, -sine).astype(bf16)
     grad_kv_raw = jnp.concatenate([grad_key_raw, kv_sums[:, KV:].astype(bf16)], axis=1)
     grad_projected = jnp.concatenate([grad_query_raw, grad_kv_raw], axis=2)
-    head_grads = exchange(jnp.transpose(grad_projected, (1, 0, 2)), "exp")
-    head_grads = head_grads.reshape(exp_count * row_count, 2 * HD)
     grad_normed_one = mat(grad_projected.reshape(row_count, exp_count * 2 * HD), full_qkv)
     scaled_one = grad_normed_one * gain_one
     grad_gain_one = jnp.sum(grad_normed_one * inputs * inv_one, axis=0)
@@ -571,18 +611,43 @@
         - inputs * inv_one**3 * jnp.mean(scaled_one * inputs, axis=-1, keepdims=True)
     )
 
+    small_rows = (per_group * D + 2 * HD) // (2 * HD)
     small = jnp.concatenate(
         [
-            contract_rows(grad_logits, normed_two),
-            grad_gain_one[None],
-            grad_gain_two[None],
-            jnp.zeros((6, D), jnp.float32),
+            contract_rows(grad_logits, normed_two).reshape(exp_count, -1, 2 * HD),
+            jnp.stack([grad_gain_one, grad_gain_two])
+            .reshape(2, exp_count, HD)
+            .transpose(1, 0, 2)
+            .reshape(exp_count, 1, 2 * HD),
+            jnp.zeros((exp_count, 7, 2 * HD), jnp.float32),
         ],
-        axis=0,
-    )
-    small = lax.psum(small, ("exp", "ctx"))
-    sum_router = lax.dynamic_slice(small, (exp_index * per_group, 0), (per_group, D)).T
-    sum_gains = lax.dynamic_slice(small, (EXPERTS, exp_index * HD), (2, HD))
+        axis=1,
+    ).astype(bf16)
+    head_grads = exchange(
+        jnp.concatenate([jnp.transpose(grad_projected, (1, 0, 2)), small], axis=1), "exp"
+    )
+    small = jnp.sum(head_grads[:, row_count : row_count + small_rows].astype(jnp.float32), axis=0)
+    head_grads = head_grads[:, :row_count].reshape(exp_count * row_count, 2 * HD)
+
+    part = jnp.concatenate(
+        [contract_rows(all_normed, head_grads), contract_rows(all_attended, head_mixed)], axis=1
+    )
+    small = jnp.pad(
+        small.reshape(2 * small_rows, HD), ((0, D // ctx_count - 2 * small_rows), (0, 0))
+    )
+    part = jnp.concatenate(
+        [
+            part.astype(bf16).reshape(ctx_count, D // ctx_count, 3 * HD),
+            jnp.broadcast_to(small.astype(bf16)[None], (ctx_count,) + small.shape),
+        ],
+        axis=2,
+    )
+    part = jnp.sum(exchange(part, "ctx").astype(jnp.float32), axis=0)
+    sums = spread(part[:, : 3 * HD].astype(bf16), "ctx", None, ctx_count)
+    sums = sums.reshape(D, 3 * HD).astype(jnp.float32)
+    small = part[: 2 * small_rows, 3 * HD :].reshape(small_rows, 2 * HD)
+    sum_router = small[:-1].reshape(per_group, D).T
+    sum_gains = small[-1].reshape(2, HD)
     router_one, router_two, router_new = adam_update(
         router, router_first, router_second, sum_router, router_rate, decay_rate
     )
@@ -590,19 +655,12 @@
         gains, gains_first, gains_second, sum_gains, gain_rate, 0.0
     )
 
-    part = jnp.concatenate(
-        [contract_rows(all_normed, head_grads), contract_rows(all_attended, head_mixed)], axis=1
-    )
-    part = exchange(part.astype(bf16).reshape(ctx_count, D // ctx_count, 3 * HD), "ctx")
-    part = jnp.sum(part.astype(jnp.float32), axis=0)
-    sums = spread(part, "ctx", None, ctx_count).reshape(D, 3 * HD)
     head_fresh, head_new = head_blocks(
         sums,
         jnp.concatenate([query_momentum, kv_momentum, output_momentum], axis=1),
         jnp.concatenate([query_weight, kv_weight, output_weight], axis=1),
     )
 
-    expert_sums = jnp.sum(expert_sums.astype(jnp.float32), axis=0)
     momenta = jnp.stack([gate_momentum, up_momentum, down_momentum])
     fresh = mom_rate * momenta + expert_sums
     matrix_count = 3 * per_group

time: 785 us -> 575 us (0.73)
  waiting for transfers between devices: 426 us -> 239 us
  blocking collectives: 87.3 us -> 38.2 us
  local copies, waits for them, and re-layouts: 46 us -> 59.4 us
    all_to_all x12 -> x10, waiting for transfers between devices: 334 us -> 87.2 us  [exchange(): lax.all_to_all(blocks, axis, split_axis=0, concat_axis=0, tiled=True, axi...]
    ppermute x0 -> x9, waiting for transfers between devices: none -> 150 us  [ctx_move(): return lax.ppermute(block, 'ctx', pairs)]
    psum x1 -> x0, waiting for transfers between devices: 87.2 us -> none  [body(): small = lax.psum(small, ('exp', 'ctx'))]
    all_to_all x2 -> x1, blocking collectives: 87.3 us -> 38.2 us  [exchange(): lax.all_to_all(blocks, axis, split_axis=0, concat_axis=0, tiled=True, axi...]
    ppermute x0 -> x9, starting transfers between devices: none -> 13.8 us  [ctx_move(): return lax.ppermute(block, 'ctx', pairs)]
    all_to_all x12 -> x10, starting transfers between devices: 58.1 us -> 52.2 us  [exchange(): lax.all_to_all(blocks, axis, split_axis=0, concat_axis=0, tiled=True, axi...]
    dot_general x8 -> x9, matrix products: 15.6 us -> 20.1 us  [mat(): return jnp.dot(left, right, preferred_element_type=jnp.float32)]
    dot_general x6 -> x5, matrix products: 16.6 us -> 12.4 us  [contract_rows(): lax.dot_general(left, right, (((0,), (0,)), ((), ())), preferred_element_...]
  transfers between devices with their start and end apart: 18 -> 24, of which waited for: 11 -> 14; matrix products, arithmetic and copies ran while one was open for 14% -> 21% of each run, Pallas kernels for 5% -> 12%
where the time goes in v2:
time: 575 us; the launch traced here: 567 us
  waiting for transfers between devices  239 us (42%)
  Pallas kernels  66.5 us (12%)
  starting transfers between devices  66.3 us (12%)
  local copies, waits for them, and re-layouts  59.4 us (10%)
  matrix products  43.3 us (8%)
  other arithmetic  39 us (7%)
  blocking collectives  38.2 us (7%)
  between operations  15.4 us (3%)
    ppermute x9, waiting for transfers between devices, ctx_move(): return lax.ppermute(block, 'ctx', pairs)  150 us
    all_to_all x10, waiting for transfers between devices, exchange(): lax.all_to_all(blocks, axis, split_axis=0, concat_axis=0, tiled=True, axi...  87.2 us
    all_to_all x10, starting transfers between devices, exchange(): lax.all_to_all(blocks, axis, split_axis=0, concat_axis=0, tiled=True, axi...  52.2 us
    all_to_all x1, blocking collectives, exchange(): lax.all_to_all(blocks, axis, split_axis=0, concat_axis=0, tiled=True, axi...  38.2 us
    pallas_call x1, Pallas kernels, expert_math(): pl.pallas_call(expert_kernel, grid_spec=pltpu.PrefetchScalarGridSpec(num_...  26.4 us
    pallas_call x1, Pallas kernels, owner_orthogonal(): pl.pallas_call(owner_kernel, out_shape=jax.ShapeDtypeStruct(stacked.shape...  21.7 us
    dot_general x9, matrix products, mat(): return jnp.dot(left, right, preferred_element_type=jnp.float32)  20.1 us
    pallas_call x2, Pallas kernels, attention_call(): pl.pallas_call(kernel, grid_spec=pltpu.PrefetchScalarGridSpec(num_scalar_...  18.4 us
  transfers between devices with their start and end apart: 24, of which 14 were waited for; matrix products, arithmetic and copies ran while one was open for 21% of the time, Pallas kernels for 12%

profile of v2, /device:TPU:0, one launch (start us, length us, event | category | flops | bytes accessed | tf_op | source)
XLA Modules:
  0.0 567.3 jit_solution(15082464511800846521)
XLA Ops:
  10.9 38.2 %all_to_all.55 = bf16[8,136,1024]{2,1,0:T(8,128)(2,1)S(1)} all-to-all(bf16[8,136,1024]{2,1,0:T(8,128)(2,1)S(1)} %broadcast_in_dim.46), channel_id=1, replica_groups={{0,2,4,6,8,10,12,14},{1,3,5,7,9,11,13,15},{16,18,20,22,24,26,28,30},{17..., dimensions={0} | all-to-all | bytes 4456448 | tf_op jit(solution)/shard_map/all_to_all | solution.py:67
  65.0 6.2 %all-to-all-start.1 = ((bf16[8,128,1024]{2,1,0:T(8,128)(2,1)}), bf16[8,128,1024]{2,1,0:T(8,128)(2,1)S(1)}, u32[]{:S(2)}, u32[]{:S(2)}) async-start(bf16[8,128,1024]{2,1,0:T(8,128)(2,1)} %broadcast_in_dim.48), calls=%async_computation.1 | async-start | bytes 4194304 | tf_op jit(solution)/shard_map/all_to_all | solution.py:67
  74.0 27.5 %all-to-all-done.1 = bf16[8,128,1024]{2,1,0:T(8,128)(2,1)S(1)} async-done(((bf16[8,128,1024]{2,1,0:T(8,128)(2,1)}), bf16[8,128,1024]{2,1,0:T(8,128)(2,1)S(1)}, u32[]{:S(2)}, u32[]{:S(2)}) %all-to-all-start.1) | async-done | bytes 2097184 | tf_op jit(solution)/shard_map/all_to_all | solution.py:67
  101.5 7.2 %attend.1 = bf16[128,1024]{1,0:T(8,128)(2,1)S(1)} custom-call(s32[1]{0:T(128)} %bitcast.1.first_ref, bf16[128,1024]{1,0:T(8,128)(2,1)S(1)} %copy.247.query_ref, bf16[1024,1024]{1,0:T(8,128)(2,1)S(1)} %bitcast.230, bf16[1024,1024]{1,0:T(8,128)(2,1)S(1)} %bitcast.231), custom_call_target="tpu_custom_call" | custom-call | flops 536870912 | bytes 4194304 | tf_op jit(solution)/shard_map/attend/pallas_call | solution.py:435
  116.6 4.1 convolution_convert_fusion
  120.7 4.5 all-to-all-start.2
  126.6 55.7 %collective-permute-done.1 = bf16[3,2,128,512]{3,2,1,0:T(8,128)(2,1)S(1)} collective-permute-done((bf16[3,2,128,512]{3,2,1,0:T(8,128)(2,1)S(1)}, bf16[3,2,128,512]{3,2,1,0:T(8,128)(2,1)S(1)}, u32[]{:S(2)}, u32[]{:S(2)}) %collective-permute-start.1) | collective-permute-done | bytes 786464 | tf_op jit(solution)/shard_map/ppermute | solution.py:88
  186.8 34.4 %collective-permute-done.2.below_ref = bf16[2,3,2,128,512]{4,3,2,1,0:T(8,128)(2,1)S(1)} collective-permute-done((bf16[2,3,2,128,512]{4,3,2,1,0:T(8,128)(2,1)}, bf16[2,3,2,128,512]{4,3,2,1,0:T(8,128)(2,1)S(1)}, u32[]{:S(2)}, u32[]{:S(2)}) %collective-permute-start.2) | collective-permute-done | bytes 1572896 | tf_op jit(solution)/shard_map/ppermute | solution.py:88
  230.5 13.0 %collective-permute-done.4.far_ref = bf16[3,2,128,512]{3,2,1,0:T(8,128)(2,1)} collective-permute-done((bf16[3,2,128,512]{3,2,1,0:T(8,128)(2,1)}, bf16[3,2,128,512]{3,2,1,0:T(8,128)(2,1)}, u32[]{:S(2)}, u32[]{:S(2)}) %collective-permute-start.4) | collective-permute-done | bytes 786464 | tf_op jit(solution)/shard_map/ppermute | solution.py:88
  246.0 26.4 %experts.1 = (bf16[16,2,48,1024]{3,2,1,0:T(8,128)(2,1)}, bf16[16,2,48,1152]{3,2,1,0:T(8,128)(2,1)}, bf16[2,3,2,128,512]{4,3,2,1,0:T(8,128)(2,1)}, bf16[2,3,2,128...) custom-call(s32[3]{0:T(128)} %pad_add_fusion.own_ref, ...), custom_call_target="tpu_custom_call" | custom-call | flops 14495514624 | bytes 31457280 | tf_op jit(solution)/shard_map/experts/pallas_call | solution.py:277
  272.3 5.7 %all-to-all-start.4 = ((bf16[16,96,1152]{2,1,0:T(8,128)(2,1)}), bf16[16,96,1152]{2,1,0:T(8,128)(2,1)}, u32[]{:S(2)}, u32[]{:S(2)}) async-start(bf16[16,96,1152]{2,1,0:T(8,128)(2,1)} %bitcast.246), calls=%async_computation.4 | async-start | bytes 7077888 | tf_op jit(solution)/shard_map/all_to_all | solution.py:67
  287.6 4.2 pad_maximum_fusion.1
  291.7 31.2 %all-to-all-done.4 = bf16[16,96,1152]{2,1,0:T(8,128)(2,1)} async-done(((bf16[16,96,1152]{2,1,0:T(8,128)(2,1)}), bf16[16,96,1152]{2,1,0:T(8,128)(2,1)}, u32[]{:S(2)}, u32[]{:S(2)}) %all-to-all-start.4) | async-done | bytes 3538976 | tf_op jit(solution)/shard_map/all_to_all | solution.py:67
  322.9 4.5 all-to-all-start.3
  327.5 22.6 %collective-permute-done.7 = bf16[2,3,2,128,512]{4,3,2,1,0:T(8,128)(2,1)} collective-permute-done((bf16[2,3,2,128,512]{4,3,2,1,0:T(8,128)(2,1)}, bf16[2,3,2,128,512]{4,3,2,1,0:T(8,128)(2,1)}, u32[]{:S(2)}, u32[]{:S(2)}) %collective-permute-start.7) | collective-permute-done | bytes 1572896 | tf_op jit(solution)/shard_map/ppermute | solution.py:88
  351.9 3.8 convert_add_fusion
  368.6 19.6 %collective-permute-done.9 = bf16[3,2,128,512]{3,2,1,0:T(8,128)(2,1)} collective-permute-done((bf16[3,2,128,512]{3,2,1,0:T(8,128)(2,1)}, bf16[3,2,128,512]{3,2,1,0:T(8,128)(2,1)}, u32[]{:S(2)}, u32[]{:S(2)}) %collective-permute-start.9) | collective-permute-done | bytes 786464 | tf_op jit(solution)/shard_map/ppermute | solution.py:88
  393.0 5.3 all-to-all-start.9
  398.3 4.4 slice.231
  417.5 11.2 %attend_back.1 = (f32[128,1024]{1,0:T(8,128)S(1)}, bf16[1024,512]{1,0:T(8,128)(2,1)S(1)}, bf16[1024,512]{1,0:T(8,128)(2,1)S(1)}) custom-call(s32[1]{0:T(128)} %bitcast.1.first_ref, bf16[128,1024]{1,0:T(8,128)(2,1)S(1)} %copy.247.query_ref, bf16[1024,1024]{1,0:T(8,128)(2,1)S(1)} %bitcast.232, bf16[1024,1024]{1,0:T(8,128)(2,1)S(1)} %bitcast.233, ...), custom_call_target="tpu_custom_call" | custom-call | flops 1342177280 | bytes 4194304 | tf_op jit(solution)/shard_map/attend_back/pallas_call | solution.py:435
  430.4 5.9 %all-to-all-start.5 = ((bf16[8,128,1024]{2,1,0:T(8,128)(2,1)}), bf16[8,128,1024]{2,1,0:T(8,128)(2,1)S(1)}, u32[]{:S(2)}, u32[]{:S(2)}) async-start(bf16[8,128,1024]{2,1,0:T(8,128)(2,1)} %bitcast.242), calls=%async_computation.5 | async-start | bytes 4194304 | tf_op jit(solution)/shard_map/all_to_all | solution.py:67
  436.3 21.7 %owner.1 = bf16[1024,512]{1,0:T(8,128)(2,1)} custom-call(bf16[1024,512]{1,0:T(8,128)(2,1)} %bitcast.63.matrix_ref), custom_call_target="tpu_custom_call" | custom-call | flops 20937965568 | bytes 2097152 | tf_op jit(solution)/shard_map/owner/pallas_call | solution.py:345
  462.7 6.1 %all-to-all-start.10 = ((bf16[8,128,512]{2,1,0:T(8,128)(2,1)}), bf16[8,128,512]{2,1,0:T(8,128)(2,1)S(1)}, u32[]{:S(2)}, u32[]{:S(2)}) async-start(bf16[8,128,512]{2,1,0:T(8,128)(2,1)} %bitcast.64), calls=%async_computation.10 | async-start | bytes 2097152 | tf_op jit(solution)/shard_map/all_to_all | solution.py:67
  482.8 6.9 %all-to-all-start.6 = ((bf16[16,152,128]{2,1,0:T(8,128)(2,1)}), bf16[16,152,128]{2,1,0:T(8,128)(2,1)S(1)}, u32[]{:S(2)}, u32[]{:S(2)}) async-start(bf16[16,152,128]{2,1,0:T(8,128)(2,1)} %copy.264), calls=%async_computation.6 | async-start | bytes 1245184 | tf_op jit(solution)/shard_map/all_to_all | solution.py:67
  491.5 11.6 %all-to-all-done.6 = bf16[16,152,128]{2,1,0:T(8,128)(2,1)S(1)} async-done(((bf16[16,152,128]{2,1,0:T(8,128)(2,1)}), bf16[16,152,128]{2,1,0:T(8,128)(2,1)S(1)}, u32[]{:S(2)}, u32[]{:S(2)}) %all-to-all-start.6) | async-done | bytes 622624 | tf_op jit(solution)/shard_map/all_to_all | solution.py:67
  503.5 6.5 %copy.282 = bf16[1024,2048]{1,0:T(8,128)(2,1)} copy(bf16[1024,2048]{0,1:T(8,128)(2,1)} %bitcast.244) | data formatting | bytes 8388608 | tf_op jit(solution)/shard_map/dot_general | solution.py:147
  510.0 3.7 convolution_convert_fusion.2
  513.8 6.6 %copy.284 = bf16[1024,2048]{1,0:T(8,128)(2,1)} copy(bf16[1024,2048]{0,1:T(8,128)(2,1)} %bitcast.245) | data formatting | bytes 8388608 | tf_op jit(solution)/shard_map/dot_general | solution.py:147
  520.3 3.6 convolution_convert_fusion.3
  529.5 8.7 %all-to-all-done.7 = bf16[8,128,256]{1,2,0:T(8,128)(2,1)S(1)} async-done(((bf16[8,128,256]{1,2,0:T(8,128)(2,1)}), bf16[8,128,256]{1,2,0:T(8,128)(2,1)S(1)}, u32[]{:S(2)}, u32[]{:S(2)}) %all-to-all-start.7) | async-done | bytes 524320 | tf_op jit(solution)/shard_map/all_to_all | solution.py:67
  539.1 3.6 all-to-all-start.8
  544.2 6.4 %all-to-all-done.8 = bf16[8,128,192]{1,2,0:T(8,128)(2,1)S(1)} async-done(((bf16[8,128,192]{1,2,0:T(8,128)(2,1)}), bf16[8,128,192]{1,2,0:T(8,128)(2,1)S(1)}, u32[]{:S(2)}, u32[]{:S(2)}) %all-to-all-start.8) | async-done | bytes 393248 | tf_op jit(solution)/shard_map/all_to_all | solution.py:67
  (314 shorter events, 131.0 us)
Async XLA Ops:
  7.2 101.6 %all-gather.6.cloned.1.call-start = ((), (), s32[]{:S(2)}) async-start(), calls=%async_computation.11 | async-start | bytes 2228224 | tf_op jit(solution)/shard_map/all_gather | solution.py:511
  7.9 238.1 %all-gather.12.cloned.1.call-start = ((), (), s32[]{:S(2)}) async-start(), calls=%async_computation.14 | async-start | bytes 5013504 | tf_op jit(solution)/shard_map/all_gather | solution.py:528
  50.3 4.6 collective-permute-start
  65.0 36.6 %all-to-all-start.1 = ((bf16[8,128,1024]{2,1,0:T(8,128)(2,1)}), bf16[8,128,1024]{2,1,0:T(8,128)(2,1)S(1)}, u32[]{:S(2)}, u32[]{:S(2)}) async-start(bf16[8,128,1024]{2,1,0:T(8,128)(2,1)} %broadcast_in_dim.48), calls=%async_computation.1 | async-start | bytes 4194304 | tf_op jit(solution)/shard_map/all_to_all | solution.py:67
  120.7 103.7 %all-to-all-start.2 = ((bf16[16,96,1152]{2,1,0:T(8,128)(2,1)}), bf16[16,96,1152]{2,1,0:T(8,128)(2,1)}, u32[]{:S(2)}, u32[]{:S(2)}) async-start(bf16[16,96,1152]{2,1,0:T(8,128)(2,1)} %bitcast.241), calls=%async_computation.2 | async-start | bytes 7077888 | tf_op jit(solution)/shard_map/all_to_all | solution.py:67
  125.2 378.3 %all-gather.8.cloned.1.call-start = ((), (), s32[]{:S(2)}) async-start(), calls=%async_computation.12 | async-start | bytes 4456448 | tf_op jit(solution)/shard_map/all_gather | solution.py:560
  126.5 55.8 %collective-permute-start.1 = (bf16[3,2,128,512]{3,2,1,0:T(8,128)(2,1)S(1)}, bf16[3,2,128,512]{3,2,1,0:T(8,128)(2,1)S(1)}, u32[]{:S(2)}, u32[]{:S(2)}) collective-permute-start(bf16[3,2,128,512]{3,2,1,0:T(8,128)(2,1)S(1)} %get-tuple-element.143), channel_id=1, source_target_pairs={{0,16},{16,0},{32,48},{48,32},{64,80},{80,64},{96,112},{112,96},{1... | collective-permute-start | bytes 2359304 | tf_op jit(solution)/shard_map/ppermute | solution.py:88
  182.3 41.2 %copy-start.38 = (f32[1024]{0:T(1024)S(1)}, f32[1024]{0:T(1024)}, u32[]{:S(2)}) copy-start(f32[1024]{0:T(1024)} %copy-done.37) | copy-start | bytes 12292
  182.3 41.2 %copy-start.52 = (f32[128]{0:T(128)S(1)}, f32[128]{0:T(128)}, u32[]{:S(2)}) copy-start(f32[128]{0:T(128)} %copy-done.51) | copy-start | bytes 1540
  183.6 37.6 %collective-permute-start.2 = (bf16[2,3,2,128,512]{4,3,2,1,0:T(8,128)(2,1)}, bf16[2,3,2,128,512]{4,3,2,1,0:T(8,128)(2,1)S(1)}, u32[]{:S(2)}, u32[]{:S(2)}) collective-permute-start(bf16[2,3,2,128,512]{4,3,2,1,0:T(8,128)(2,1)} %pad_maximum_fusion.3.same_ref), channel_id=1, source_target_pairs={{0,32},{16,48},{32,64},{48,80},{64,96},{80,112},{96,0},{112,16},{1... | collective-permute-start | bytes 4718600 | tf_op jit(solution)/shard_map/ppermute | solution.py:88
  183.9 40.4 %collective-permute-start.3 = (bf16[2,3,2,128,512]{4,3,2,1,0:T(8,128)(2,1)}, bf16[2,3,2,128,512]{4,3,2,1,0:T(8,128)(2,1)}, u32[]{:S(2)}, u32[]{:S(2)}) collective-permute-start(bf16[2,3,2,128,512]{4,3,2,1,0:T(8,128)(2,1)} %pad_maximum_fusion.3.same_ref), channel_id=1, source_target_pairs={{0,96},{16,112},{32,0},{48,16},{64,32},{80,48},{96,64},{112,80},{1... | collective-permute-start | bytes 4718600 | tf_op jit(solution)/shard_map/ppermute | solution.py:88
  223.5 20.0 %collective-permute-start.4 = (bf16[3,2,128,512]{3,2,1,0:T(8,128)(2,1)}, bf16[3,2,128,512]{3,2,1,0:T(8,128)(2,1)}, u32[]{:S(2)}, u32[]{:S(2)}) collective-permute-start(bf16[3,2,128,512]{3,2,1,0:T(8,128)(2,1)} %slice_bitcast_fusion.2), channel_id=1, source_target_pairs={{0,32},{16,48},{32,64},{48,80},{64,96},{80,112},{96,0},{112,16},{1... | collective-permute-start | bytes 2359304 | tf_op jit(solution)/shard_map/ppermute | solution.py:88
  226.5 19.4 %collective-permute-start.5 = (bf16[3,2,128,512]{3,2,1,0:T(8,128)(2,1)}, bf16[3,2,128,512]{3,2,1,0:T(8,128)(2,1)}, u32[]{:S(2)}, u32[]{:S(2)}) collective-permute-start(bf16[3,2,128,512]{3,2,1,0:T(8,128)(2,1)} %slice_bitcast_fusion.1), channel_id=1, source_target_pairs={{0,96},{16,112},{32,0},{48,16},{64,32},{80,48},{96,64},{112,80},{1... | collective-permute-start | bytes 2359304 | tf_op jit(solution)/shard_map/ppermute | solution.py:88
  272.3 50.6 %all-to-all-start.4 = ((bf16[16,96,1152]{2,1,0:T(8,128)(2,1)}), bf16[16,96,1152]{2,1,0:T(8,128)(2,1)}, u32[]{:S(2)}, u32[]{:S(2)}) async-start(bf16[16,96,1152]{2,1,0:T(8,128)(2,1)} %bitcast.246), calls=%async_computation.4 | async-start | bytes 7077888 | tf_op jit(solution)/shard_map/all_to_all | solution.py:67
  278.1 49.4 %collective-permute-start.6 = (bf16[2,3,2,128,512]{4,3,2,1,0:T(8,128)(2,1)}, bf16[2,3,2,128,512]{4,3,2,1,0:T(8,128)(2,1)}, u32[]{:S(2)}, u32[]{:S(2)}) collective-permute-start(bf16[2,3,2,128,512]{4,3,2,1,0:T(8,128)(2,1)} %get-tuple-element.39), channel_id=1, source_target_pairs={{0,32},{16,48},{32,64},{48,80},{64,96},{80,112},{96,0},{112,16},{1... | collective-permute-start | bytes 4718600 | tf_op jit(solution)/shard_map/ppermute | solution.py:88
  278.7 71.3 %collective-permute-start.7 = (bf16[2,3,2,128,512]{4,3,2,1,0:T(8,128)(2,1)}, bf16[2,3,2,128,512]{4,3,2,1,0:T(8,128)(2,1)}, u32[]{:S(2)}, u32[]{:S(2)}) collective-permute-start(bf16[2,3,2,128,512]{4,3,2,1,0:T(8,128)(2,1)} %get-tuple-element.40), channel_id=1, source_target_pairs={{0,96},{16,112},{32,0},{48,16},{64,32},{80,48},{96,64},{112,80},{1... | collective-permute-start | bytes 4718600 | tf_op jit(solution)/shard_map/ppermute | solution.py:88
  281.9 70.0 %collective-permute-start.8 = (bf16[2,3,2,128,512]{4,3,2,1,0:T(8,128)(2,1)}, bf16[2,3,2,128,512]{4,3,2,1,0:T(8,128)(2,1)}, u32[]{:S(2)}, u32[]{:S(2)}) collective-permute-start(bf16[2,3,2,128,512]{4,3,2,1,0:T(8,128)(2,1)} %get-tuple-element.41), channel_id=1, source_target_pairs={{0,64},{16,80},{32,96},{48,112},{64,0},{80,16},{96,32},{112,48},{1... | collective-permute-start | bytes 4718600 | tf_op jit(solution)/shard_map/ppermute | solution.py:88
  322.9 70.1 %all-to-all-start.3 = ((bf16[16,104,1024]{2,1,0:T(8,128)(2,1)}), bf16[16,104,1024]{2,1,0:T(8,128)(2,1)}, u32[]{:S(2)}, u32[]{:S(2)}) async-start(bf16[16,104,1024]{2,1,0:T(8,128)(2,1)} %pad_maximum_fusion.1), calls=%async_computation.3 | async-start | bytes 6815744 | tf_op jit(solution)/shard_map/all_to_all | solution.py:67
  327.4 186.3 %all-gather.10.cloned.1.call-start = ((), (), s32[]{:S(2)}) async-start(), calls=%async_computation.13 | async-start | bytes 4456448 | tf_op jit(solution)/shard_map/all_gather | solution.py:591
  356.9 31.4 %collective-permute-start.9 = (bf16[3,2,128,512]{3,2,1,0:T(8,128)(2,1)}, bf16[3,2,128,512]{3,2,1,0:T(8,128)(2,1)}, u32[]{:S(2)}, u32[]{:S(2)}) collective-permute-start(bf16[3,2,128,512]{3,2,1,0:T(8,128)(2,1)} %fusion.16), channel_id=1, source_target_pairs={{0,16},{16,0},{32,48},{48,32},{64,80},{80,64},{96,112},{112,96},{1... | collective-permute-start | bytes 2359304 | tf_op jit(solution)/shard_map/ppermute | solution.py:88
  393.0 37.4 %all-to-all-start.9 = ((bf16[8,128,512]{2,1,0:T(8,128)(2,1)}), bf16[8,128,512]{2,1,0:T(8,128)(2,1)}, u32[]{:S(2)}, u32[]{:S(2)}) async-start(bf16[8,128,512]{2,1,0:T(8,128)(2,1)} %pad.15), calls=%async_computation.9 | async-start | bytes 2097152 | tf_op jit(solution)/shard_map/all_to_all | solution.py:67
  430.4 32.3 %all-to-all-start.5 = ((bf16[8,128,1024]{2,1,0:T(8,128)(2,1)}), bf16[8,128,1024]{2,1,0:T(8,128)(2,1)S(1)}, u32[]{:S(2)}, u32[]{:S(2)}) async-start(bf16[8,128,1024]{2,1,0:T(8,128)(2,1)} %bitcast.242), calls=%async_computation.5 | async-start | bytes 4194304 | tf_op jit(solution)/shard_map/all_to_all | solution.py:67
  436.2 22.8 %copy-start.6 = (bf16[128,1024]{1,0:T(8,128)(2,1)S(1)}, bf16[128,1024]{1,0:T(8,128)(2,1)}, u32[]{:S(2)}) copy-start(bf16[128,1024]{1,0:T(8,128)(2,1)} %copy-done.5) | copy-start | bytes 786436
  436.2 22.8 %copy-start.25 = (bf16[128,32]{1,0:T(8,128)(2,1)S(1)}, bf16[128,32]{1,0:T(8,128)(2,1)}, u32[]{:S(2)}) copy-start(bf16[128,32]{1,0:T(8,128)(2,1)} %copy-done.24) | copy-start | bytes 24580
  436.2 24.0 %copy-start.48 = (bf16[1024]{0:T(1024)(128)(2,1)S(1)}, bf16[1024]{0:T(1024)(128)(2,1)}, u32[]{:S(2)}) copy-start(bf16[1024]{0:T(1024)(128)(2,1)} %get-tuple-element.102) | copy-start | bytes 6148
  436.2 24.7 %copy-start.32 = (f32[128,32]{0,1:T(8,128)S(1)}, f32[128,32]{0,1:T(8,128)}, u32[]{:S(2)}) copy-start(f32[128,32]{0,1:T(8,128)} %get-tuple-element.150) | copy-start | bytes 49156
  462.7 20.2 %all-to-all-start.10 = ((bf16[8,128,512]{2,1,0:T(8,128)(2,1)}), bf16[8,128,512]{2,1,0:T(8,128)(2,1)S(1)}, u32[]{:S(2)}, u32[]{:S(2)}) async-start(bf16[8,128,512]{2,1,0:T(8,128)(2,1)} %bitcast.64), calls=%async_computation.10 | async-start | bytes 2097152 | tf_op jit(solution)/shard_map/all_to_all | solution.py:67
  482.8 20.4 %all-to-all-start.6 = ((bf16[16,152,128]{2,1,0:T(8,128)(2,1)}), bf16[16,152,128]{2,1,0:T(8,128)(2,1)S(1)}, u32[]{:S(2)}, u32[]{:S(2)}) async-start(bf16[16,152,128]{2,1,0:T(8,128)(2,1)} %copy.264), calls=%async_computation.6 | async-start | bytes 1245184 | tf_op jit(solution)/shard_map/all_to_all | solution.py:67
  524.8 13.3 %all-to-all-start.7 = ((bf16[8,128,256]{1,2,0:T(8,128)(2,1)}), bf16[8,128,256]{1,2,0:T(8,128)(2,1)S(1)}, u32[]{:S(2)}, u32[]{:S(2)}) async-start(bf16[8,128,256]{1,2,0:T(8,128)(2,1)} %pad_maximum_fusion.5), calls=%async_computation.7 | async-start | bytes 1048576 | tf_op jit(solution)/shard_map/all_to_all | solution.py:67
  528.4 22.3 %copy-start.26 = (f32[8,128,64]{1,2,0:T(8,128)S(1)}, f32[8,128,64]{1,2,0:T(8,128)}, u32[]{:S(2)}) copy-start(f32[8,128,64]{1,2,0:T(8,128)} %copy_bitcast_fusion.2) | copy-start | bytes 786436
  528.4 22.3 %copy-start.27 = (f32[8,128,64]{1,2,0:T(8,128)S(1)}, f32[8,128,64]{1,2,0:T(8,128)}, u32[]{:S(2)}) copy-start(f32[8,128,64]{1,2,0:T(8,128)} %get-tuple-element.167) | copy-start | bytes 786436
  539.1 11.5 %all-to-all-start.8 = ((bf16[8,128,192]{1,2,0:T(8,128)(2,1)}), bf16[8,128,192]{1,2,0:T(8,128)(2,1)S(1)}, u32[]{:S(2)}, u32[]{:S(2)}) async-start(bf16[8,128,192]{1,2,0:T(8,128)(2,1)} %broadcast_in_dim.64), calls=%async_computation.8 | async-start | bytes 786432 | tf_op jit(solution)/shard_map/all_to_all | solution.py:67
  (57 other events, 342.3 us)
Sparse Core Ops, SparseCore 0:
  10.5 55.9 all-gather.5
  69.5 59.3 all-gather.11
  224.5 56.7 all-gather.7
  364.0 68.2 all-gather.9

commit v3 on v2

--- a/solution.py
+++ b/solution.py
@@ -88,18 +88,8 @@
     return lax.ppermute(block, "ctx", pairs)
 
 
-def gather_rows(block):
-    same = jnp.stack([block, ctx_move(block, 0, 1)])
-    below = ctx_move(same, 1, 0)
-    above = ctx_move(same, 3, 0)
-    return same, below, above, ctx_move(below[0], 1, 0), ctx_move(above[1], 3, 0)
-
-
-def reduce_rows(same, up, down, far):
-    total = same.astype(jnp.float32) + ctx_move(up, 1, 0).astype(jnp.float32)
-    total = total + ctx_move(down, 3, 0).astype(jnp.float32)
-    total = total + ctx_move(far, 2, 0).astype(jnp.float32)
-    return total[0] + ctx_move(total[1].astype(jnp.bfloat16), 0, 1).astype(jnp.float32)
+def after(value, *others):
+    return lax.optimization_barrier((value,) + others)[0]
 
 
 def three_parts(value):
@@ -490,7 +480,11 @@
         ],
         axis=0,
     )
+    own_experts = jnp.stack([gate_weight, up_weight, down_weight])
+    same = jnp.stack([own_experts, ctx_move(own_experts, 0, 1)])
     mine = spread(packed, "exp", parity_groups(exp_count), exp_count // 2)
+    mine, same = lax.optimization_barrier((mine, same))
+    below, above = ctx_move(same, 1, 0), ctx_move(same, 3, 0)
     other = core_swap(mine, exp_count)
     even = (exp_index % 2 == 0)
 
@@ -507,7 +501,6 @@
     gain_one = full_gains[0].astype(jnp.float32)
     gain_two = full_gains[1].astype(jnp.float32)
 
-    full_experts = gather_rows(jnp.stack([gate_weight, up_weight, down_weight]))
     full_output = lax.all_gather(output_weight.T, "exp", axis=0, tiled=True)
 
     expert_ids = jnp.arange(EXPERTS, dtype=jnp.int32)
@@ -538,6 +531,8 @@
     keys = rotate(kv_raw[:, :KV], cosine, sine).astype(bf16)
     values = kv_raw[:, KV:].astype(bf16)
     sent_kv = jnp.concatenate([keys, values], axis=1).reshape(row_count, 2 * KV * HD)
+    sent_kv, below, above = lax.optimization_barrier((sent_kv, below, above))
+    full_experts = (same, below, above, ctx_move(below[0], 1, 0), ctx_move(above[1], 3, 0))
     all_kv = spread(sent_kv, "ctx", None, ctx_count).reshape(ctx_count * row_count, 2 * KV * HD)
     flat_queries = queries.reshape(row_count, HEADS * HD)
     mixed_low = attention_call(attend_kernel, (flat_queries, all_kv), None, first_row, "attend")
@@ -563,13 +558,17 @@
     )
     returned = exchange(back.reshape(exp_count, per_group * CAP, D + WIDE), "exp")
     returned = returned.reshape(EXPERTS * CAP, D + WIDE)
+    produced = after(produced, returned)
     route_values = exchange(
         jnp.concatenate([produced.reshape(exp_count, per_group * CAP, D), sent_mixed], axis=1),
         "exp",
     )
-    head_mixed = route_values[:, per_group * CAP :].reshape(exp_count * row_count, HD)
-    route_values = route_values[:, : per_group * CAP].reshape(EXPERTS * CAP, D)
-    expert_sums = reduce_rows(*expert_grads)
+    sum_same, sum_up, sum_down, sum_far = expert_grads
+    sum_up, sum_down, sum_far = (
+        ctx_move(sum_up, 1, 0),
+        ctx_move(sum_down, 3, 0),
+        ctx_move(sum_far, 2, 0),
+    )
 
     summed_back = mat(select, returned)
     tail = summed_back[:, D:]
@@ -588,16 +587,48 @@
         - residual * inv_two**3 * jnp.mean(scaled_two * residual, axis=-1, keepdims=True)
     )
     grad_attended = grad_residual.astype(bf16)
+    grad_attended, sum_up, sum_down, sum_far = lax.optimization_barrier(
+        (grad_attended, sum_up, sum_down, sum_far)
+    )
+    both_sums = (
+        sum_same.astype(jnp.float32)
+        + sum_up.astype(jnp.float32)
+        + sum_down.astype(jnp.float32)
+        + sum_far.astype(jnp.float32)
+    )
+    other_sums = ctx_move(both_sums[1].astype(bf16), 0, 1)
     all_attended = lax.all_gather(grad_attended, "exp", axis=0, tiled=True)
     grad_mixed = contract_cols(grad_attended, full_output).astype(bf16)
     grad_queries, key_terms, value_terms = attention_call(
         attend_back_kernel, (flat_queries, all_kv), grad_mixed, first_row, "attend_back"
     )
     kv_terms = jnp.concatenate([key_terms, value_terms], axis=1)
+    kv_terms, other_sums, route_values = lax.optimization_barrier(
+        (kv_terms, other_sums, route_values)
+    )
     kv_terms = exchange(kv_terms.reshape(ctx_count, row_count, 2 * KV * HD), "ctx")
     grad_query_raw = rotate(
         grad_queries.reshape(row_count, HEADS, HD), cosine, -sine
     ).astype(bf16)
+    expert_sums = both_sums[0] + other_sums.astype(jnp.float32)
+    momenta = jnp.stack([gate_momentum, up_momentum, down_momentum])
+    fresh = mom_rate * momenta + expert_sums
+    matrix_count = 3 * per_group
+    rows_each = fresh.shape[2]
+    sent_fresh = jnp.pad(
+        fresh.astype(bf16).reshape(matrix_count, rows_each, -1),
+        ((0, ctx_count - matrix_count), (0, 0), (0, 0)),
+    )
+    level, side = lax.axis_index("ctx") // 2, lax.axis_index("ctx") % 2
+    moves = [(up, other) for up in range(4) for other in range(2)]
+    owned = []
+    for up, other in moves:
+        owner = 2 * ((level + up) % 4) + (side + other) % 2
+        block = lax.dynamic_index_in_dim(sent_fresh, owner, 0, keepdims=False)
+        owned.append(ctx_move(block, up, other) if up or other else block)
+    ortho = owner_orthogonal(jnp.stack(owned).reshape(ctx_count * rows_each, -1))
+    ortho = ortho.reshape(ctx_count, rows_each, -1)
+    kv_terms, ortho = lax.optimization_barrier((kv_terms, ortho))
     kv_sums = jnp.sum(kv_terms.astype(jnp.float32), axis=0).reshape(row_count, 2 * KV, HD)
     grad_key_raw = rotate(kv_sums[:, :KV], cosine, -sine).astype(bf16)
     grad_kv_raw = jnp.concatenate([grad_key_raw, kv_sums[:, KV:].astype(bf16)], axis=1)
@@ -623,6 +654,8 @@
         ],
         axis=1,
     ).astype(bf16)
+    head_mixed = route_values[:, per_group * CAP :].reshape(exp_count * row_count, HD)
+    route_values = route_values[:, : per_group * CAP].reshape(EXPERTS * CAP, D)
     head_grads = exchange(
         jnp.concatenate([jnp.transpose(grad_projected, (1, 0, 2)), small], axis=1), "exp"
     )
@@ -630,22 +663,22 @@
     head_grads = head_grads[:, :row_count].reshape(exp_count * row_count, 2 * HD)
 
     part = jnp.concatenate(
-        [contract_rows(all_normed, head_grads), contract_rows(all_attended, head_mixed)], axis=1
-    )
-    small = jnp.pad(
-        small.reshape(2 * small_rows, HD), ((0, D // ctx_count - 2 * small_rows), (0, 0))
-    )
+        [contract_rows(head_grads, all_normed), contract_rows(head_mixed, all_attended)], axis=0
+    )
+    width = D // ctx_count
     part = jnp.concatenate(
         [
-            part.astype(bf16).reshape(ctx_count, D // ctx_count, 3 * HD),
-            jnp.broadcast_to(small.astype(bf16)[None], (ctx_count,) + small.shape),
+            jnp.transpose(part.astype(bf16).reshape(3 * HD, ctx_count, width), (1, 0, 2)),
+            jnp.broadcast_to(
+                jnp.pad(small.astype(bf16), ((0, 7), (0, 0)))[None], (ctx_count, 24, width)
+            ),
         ],
-        axis=2,
+        axis=1,
     )
     part = jnp.sum(exchange(part, "ctx").astype(jnp.float32), axis=0)
-    sums = spread(part[:, : 3 * HD].astype(bf16), "ctx", None, ctx_count)
-    sums = sums.reshape(D, 3 * HD).astype(jnp.float32)
-    small = part[: 2 * small_rows, 3 * HD :].reshape(small_rows, 2 * HD)
+    sums = spread(part[: 3 * HD].astype(bf16), "ctx", None, ctx_count)
+    sums = jnp.transpose(sums, (0, 2, 1)).reshape(D, 3 * HD).astype(jnp.float32)
+    small = part[3 * HD : 3 * HD + small_rows]
     sum_router = small[:-1].reshape(per_group, D).T
     sum_gains = small[-1].reshape(2, HD)
     router_one, router_two, router_new = adam_update(
@@ -661,18 +694,23 @@
         jnp.concatenate([query_weight, kv_weight, output_weight], axis=1),
     )
 
-    momenta = jnp.stack([gate_momentum, up_momentum, down_momentum])
-    fresh = mom_rate * momenta + expert_sums
-    matrix_count = 3 * per_group
-    rows_each = fresh.shape[2]
-    sent_fresh = jnp.pad(
-        fresh.astype(bf16).reshape(matrix_count, rows_each, -1),
-        ((0, ctx_count - matrix_count), (0, 0), (0, 0)),
-    )
-    owned = exchange(sent_fresh, "ctx").reshape(ctx_count * rows_each, -1)
-    ortho = owner_orthogonal(owned).astype(bf16)
-    ortho = exchange(ortho.reshape(ctx_count, rows_each, -1), "ctx")
-    ortho = ortho[:matrix_count].reshape(fresh.shape).astype(jnp.float32)
+    returned_rows = [
+        ctx_move(ortho[index], (4 - up) % 4, other) if up or other else ortho[index]
+        for index, (up, other) in enumerate(moves)
+    ]
+    returned_rows = jnp.stack(returned_rows)
+    ortho = jnp.stack(
+        [
+            lax.dynamic_index_in_dim(
+                returned_rows,
+                2 * ((matrix // 2 - level) % 4) + (matrix + side) % 2,
+                0,
+                keepdims=False,
+            )
+            for matrix in range(matrix_count)
+        ]
+    )
+    ortho = ortho.reshape(fresh.shape).astype(jnp.float32)
     new = step_weight(jnp.stack([gate_weight, up_weight, down_weight]), ortho)
 
     gates_wide = [mat(part, widen) for part in gate_parts]

time: 575 us -> 561 us (0.976)
  blocking collectives: 38.2 us -> 0 us
  starting transfers between devices: 66.3 us -> 83.9 us
  local copies, waits for them, and re-layouts: 59.4 us -> 71.2 us
    all_to_all x1 -> x0, blocking collectives: 38.2 us -> none  [exchange(): lax.all_to_all(blocks, axis, split_axis=0, concat_axis=0, tiled=True, axi...]
    ppermute x9 -> x23, waiting for transfers between devices: 150 us -> 115 us  [ctx_move(): return lax.ppermute(block, 'ctx', pairs)]
    all_to_all x10 -> x9, waiting for transfers between devices: 87.2 us -> 121 us  [exchange(): lax.all_to_all(blocks, axis, split_axis=0, concat_axis=0, tiled=True, axi...]
    ppermute x9 -> x23, starting transfers between devices: 13.8 us -> 36.7 us  [ctx_move(): return lax.ppermute(block, 'ctx', pairs)]
    unnamed x132 -> x183, local copies, waits for them, and re-layouts: 3.03 us -> 14.8 us
    all_to_all x10 -> x9, starting transfers between devices: 52.2 us -> 47 us  [exchange(): lax.all_to_all(blocks, axis, split_axis=0, concat_axis=0, tiled=True, axi...]
  transfers between devices with their start and end apart: 24 -> 37, of which waited for: 14 -> 13; matrix products, arithmetic and copies ran while one was open for 21% -> 22% of each run, Pallas kernels for 12% -> 12%
where the time goes in v3:
time: 561 us; the launch traced here: 552 us
  waiting for transfers between devices  237 us (42%)
  starting transfers between devices  83.9 us (15%)
  local copies, waits for them, and re-layouts  71.2 us (13%)
  Pallas kernels  64.3 us (11%)
  matrix products  41 us (7%)
  other arithmetic  38.4 us (7%)
  between operations  16 us (3%)
    all_to_all x9, waiting for transfers between devices, exchange(): lax.all_to_all(blocks, axis, split_axis=0, concat_axis=0, tiled=True, axi...  121 us
    ppermute x23, waiting for transfers between devices, ctx_move(): return lax.ppermute(block, 'ctx', pairs)  115 us
    all_to_all x9, starting transfers between devices, exchange(): lax.all_to_all(blocks, axis, split_axis=0, concat_axis=0, tiled=True, axi...  47 us
    ppermute x23, starting transfers between devices, ctx_move(): return lax.ppermute(block, 'ctx', pairs)  36.7 us
    pallas_call x1, Pallas kernels, expert_math(): pl.pallas_call(expert_kernel, grid_spec=pltpu.PrefetchScalarGridSpec(num_...  26.4 us
    pallas_call x1, Pallas kernels, owner_orthogonal(): pl.pallas_call(owner_kernel, out_shape=jax.ShapeDtypeStruct(stacked.shape...  19.5 us
    dot_general x9, matrix products, mat(): return jnp.dot(left, right, preferred_element_type=jnp.float32)  18.4 us
    pallas_call x2, Pallas kernels, attention_call(): pl.pallas_call(kernel, grid_spec=pltpu.PrefetchScalarGridSpec(num_scalar_...  18.4 us
  transfers between devices with their start and end apart: 37, of which 13 were waited for; matrix products, arithmetic and copies ran while one was open for 22% of the time, Pallas kernels for 12%

profile of v3, /device:TPU:0, one launch (start us, length us, event | category | flops | bytes accessed | tf_op | source)
XLA Modules:
  0.0 552.0 jit_solution(4036255814998503239)
XLA Ops:
  12.2 7.1 %all-to-all-start = ((bf16[8,136,1024]{2,1,0:T(8,128)(2,1)}), bf16[8,136,1024]{2,1,0:T(8,128)(2,1)S(1)}, u32[]{:S(2)}, u32[]{:S(2)}) async-start(bf16[8,136,1024]{2,1,0:T(8,128)(2,1)} %broadcast_in_dim.44), calls=%async_computation | async-start | bytes 4456448 | tf_op jit(solution)/shard_map/all_to_all | solution.py:67
  20.2 47.0 %collective-permute-done = bf16[3,2,128,512]{3,2,1,0:T(8,128)(2,1)S(1)} collective-permute-done((bf16[3,2,128,512]{3,2,1,0:T(8,128)(2,1)S(1)}, bf16[3,2,128,512]{3,2,1,0:T(8,128)(2,1)S(1)}, u32[]{:S(2)}, u32[]{:S(2)}) %collective-permute-start) | collective-permute-done | bytes 786464 | tf_op jit(solution)/shard_map/ppermute | solution.py:88
  87.7 26.6 %collective-permute-done.2.below_ref = bf16[2,3,2,128,512]{4,3,2,1,0:T(8,128)(2,1)} collective-permute-done((bf16[2,3,2,128,512]{4,3,2,1,0:T(8,128)(2,1)}, bf16[2,3,2,128,512]{4,3,2,1,0:T(8,128)(2,1)}, u32[]{:S(2)}, u32[]{:S(2)}) %collective-permute-start.2) | collective-permute-done | bytes 1572896 | tf_op jit(solution)/shard_map/ppermute | solution.py:88
  116.0 6.0 %all-to-all-start.1 = ((bf16[8,128,1024]{2,1,0:T(8,128)(2,1)}), bf16[8,128,1024]{2,1,0:T(8,128)(2,1)S(1)}, u32[]{:S(2)}, u32[]{:S(2)}) async-start(bf16[8,128,1024]{2,1,0:T(8,128)(2,1)} %broadcast_in_dim.45), calls=%async_computation.1 | async-start | bytes 4194304 | tf_op jit(solution)/shard_map/all_to_all | solution.py:67
  125.2 28.9 %all-to-all-done.1 = bf16[8,128,1024]{2,1,0:T(8,128)(2,1)S(1)} async-done(((bf16[8,128,1024]{2,1,0:T(8,128)(2,1)}), bf16[8,128,1024]{2,1,0:T(8,128)(2,1)S(1)}, u32[]{:S(2)}, u32[]{:S(2)}) %all-to-all-start.1) | async-done | bytes 2097184 | tf_op jit(solution)/shard_map/all_to_all | solution.py:67
  154.2 7.2 %attend.1 = bf16[128,1024]{1,0:T(8,128)(2,1)S(1)} custom-call(s32[1]{0:T(128)} %bitcast.1.first_ref, bf16[128,1024]{1,0:T(8,128)(2,1)S(1)} %copy.147.query_ref, bf16[1024,1024]{1,0:T(8,128)(2,1)S(1)} %bitcast.295, bf16[1024,1024]{1,0:T(8,128)(2,1)S(1)} %bitcast.296), custom_call_target="tpu_custom_call" | custom-call | flops 536870912 | bytes 4194304 | tf_op jit(solution)/shard_map/attend/pallas_call | solution.py:425
  169.9 4.1 convolution_convert_fusion
  174.0 6.6 %all-to-all-start.2 = ((bf16[16,96,1152]{2,1,0:T(8,128)(2,1)}), bf16[16,96,1152]{2,1,0:T(8,128)(2,1)}, u32[]{:S(2)}, u32[]{:S(2)}) async-start(bf16[16,96,1152]{2,1,0:T(8,128)(2,1)} %bitcast.308), calls=%async_computation.2 | async-start | bytes 7077888 | tf_op jit(solution)/shard_map/all_to_all | solution.py:67
  189.0 36.5 %all-to-all-done.2 = bf16[16,96,1152]{2,1,0:T(8,128)(2,1)} async-done(((bf16[16,96,1152]{2,1,0:T(8,128)(2,1)}), bf16[16,96,1152]{2,1,0:T(8,128)(2,1)}, u32[]{:S(2)}, u32[]{:S(2)}) %all-to-all-start.2) | async-done | bytes 3538976 | tf_op jit(solution)/shard_map/all_to_all | solution.py:67
  226.1 26.4 %experts.1 = (bf16[16,2,48,1024]{3,2,1,0:T(8,128)(2,1)}, bf16[16,2,48,1152]{3,2,1,0:T(8,128)(2,1)}, bf16[2,3,2,128,512]{4,3,2,1,0:T(8,128)(2,1)}, bf16[2,3,2,128...) custom-call(s32[3]{0:T(128)} %pad_add_fusion.own_ref, ...), custom_call_target="tpu_custom_call" | custom-call | flops 14495514624 | bytes 31457280 | tf_op jit(solution)/shard_map/experts/pallas_call | solution.py:267
  252.5 4.8 all-to-all-start.3
  267.8 40.8 %all-to-all-done.3 = bf16[16,96,1152]{2,1,0:T(8,128)(2,1)} async-done(((bf16[16,96,1152]{2,1,0:T(8,128)(2,1)}), bf16[16,96,1152]{2,1,0:T(8,128)(2,1)}, u32[]{:S(2)}, u32[]{:S(2)}) %all-to-all-start.3) | async-done | bytes 3538976 | tf_op jit(solution)/shard_map/all_to_all | solution.py:67
  308.5 4.2 pad_maximum_fusion.1
  312.7 4.6 all-to-all-start.4
  322.5 13.9 %collective-permute-done.6 = bf16[2,3,2,128,512]{4,3,2,1,0:T(8,128)(2,1)} collective-permute-done((bf16[2,3,2,128,512]{4,3,2,1,0:T(8,128)(2,1)}, bf16[2,3,2,128,512]{4,3,2,1,0:T(8,128)(2,1)}, u32[]{:S(2)}, u32[]{:S(2)}) %collective-permute-start.6) | collective-permute-done | bytes 1572896 | tf_op jit(solution)/shard_map/ppermute | solution.py:88
  336.4 3.9 convert_add_fusion
  343.0 11.2 %attend_back.1 = (f32[128,1024]{1,0:T(8,128)S(1)}, bf16[1024,512]{1,0:T(8,128)(2,1)S(1)}, bf16[1024,512]{1,0:T(8,128)(2,1)S(1)}) custom-call(s32[1]{0:T(128)} %bitcast.1.first_ref, bf16[128,1024]{1,0:T(8,128)(2,1)S(1)} %copy.147.query_ref, bf16[1024,1024]{1,0:T(8,128)(2,1)S(1)} %bitcast.297, bf16[1024,1024]{1,0:T(8,128)(2,1)S(1)} %bitcast.298, ...), custom_call_target="tpu_custom_call" | custom-call | flops 1342177280 | bytes 4194304 | tf_op jit(solution)/shard_map/attend_back/pallas_call | solution.py:425
  362.0 12.1 %collective-permute-done.9 = bf16[3,2,128,512]{3,2,1,0:T(8,128)(2,1)} collective-permute-done((bf16[3,2,128,512]{3,2,1,0:T(8,128)(2,1)}, bf16[3,2,128,512]{3,2,1,0:T(8,128)(2,1)}, u32[]{:S(2)}, u32[]{:S(2)}) %collective-permute-start.9) | collective-permute-done | bytes 786464 | tf_op jit(solution)/shard_map/ppermute | solution.py:88
  374.1 3.7 fusion.107
  388.6 4.6 all-to-all-start.5
  393.2 4.3 slice.208
  419.4 11.6 %collective-permute-done.16 = bf16[128,512]{1,0:T(8,128)(2,1)S(1)} collective-permute-done((bf16[128,512]{1,0:T(8,128)(2,1)S(1)}, bf16[128,512]{1,0:T(8,128)(2,1)S(1)}, u32[]{:S(2)}, u32[]{:S(2)}) %collective-permute-start.16) | collective-permute-done | bytes 131104 | tf_op jit(solution)/shard_map/ppermute | solution.py:88
  431.0 19.5 %owner.1 = bf16[1024,512]{1,0:T(8,128)(2,1)S(1)} custom-call(bf16[1024,512]{1,0:T(8,128)(2,1)S(1)} %bitcast.300), custom_call_target="tpu_custom_call" | custom-call | flops 20937965568 | bytes 2097152 | tf_op jit(solution)/shard_map/owner/pallas_call | solution.py:335
  450.6 6.5 %copy.180 = bf16[1024,2048]{1,0:T(8,128)(2,1)} copy(bf16[1024,2048]{0,1:T(8,128)(2,1)} %bitcast.311) | data formatting | bytes 8388608 | tf_op jit(solution)/shard_map/dot_general | solution.py:137
  475.9 6.2 %all-to-all-start.6 = ((bf16[16,152,128]{2,1,0:T(8,128)(2,1)}), bf16[16,152,128]{2,1,0:T(8,128)(2,1)S(1)}, u32[]{:S(2)}, u32[]{:S(2)}) async-start(bf16[16,152,128]{2,1,0:T(8,128)(2,1)} %copy.164), calls=%async_computation.6 | async-start | bytes 1245184 | tf_op jit(solution)/shard_map/all_to_all | solution.py:67
  496.1 3.7 convolution_convert_fusion.2
  499.9 6.6 %copy.182 = bf16[1024,2048]{1,0:T(8,128)(2,1)} copy(bf16[1024,2048]{0,1:T(8,128)(2,1)} %bitcast.312) | data formatting | bytes 8388608 | tf_op jit(solution)/shard_map/dot_general | solution.py:137
  506.4 3.6 convolution_convert_fusion.3
  510.9 3.5 all-to-all-start.7
  516.0 6.9 %all-to-all-done.7 = bf16[8,216,128]{2,1,0:T(8,128)(2,1)S(1)} async-done(((bf16[8,216,128]{2,1,0:T(8,128)(2,1)}), bf16[8,216,128]{2,1,0:T(8,128)(2,1)S(1)}, u32[]{:S(2)}, u32[]{:S(2)}) %all-to-all-start.7) | async-done | bytes 442400 | tf_op jit(solution)/shard_map/all_to_all | solution.py:67
  523.8 3.6 all-to-all-start.8
  528.8 6.6 %all-to-all-done.8 = bf16[8,192,128]{2,1,0:T(8,128)(2,1)S(1)} async-done(((bf16[8,192,128]{2,1,0:T(8,128)(2,1)}), bf16[8,192,128]{2,1,0:T(8,128)(2,1)S(1)}, u32[]{:S(2)}, u32[]{:S(2)}) %all-to-all-start.8) | async-done | bytes 393248 | tf_op jit(solution)/shard_map/all_to_all | solution.py:67
  (394 shorter events, 153.4 us)
Async XLA Ops:
  7.2 154.2 %all-gather.6.cloned.1.call-start = ((), (), s32[]{:S(2)}) async-start(), calls=%async_computation.9 | async-start | bytes 2228224 | tf_op jit(solution)/shard_map/all_gather | solution.py:504
  12.2 56.4 %all-to-all-start = ((bf16[8,136,1024]{2,1,0:T(8,128)(2,1)}), bf16[8,136,1024]{2,1,0:T(8,128)(2,1)S(1)}, u32[]{:S(2)}, u32[]{:S(2)}) async-start(bf16[8,136,1024]{2,1,0:T(8,128)(2,1)} %broadcast_in_dim.44), calls=%async_computation | async-start | bytes 4456448 | tf_op jit(solution)/shard_map/all_to_all | solution.py:67
  19.4 206.7 %all-gather.12.cloned.1.call-start = ((), (), s32[]{:S(2)}) async-start(), calls=%async_computation.12 | async-start | bytes 5013504 | tf_op jit(solution)/shard_map/all_gather | solution.py:521
  19.6 47.7 %collective-permute-start = (bf16[3,2,128,512]{3,2,1,0:T(8,128)(2,1)S(1)}, bf16[3,2,128,512]{3,2,1,0:T(8,128)(2,1)S(1)}, u32[]{:S(2)}, u32[]{:S(2)}) collective-permute-start(bf16[3,2,128,512]{3,2,1,0:T(8,128)(2,1)S(1)} %get-tuple-element.129), channel_id=1, source_target_pairs={{0,16},{16,0},{32,48},{48,32},{64,80},{80,64},{96,112},{112,96},{1... | collective-permute-start | bytes 2359304 | tf_op jit(solution)/shard_map/ppermute | solution.py:88
  73.8 40.4 %collective-permute-start.2 = (bf16[2,3,2,128,512]{4,3,2,1,0:T(8,128)(2,1)}, bf16[2,3,2,128,512]{4,3,2,1,0:T(8,128)(2,1)}, u32[]{:S(2)}, u32[]{:S(2)}) collective-permute-start(bf16[2,3,2,128,512]{4,3,2,1,0:T(8,128)(2,1)} %pad_maximum_fusion.3.same_ref), channel_id=1, source_target_pairs={{0,32},{16,48},{32,64},{48,80},{64,96},{80,112},{96,0},{112,16},{1... | collective-permute-start | bytes 4718600 | tf_op jit(solution)/shard_map/ppermute | solution.py:88
  76.0 38.2 %collective-permute-start.3 = (bf16[2,3,2,128,512]{4,3,2,1,0:T(8,128)(2,1)}, bf16[2,3,2,128,512]{4,3,2,1,0:T(8,128)(2,1)}, u32[]{:S(2)}, u32[]{:S(2)}) collective-permute-start(bf16[2,3,2,128,512]{4,3,2,1,0:T(8,128)(2,1)} %pad_maximum_fusion.3.same_ref), channel_id=1, source_target_pairs={{0,96},{16,112},{32,0},{48,16},{64,32},{80,48},{96,64},{112,80},{1... | collective-permute-start | bytes 4718600 | tf_op jit(solution)/shard_map/ppermute | solution.py:88
  116.0 38.2 %all-to-all-start.1 = ((bf16[8,128,1024]{2,1,0:T(8,128)(2,1)}), bf16[8,128,1024]{2,1,0:T(8,128)(2,1)S(1)}, u32[]{:S(2)}, u32[]{:S(2)}) async-start(bf16[8,128,1024]{2,1,0:T(8,128)(2,1)} %broadcast_in_dim.45), calls=%async_computation.1 | async-start | bytes 4194304 | tf_op jit(solution)/shard_map/all_to_all | solution.py:67
  174.0 51.5 %all-to-all-start.2 = ((bf16[16,96,1152]{2,1,0:T(8,128)(2,1)}), bf16[16,96,1152]{2,1,0:T(8,128)(2,1)}, u32[]{:S(2)}, u32[]{:S(2)}) async-start(bf16[16,96,1152]{2,1,0:T(8,128)(2,1)} %bitcast.308), calls=%async_computation.2 | async-start | bytes 7077888 | tf_op jit(solution)/shard_map/all_to_all | solution.py:67
  180.6 270.0 %all-gather.8.cloned.1.call-start = ((), (), s32[]{:S(2)}) async-start(), calls=%async_computation.10 | async-start | bytes 4456448 | tf_op jit(solution)/shard_map/all_gather | solution.py:555
  182.8 43.3 %collective-permute-start.4 = (bf16[3,2,128,512]{3,2,1,0:T(8,128)(2,1)}, bf16[3,2,128,512]{3,2,1,0:T(8,128)(2,1)}, u32[]{:S(2)}, u32[]{:S(2)}) collective-permute-start(bf16[3,2,128,512]{3,2,1,0:T(8,128)(2,1)} %slice_bitcast_fusion.2), channel_id=1, source_target_pairs={{0,32},{16,48},{32,64},{48,80},{64,96},{80,112},{96,0},{112,16},{1... | collective-permute-start | bytes 2359304 | tf_op jit(solution)/shard_map/ppermute | solution.py:88
  185.0 41.1 %collective-permute-start.5 = (bf16[3,2,128,512]{3,2,1,0:T(8,128)(2,1)}, bf16[3,2,128,512]{3,2,1,0:T(8,128)(2,1)}, u32[]{:S(2)}, u32[]{:S(2)}) collective-permute-start(bf16[3,2,128,512]{3,2,1,0:T(8,128)(2,1)} %slice_bitcast_fusion.1), channel_id=1, source_target_pairs={{0,96},{16,112},{32,0},{48,16},{64,32},{80,48},{96,64},{112,80},{1... | collective-permute-start | bytes 2359304 | tf_op jit(solution)/shard_map/ppermute | solution.py:88
  252.5 56.0 %all-to-all-start.3 = ((bf16[16,96,1152]{2,1,0:T(8,128)(2,1)}), bf16[16,96,1152]{2,1,0:T(8,128)(2,1)}, u32[]{:S(2)}, u32[]{:S(2)}) async-start(bf16[16,96,1152]{2,1,0:T(8,128)(2,1)} %bitcast.313), calls=%async_computation.3 | async-start | bytes 7077888 | tf_op jit(solution)/shard_map/all_to_all | solution.py:67
  264.5 71.9 %collective-permute-start.6 = (bf16[2,3,2,128,512]{4,3,2,1,0:T(8,128)(2,1)}, bf16[2,3,2,128,512]{4,3,2,1,0:T(8,128)(2,1)}, u32[]{:S(2)}, u32[]{:S(2)}) collective-permute-start(bf16[2,3,2,128,512]{4,3,2,1,0:T(8,128)(2,1)} %get-tuple-element.53), channel_id=1, source_target_pairs={{0,32},{16,48},{32,64},{48,80},{64,96},{80,112},{96,0},{112,16},{1... | collective-permute-start | bytes 4718600 | tf_op jit(solution)/shard_map/ppermute | solution.py:88
  264.7 71.7 %collective-permute-start.7 = (bf16[2,3,2,128,512]{4,3,2,1,0:T(8,128)(2,1)}, bf16[2,3,2,128,512]{4,3,2,1,0:T(8,128)(2,1)}, u32[]{:S(2)}, u32[]{:S(2)}) collective-permute-start(bf16[2,3,2,128,512]{4,3,2,1,0:T(8,128)(2,1)} %get-tuple-element.54), channel_id=1, source_target_pairs={{0,96},{16,112},{32,0},{48,16},{64,32},{80,48},{96,64},{112,80},{1... | collective-permute-start | bytes 4718600 | tf_op jit(solution)/shard_map/ppermute | solution.py:88
  267.8 68.7 %collective-permute-start.8 = (bf16[2,3,2,128,512]{4,3,2,1,0:T(8,128)(2,1)}, bf16[2,3,2,128,512]{4,3,2,1,0:T(8,128)(2,1)}, u32[]{:S(2)}, u32[]{:S(2)}) collective-permute-start(bf16[2,3,2,128,512]{4,3,2,1,0:T(8,128)(2,1)} %get-tuple-element.55), channel_id=1, source_target_pairs={{0,64},{16,80},{32,96},{48,112},{64,0},{80,16},{96,32},{112,48},{1... | collective-permute-start | bytes 4718600 | tf_op jit(solution)/shard_map/ppermute | solution.py:88
  312.7 61.3 %all-to-all-start.4 = ((bf16[16,104,1024]{2,1,0:T(8,128)(2,1)}), bf16[16,104,1024]{2,1,0:T(8,128)(2,1)}, u32[]{:S(2)}, u32[]{:S(2)}) async-start(bf16[16,104,1024]{2,1,0:T(8,128)(2,1)} %pad_maximum_fusion.1), calls=%async_computation.4 | async-start | bytes 6815744 | tf_op jit(solution)/shard_map/all_to_all | solution.py:67
  317.4 182.4 %all-gather.10.cloned.1.call-start = ((), (), s32[]{:S(2)}) async-start(), calls=%async_computation.11 | async-start | bytes 4456448 | tf_op jit(solution)/shard_map/all_gather | solution.py:600
  341.4 32.7 %collective-permute-start.9 = (bf16[3,2,128,512]{3,2,1,0:T(8,128)(2,1)}, bf16[3,2,128,512]{3,2,1,0:T(8,128)(2,1)}, u32[]{:S(2)}, u32[]{:S(2)}) collective-permute-start(bf16[3,2,128,512]{3,2,1,0:T(8,128)(2,1)} %fusion.18), channel_id=1, source_target_pairs={{0,16},{16,0},{32,48},{48,32},{64,80},{80,64},{96,112},{112,96},{1... | collective-permute-start | bytes 2359304 | tf_op jit(solution)/shard_map/ppermute | solution.py:88
  378.8 31.1 %collective-permute-start.10 = (bf16[128,512]{1,0:T(8,128)(2,1)}, bf16[128,512]{1,0:T(8,128)(2,1)}, u32[]{:S(2)}, u32[]{:S(2)}) collective-permute-start(bf16[128,512]{1,0:T(8,128)(2,1)} %get-tuple-element.121), channel_id=1, source_target_pairs={{0,16},{16,0},{32,48},{48,32},{64,80},{80,64},{96,112},{112,96},{1... | collective-permute-start | bytes 393224 | tf_op jit(solution)/shard_map/ppermute | solution.py:88
  381.2 32.8 %collective-permute-start.11 = (bf16[128,512]{1,0:T(8,128)(2,1)}, bf16[128,512]{1,0:T(8,128)(2,1)}, u32[]{:S(2)}, u32[]{:S(2)}) collective-permute-start(bf16[128,512]{1,0:T(8,128)(2,1)} %get-tuple-element.122), channel_id=1, source_target_pairs={{0,32},{16,48},{32,64},{48,80},{64,96},{80,112},{96,0},{112,16},{1... | collective-permute-start | bytes 393224 | tf_op jit(solution)/shard_map/ppermute | solution.py:88
  382.6 34.0 %collective-permute-start.12 = (bf16[128,512]{1,0:T(8,128)(2,1)}, bf16[128,512]{1,0:T(8,128)(2,1)}, u32[]{:S(2)}, u32[]{:S(2)}) collective-permute-start(bf16[128,512]{1,0:T(8,128)(2,1)} %get-tuple-element.123), channel_id=1, source_target_pairs={{0,48},{16,32},{32,80},{48,64},{64,112},{80,96},{96,16},{112,0},{1... | collective-permute-start | bytes 393224 | tf_op jit(solution)/shard_map/ppermute | solution.py:88
  383.6 33.9 %collective-permute-start.13 = (bf16[128,512]{1,0:T(8,128)(2,1)}, bf16[128,512]{1,0:T(8,128)(2,1)}, u32[]{:S(2)}, u32[]{:S(2)}) collective-permute-start(bf16[128,512]{1,0:T(8,128)(2,1)} %get-tuple-element.124), channel_id=1, source_target_pairs={{0,64},{16,80},{32,96},{48,112},{64,0},{80,16},{96,32},{112,48},{1... | collective-permute-start | bytes 393224 | tf_op jit(solution)/shard_map/ppermute | solution.py:88
  385.5 33.0 %collective-permute-start.14 = (bf16[128,512]{1,0:T(8,128)(2,1)}, bf16[128,512]{1,0:T(8,128)(2,1)}, u32[]{:S(2)}, u32[]{:S(2)}) collective-permute-start(bf16[128,512]{1,0:T(8,128)(2,1)} %get-tuple-element.125), channel_id=1, source_target_pairs={{0,80},{16,64},{32,112},{48,96},{64,16},{80,0},{96,48},{112,32},{1... | collective-permute-start | bytes 393224 | tf_op jit(solution)/shard_map/ppermute | solution.py:88
  388.6 68.4 %all-to-all-start.5 = ((bf16[8,128,1024]{2,1,0:T(8,128)(2,1)}), bf16[8,128,1024]{2,1,0:T(8,128)(2,1)}, u32[]{:S(2)}, u32[]{:S(2)}) async-start(bf16[8,128,1024]{2,1,0:T(8,128)(2,1)} %bitcast.309), calls=%async_computation.5 | async-start | bytes 4194304 | tf_op jit(solution)/shard_map/all_to_all | solution.py:67
  414.0 17.0 %collective-permute-start.16 = (bf16[128,512]{1,0:T(8,128)(2,1)S(1)}, bf16[128,512]{1,0:T(8,128)(2,1)S(1)}, u32[]{:S(2)}, u32[]{:S(2)}) collective-permute-start(bf16[128,512]{1,0:T(8,128)(2,1)S(1)} %copy-done.52), channel_id=1, source_target_pairs={{0,112},{16,96},{32,16},{48,0},{64,48},{80,32},{96,80},{112,64},{1... | collective-permute-start | bytes 393224 | tf_op jit(solution)/shard_map/ppermute | solution.py:88
  458.0 26.2 %collective-permute-start.17 = (bf16[128,512]{1,0:T(8,128)(2,1)}, bf16[128,512]{1,0:T(8,128)(2,1)}, u32[]{:S(2)}, u32[]{:S(2)}) collective-permute-start(bf16[128,512]{1,0:T(8,128)(2,1)} %get-tuple-element.112), channel_id=1, source_target_pairs={{0,16},{16,0},{32,48},{48,32},{64,80},{80,64},{96,112},{112,96},{1... | collective-permute-start | bytes 393224 | tf_op jit(solution)/shard_map/ppermute | solution.py:88
  458.6 27.4 %collective-permute-start.18 = (bf16[128,512]{1,0:T(8,128)(2,1)}, bf16[128,512]{1,0:T(8,128)(2,1)}, u32[]{:S(2)}, u32[]{:S(2)}) collective-permute-start(bf16[128,512]{1,0:T(8,128)(2,1)} %get-tuple-element.111), channel_id=1, source_target_pairs={{0,96},{16,112},{32,0},{48,16},{64,32},{80,48},{96,64},{112,80},{1... | collective-permute-start | bytes 393224 | tf_op jit(solution)/shard_map/ppermute | solution.py:88
  460.7 26.4 %collective-permute-start.19 = (bf16[128,512]{1,0:T(8,128)(2,1)}, bf16[128,512]{1,0:T(8,128)(2,1)}, u32[]{:S(2)}, u32[]{:S(2)}) collective-permute-start(bf16[128,512]{1,0:T(8,128)(2,1)} %get-tuple-element.110), channel_id=1, source_target_pairs={{0,112},{16,96},{32,16},{48,0},{64,48},{80,32},{96,80},{112,64},{1... | collective-permute-start | bytes 393224 | tf_op jit(solution)/shard_map/ppermute | solution.py:88
  462.7 25.4 %collective-permute-start.20 = (bf16[128,512]{1,0:T(8,128)(2,1)}, bf16[128,512]{1,0:T(8,128)(2,1)}, u32[]{:S(2)}, u32[]{:S(2)}) collective-permute-start(bf16[128,512]{1,0:T(8,128)(2,1)} %get-tuple-element.109), channel_id=1, source_target_pairs={{0,64},{16,80},{32,96},{48,112},{64,0},{80,16},{96,32},{112,48},{1... | collective-permute-start | bytes 393224 | tf_op jit(solution)/shard_map/ppermute | solution.py:88
  463.6 25.5 %collective-permute-start.21 = (bf16[128,512]{1,0:T(8,128)(2,1)}, bf16[128,512]{1,0:T(8,128)(2,1)}, u32[]{:S(2)}, u32[]{:S(2)}) collective-permute-start(bf16[128,512]{1,0:T(8,128)(2,1)} %get-tuple-element.108), channel_id=1, source_target_pairs={{0,80},{16,64},{32,112},{48,96},{64,16},{80,0},{96,48},{112,32},{1... | collective-permute-start | bytes 393224 | tf_op jit(solution)/shard_map/ppermute | solution.py:88
  475.9 20.1 %all-to-all-start.6 = ((bf16[16,152,128]{2,1,0:T(8,128)(2,1)}), bf16[16,152,128]{2,1,0:T(8,128)(2,1)S(1)}, u32[]{:S(2)}, u32[]{:S(2)}) async-start(bf16[16,152,128]{2,1,0:T(8,128)(2,1)} %copy.164), calls=%async_computation.6 | async-start | bytes 1245184 | tf_op jit(solution)/shard_map/all_to_all | solution.py:67
  510.9 11.9 %all-to-all-start.7 = ((bf16[8,216,128]{2,1,0:T(8,128)(2,1)}), bf16[8,216,128]{2,1,0:T(8,128)(2,1)S(1)}, u32[]{:S(2)}, u32[]{:S(2)}) async-start(bf16[8,216,128]{2,1,0:T(8,128)(2,1)} %pad_maximum_fusion.5), calls=%async_computation.7 | async-start | bytes 884736 | tf_op jit(solution)/shard_map/all_to_all | solution.py:67
  (88 other events, 956.3 us)
Sparse Core Ops, SparseCore 0:
  10.5 68.0 all-gather.5
  81.7 62.8 all-gather.11
  225.6 72.3 all-gather.7
  360.3 67.9 all-gather.9

commit v4 on v3

--- a/solution.py
+++ b/solution.py
@@ -88,6 +88,21 @@
     return lax.ppermute(block, "ctx", pairs)
 
 
+def exp_move(block, up, far, core):
+    pairs = [
+        (4 * y + 2 * h + c, 4 * ((y + up) % 4) + 2 * (h ^ far) + (c ^ core))
+        for y in range(4)
+        for h in range(2)
+        for c in range(2)
+    ]
+    return lax.ppermute(block, "exp", pairs)
+
+
+def ring_order(blocks, shift, axis):
+    double = jnp.concatenate([blocks, blocks], axis=axis)
+    return lax.dynamic_slice_in_dim(double, (4 - shift) % 4, 4, axis)
+
+
 def after(value, *others):
     return lax.optimization_barrier((value,) + others)[0]
 
@@ -167,7 +182,12 @@
     return fresh, step_weight(weights, ortho)
 
 
-def expert_kernel(own_ref, arrived_ref, grads_ref, same_ref, below_ref, above_ref, far_ref, far_two_ref,
+def expert_kernel(own_ref, arrived_ref, grads_ref, *refs_in_order):
+    blocks, refs = refs_in_order[:8], refs_in_order[8:]
+    expert_steps(own_ref, arrived_ref, grads_ref, blocks, *refs)
+
+
+def expert_steps(own_ref, arrived_ref, grads_ref, blocks,
                   made_ref, back_ref, sums_ref, sums_up_ref, sums_down_ref, sums_far_ref,
                   weight_ref, rows_ref, hidden_ref, dgate_ref, dup_ref, dy_ref):
     expert = own_ref[0] + pl.program_id(0)
@@ -178,13 +198,10 @@
         index = 2 * lax.rem(level + up, 4) + (1 - side if other else side)
         return pl.ds(pl.multiple_of(index * width, width), width)
 
-    for up, ref in ((0, same_ref), (3, below_ref), (1, above_ref)):
+    for index, up in enumerate((0, 3, 1, 2)):
         for other in range(2):
             for kind in range(3):
-                weight_ref[kind, part(up, other)] = ref[other, kind, 0]
-    for kind in range(3):
-        weight_ref[kind, part(2, 0)] = far_ref[kind, 0]
-        weight_ref[kind, part(2, 1)] = far_two_ref[kind, 0]
+                weight_ref[kind, part(up, other)] = blocks[2 * index + other][kind, 0]
     full_gate, full_up, full_down = weight_ref[0], weight_ref[1], weight_ref[2]
     chunk = ROWS // CHUNKS
     seqs = chunk // CAP
@@ -269,7 +286,7 @@
         grid_spec=pltpu.PrefetchScalarGridSpec(
             num_scalar_prefetch=1,
             grid=(per_group,),
-            in_specs=[rows_spec(D + WIDE), whole, two, two, two, one, one],
+            in_specs=[rows_spec(D + WIDE), whole] + [one] * 8,
             out_specs=[rows_spec(D), rows_spec(D + WIDE), two, two, two, two],
             scratch_shapes=[
                 pltpu.VMEM((3, D, FF), jnp.bfloat16),
@@ -481,22 +498,40 @@
         axis=0,
     )
     own_experts = jnp.stack([gate_weight, up_weight, down_weight])
-    same = jnp.stack([own_experts, ctx_move(own_experts, 0, 1)])
-    mine = spread(packed, "exp", parity_groups(exp_count), exp_count // 2)
-    mine, same = lax.optimization_barrier((mine, same))
-    below, above = ctx_move(same, 1, 0), ctx_move(same, 3, 0)
-    other = core_swap(mine, exp_count)
-    even = (exp_index % 2 == 0)
-
-    def ordered(first, last):
-        left, right = mine[:, first:last], other[:, first:last]
-        return jnp.stack(
-            [jnp.where(even, left, right), jnp.where(even, right, left)], axis=1
-        ).reshape((exp_count, last - first, D))
-
-    full_qkv = ordered(0, 2 * HD).reshape(exp_count * 2 * HD, D)
-    full_router = ordered(2 * HD, 2 * HD + per_group).reshape(EXPERTS, D)
-    full_gains = ordered(2 * HD + per_group, 2 * HD + per_group + 1)[:, 0, : 2 * HD]
+    row_y, far_x, core = exp_index // 4, (exp_index // 2) % 2, exp_index % 2
+    packed_far = exp_move(packed, 0, 1, 0)
+    other_experts = ctx_move(own_experts, 0, 1)
+    below, above = ctx_move(own_experts, 1, 0), ctx_move(own_experts, 3, 0)
+    pair = jnp.stack(
+        [
+            jnp.where(far_x == 0, packed, packed_far),
+            jnp.where(far_x == 0, packed_far, packed),
+        ]
+    )
+    from_below, from_above = exp_move(pair, 1, 0, 0), exp_move(pair, 3, 0, 0)
+    from_below, from_above, other_experts, below, above = lax.optimization_barrier(
+        (from_below, from_above, other_experts, below, above)
+    )
+    below_other, above_other = ctx_move(other_experts, 1, 0), ctx_move(other_experts, 3, 0)
+    far = ctx_move(below, 1, 0)
+    from_two = jnp.stack([exp_move(from_below[0], 1, 0, 0), exp_move(from_above[1], 3, 0, 0)])
+    mine = jnp.stack([pair, from_above, from_two, from_below])
+    other = exp_move(mine, 0, 0, 1)
+
+    def ordered(left, right, axis):
+        both = jnp.stack(
+            [jnp.where(core == 0, left, right), jnp.where(core == 0, right, left)], axis=axis + 2
+        )
+        return ring_order(both, row_y, axis)
+
+    packed_rows = packed.shape[0]
+    mine_flat = mine.reshape(8 * packed_rows, D)
+    other_flat = other.reshape(8 * packed_rows, D)
+    full_router = ordered(
+        mine[:, :, 2 * HD : 2 * HD + per_group], other[:, :, 2 * HD : 2 * HD + per_group], 0
+    ).reshape(EXPERTS, D)
+    gains_row = 2 * HD + per_group
+    full_gains = ordered(mine[:, :, gains_row, : 2 * HD], other[:, :, gains_row, : 2 * HD], 0)
     full_gains = full_gains.reshape(exp_count, 2, HD).transpose(1, 0, 2).reshape(2, D)
     gain_one = full_gains[0].astype(jnp.float32)
     gain_two = full_gains[1].astype(jnp.float32)
@@ -522,7 +557,11 @@
 
     inv_one = lax.rsqrt(jnp.mean(inputs * inputs, axis=-1, keepdims=True) + eps_norm)
     normed_one = (inputs * inv_one * gain_one).astype(bf16)
-    projected = contract_cols(normed_one, full_qkv).reshape(row_count, exp_count, 2 * HD)
+    halves = [
+        contract_cols(normed_one, flat).reshape(row_count, 4, 2, packed_rows)[..., : 2 * HD]
+        for flat in (mine_flat, other_flat)
+    ]
+    projected = ordered(*halves, 1).reshape(row_count, exp_count, 2 * HD)
     query_raw = projected[:, :, :HD]
     kv_raw = projected[:, :, HD:]
     first_row = lax.axis_index("ctx") * row_count
@@ -531,8 +570,13 @@
     keys = rotate(kv_raw[:, :KV], cosine, sine).astype(bf16)
     values = kv_raw[:, KV:].astype(bf16)
     sent_kv = jnp.concatenate([keys, values], axis=1).reshape(row_count, 2 * KV * HD)
-    sent_kv, below, above = lax.optimization_barrier((sent_kv, below, above))
-    full_experts = (same, below, above, ctx_move(below[0], 1, 0), ctx_move(above[1], 3, 0))
+    sent_kv, below_other, above_other, far = lax.optimization_barrier(
+        (sent_kv, below_other, above_other, far)
+    )
+    far_other = ctx_move(above_other, 3, 0)
+    full_experts = (
+        own_experts, other_experts, below, below_other, above, above_other, far, far_other
+    )
     all_kv = spread(sent_kv, "ctx", None, ctx_count).reshape(ctx_count * row_count, 2 * KV * HD)
     flat_queries = queries.reshape(row_count, HEADS * HD)
     mixed_low = attention_call(attend_kernel, (flat_queries, all_kv), None, first_row, "attend")
@@ -558,18 +602,18 @@
     )
     returned = exchange(back.reshape(exp_count, per_group * CAP, D + WIDE), "exp")
     returned = returned.reshape(EXPERTS * CAP, D + WIDE)
-    produced = after(produced, returned)
-    route_values = exchange(
-        jnp.concatenate([produced.reshape(exp_count, per_group * CAP, D), sent_mixed], axis=1),
-        "exp",
-    )
     sum_same, sum_up, sum_down, sum_far = expert_grads
     sum_up, sum_down, sum_far = (
         ctx_move(sum_up, 1, 0),
         ctx_move(sum_down, 3, 0),
         ctx_move(sum_far, 2, 0),
     )
-
+    returned, sum_up, sum_down = lax.optimization_barrier((returned, sum_up, sum_down))
+    produced = after(produced, returned)
+    route_values = exchange(
+        jnp.concatenate([produced.reshape(exp_count, per_group * CAP, D), sent_mixed], axis=1),
+        "exp",
+    )
     summed_back = mat(select, returned)
     tail = summed_back[:, D:]
     grad_gates = (
@@ -587,8 +631,14 @@
         - residual * inv_two**3 * jnp.mean(scaled_two * residual, axis=-1, keepdims=True)
     )
     grad_attended = grad_residual.astype(bf16)
-    grad_attended, sum_up, sum_down, sum_far = lax.optimization_barrier(
-        (grad_attended, sum_up, sum_down, sum_far)
+    all_attended = lax.all_gather(grad_attended, "exp", axis=0, tiled=True)
+    grad_mixed = contract_cols(grad_attended, full_output).astype(bf16)
+    grad_queries, key_terms, value_terms = attention_call(
+        attend_back_kernel, (flat_queries, all_kv), grad_mixed, first_row, "attend_back"
+    )
+    kv_terms = jnp.concatenate([key_terms, value_terms], axis=1)
+    kv_terms, route_values, sum_far = lax.optimization_barrier(
+        (kv_terms, route_values, sum_far)
     )
     both_sums = (
         sum_same.astype(jnp.float32)
@@ -597,15 +647,6 @@
         + sum_far.astype(jnp.float32)
     )
     other_sums = ctx_move(both_sums[1].astype(bf16), 0, 1)
-    all_attended = lax.all_gather(grad_attended, "exp", axis=0, tiled=True)
-    grad_mixed = contract_cols(grad_attended, full_output).astype(bf16)
-    grad_queries, key_terms, value_terms = attention_call(
-        attend_back_kernel, (flat_queries, all_kv), grad_mixed, first_row, "attend_back"
-    )
-    kv_terms = jnp.concatenate([key_terms, value_terms], axis=1)
-    kv_terms, other_sums, route_values = lax.optimization_barrier(
-        (kv_terms, other_sums, route_values)
-    )
     kv_terms = exchange(kv_terms.reshape(ctx_count, row_count, 2 * KV * HD), "ctx")
     grad_query_raw = rotate(
         grad_queries.reshape(row_count, HEADS, HD), cosine, -sine
@@ -626,14 +667,16 @@
         owner = 2 * ((level + up) % 4) + (side + other) % 2
         block = lax.dynamic_index_in_dim(sent_fresh, owner, 0, keepdims=False)
         owned.append(ctx_move(block, up, other) if up or other else block)
-    ortho = owner_orthogonal(jnp.stack(owned).reshape(ctx_count * rows_each, -1))
-    ortho = ortho.reshape(ctx_count, rows_each, -1)
-    kv_terms, ortho = lax.optimization_barrier((kv_terms, ortho))
     kv_sums = jnp.sum(kv_terms.astype(jnp.float32), axis=0).reshape(row_count, 2 * KV, HD)
     grad_key_raw = rotate(kv_sums[:, :KV], cosine, -sine).astype(bf16)
     grad_kv_raw = jnp.concatenate([grad_key_raw, kv_sums[:, KV:].astype(bf16)], axis=1)
     grad_projected = jnp.concatenate([grad_query_raw, grad_kv_raw], axis=2)
-    grad_normed_one = mat(grad_projected.reshape(row_count, exp_count * 2 * HD), full_qkv)
+    by_core = ring_order(grad_projected.reshape(row_count, 4, 2, 2, 2 * HD), -row_y, 1)
+    by_core = jnp.pad(by_core, ((0, 0),) * 4 + ((0, packed_rows - 2 * HD),))
+    first_core, second_core = by_core[:, :, :, 0], by_core[:, :, :, 1]
+    grad_normed_one = mat(
+        jnp.where(core == 0, first_core, second_core).reshape(row_count, -1), mine_flat
+    ) + mat(jnp.where(core == 0, second_core, first_core).reshape(row_count, -1), other_flat)
     scaled_one = grad_normed_one * gain_one
     grad_gain_one = jnp.sum(grad_normed_one * inputs * inv_one, axis=0)
     input_grad = (
@@ -656,14 +699,25 @@
     ).astype(bf16)
     head_mixed = route_values[:, per_group * CAP :].reshape(exp_count * row_count, HD)
     route_values = route_values[:, : per_group * CAP].reshape(EXPERTS * CAP, D)
-    head_grads = exchange(
-        jnp.concatenate([jnp.transpose(grad_projected, (1, 0, 2)), small], axis=1), "exp"
-    )
+    head_send = jnp.concatenate([jnp.transpose(grad_projected, (1, 0, 2)), small], axis=1)
+    head_send, owned = lax.optimization_barrier((head_send, owned))
+    head_grads = exchange(head_send, "exp")
+    ortho = owner_orthogonal(jnp.stack(owned).reshape(ctx_count * rows_each, -1))
+    head_grads, ortho = lax.optimization_barrier((head_grads, ortho))
+    ortho = ortho.reshape(ctx_count, rows_each, -1)
+    returned_rows = [
+        ctx_move(ortho[index], (4 - up) % 4, other) if up or other else ortho[index]
+        for index, (up, other) in enumerate(moves)
+    ]
     small = jnp.sum(head_grads[:, row_count : row_count + small_rows].astype(jnp.float32), axis=0)
     head_grads = head_grads[:, :row_count].reshape(exp_count * row_count, 2 * HD)
 
     part = jnp.concatenate(
-        [contract_rows(head_grads, all_normed), contract_rows(head_mixed, all_attended)], axis=0
+        [
+            mat(lax.optimization_barrier(head_grads.T), all_normed),
+            mat(lax.optimization_barrier(head_mixed.T), all_attended),
+        ],
+        axis=0,
     )
     width = D // ctx_count
     part = jnp.concatenate(
@@ -675,7 +729,8 @@
         ],
         axis=1,
     )
-    part = jnp.sum(exchange(part, "ctx").astype(jnp.float32), axis=0)
+    part, *returned_rows = lax.optimization_barrier((exchange(part, "ctx"), *returned_rows))
+    part = jnp.sum(part.astype(jnp.float32), axis=0)
     sums = spread(part[: 3 * HD].astype(bf16), "ctx", None, ctx_count)
     sums = jnp.transpose(sums, (0, 2, 1)).reshape(D, 3 * HD).astype(jnp.float32)
     small = part[3 * HD : 3 * HD + small_rows]
@@ -694,10 +749,6 @@
         jnp.concatenate([query_weight, kv_weight, output_weight], axis=1),
     )
 
-    returned_rows = [
-        ctx_move(ortho[index], (4 - up) % 4, other) if up or other else ortho[index]
-        for index, (up, other) in enumerate(moves)
-    ]
     returned_rows = jnp.stack(returned_rows)
     ortho = jnp.stack(
         [

time: 561 us -> 542 us (0.966)
  local copies, waits for them, and re-layouts: 71.2 us -> 55.7 us
  waiting for transfers between devices: 237 us -> 225 us
  starting transfers between devices: 83.9 us -> 92.1 us
    all_to_all x9 -> x8, waiting for transfers between devices: 121 us -> 84.7 us  [exchange(): lax.all_to_all(blocks, axis, split_axis=0, concat_axis=0, tiled=True, axi...]
    ppermute x23 -> x25, waiting for transfers between devices: 115 us -> 130 us  [ctx_move(): return lax.ppermute(block, 'ctx', pairs)]
    dot_general x2 -> x0, local copies, waits for them, and re-layouts: 13.1 us -> none  [contract_rows(): lax.dot_general(left, right, (((0,), (0,)), ((), ())), preferred_element_...]
    ppermute x1 -> x6, starting transfers between devices: 0.01 us -> 9.95 us  [exp_move(): return lax.ppermute(block, 'exp', pairs)]
    ppermute x1 -> x6, waiting for transfers between devices: 0.01 us -> 9.04 us  [exp_move(): return lax.ppermute(block, 'exp', pairs)]
    all_to_all x9 -> x8, starting transfers between devices: 47 us -> 38.5 us  [exchange(): lax.all_to_all(blocks, axis, split_axis=0, concat_axis=0, tiled=True, axi...]
    squeeze x4 -> x2, local copies, waits for them, and re-layouts: 7.77 us -> 0.04 us  [the longest x1 0.02 us: body(): from_below[0]]
    dot_general x5 -> x3, matrix products: 13.4 us -> 6.51 us  [contract_rows(): lax.dot_general(left, right, (((0,), (0,)), ((), ())), preferred_element_...]
  transfers between devices with their start and end apart: 37 -> 43, of which waited for: 13 -> 19; matrix products, arithmetic and copies ran while one was open for 22% -> 22% of each run, Pallas kernels for 12% -> 12%
where the time goes in v4:
time: 542 us; the launch traced here: 534 us
  waiting for transfers between devices  225 us (42%)
  starting transfers between devices  92.1 us (17%)
  Pallas kernels  64.2 us (12%)
  local copies, waits for them, and re-layouts  55.7 us (10%)
  matrix products  43.3 us (8%)
  other arithmetic  37.9 us (7%)
  between operations  15.9 us (3%)
    ppermute x25, waiting for transfers between devices, ctx_move(): return lax.ppermute(block, 'ctx', pairs)  130 us
    all_to_all x8, waiting for transfers between devices, exchange(): lax.all_to_all(blocks, axis, split_axis=0, concat_axis=0, tiled=True, axi...  84.7 us
    ppermute x25, starting transfers between devices, ctx_move(): return lax.ppermute(block, 'ctx', pairs)  43.5 us
    all_to_all x8, starting transfers between devices, exchange(): lax.all_to_all(blocks, axis, split_axis=0, concat_axis=0, tiled=True, axi...  38.5 us
    pallas_call x1, Pallas kernels, expert_math(): pl.pallas_call(expert_kernel, grid_spec=pltpu.PrefetchScalarGridSpec(num_...  26.3 us
    dot_general x12, matrix products, mat(): return jnp.dot(left, right, preferred_element_type=jnp.float32)  24.1 us
    pallas_call x1, Pallas kernels, owner_orthogonal(): pl.pallas_call(owner_kernel, out_shape=jax.ShapeDtypeStruct(stacked.shape...  19.5 us
    pallas_call x2, Pallas kernels, attention_call(): pl.pallas_call(kernel, grid_spec=pltpu.PrefetchScalarGridSpec(num_scalar_...  18.4 us
  transfers between devices with their start and end apart: 43, of which 19 were waited for; matrix products, arithmetic and copies ran while one was open for 22% of the time, Pallas kernels for 12%

profile of v4, /device:TPU:0, one launch (start us, length us, event | category | flops | bytes accessed | tf_op | source)
XLA Modules:
  0.0 533.6 jit_solution(3741788619243558645)
XLA Ops:
  25.4 13.8 %collective-permute-done.3.refs_in_order_1_ = bf16[3,2,128,512]{3,2,1,0:T(8,128)(2,1)} collective-permute-done((bf16[3,2,128,512]{3,2,1,0:T(8,128)(2,1)S(1)}, bf16[3,2,128,512]{3,2,1,0:T(8,128)(2,1)}, u32[]{:S(2)}, u32[]{:S(2)}) %collective-permute-start.3) | collective-permute-done | bytes 786464 | tf_op jit(solution)/shard_map/ppermute | solution.py:88
  42.6 5.5 %collective-permute-done.6 = bf16[136,1024]{1,0:T(8,128)(2,1)S(1)} collective-permute-done((bf16[136,1024]{1,0:T(8,128)(2,1)S(1)}, bf16[136,1024]{1,0:T(8,128)(2,1)S(1)}, u32[]{:S(2)}, u32[]{:S(2)}) %collective-permute-start.6) | collective-permute-done | bytes 278560 | tf_op jit(solution)/shard_map/ppermute | solution.py:98
  53.0 4.2 collective-permute-start.10
  63.5 11.2 %collective-permute-done.10.refs_in_order_5_ = bf16[3,2,128,512]{3,2,1,0:T(8,128)(2,1)} collective-permute-done((bf16[3,2,128,512]{3,2,1,0:T(8,128)(2,1)}, bf16[3,2,128,512]{3,2,1,0:T(8,128)(2,1)}, u32[]{:S(2)}, u32[]{:S(2)}) %collective-permute-start.10) | collective-permute-done | bytes 786464 | tf_op jit(solution)/shard_map/ppermute | solution.py:88
  74.7 20.3 %collective-permute-done.11.refs_in_order_6_ = bf16[3,2,128,512]{3,2,1,0:T(8,128)(2,1)} collective-permute-done((bf16[3,2,128,512]{3,2,1,0:T(8,128)(2,1)}, bf16[3,2,128,512]{3,2,1,0:T(8,128)(2,1)}, u32[]{:S(2)}, u32[]{:S(2)}) %collective-permute-start.11) | collective-permute-done | bytes 786464 | tf_op jit(solution)/shard_map/ppermute | solution.py:88
  96.8 3.8 all-to-all-start
  109.5 26.4 %all-to-all-done = bf16[8,128,1024]{2,1,0:T(8,128)(2,1)S(1)} async-done(((bf16[8,128,1024]{2,1,0:T(8,128)(2,1)}), bf16[8,128,1024]{2,1,0:T(8,128)(2,1)S(1)}, u32[]{:S(2)}, u32[]{:S(2)}) %all-to-all-start) | async-done | bytes 2097184 | tf_op jit(solution)/shard_map/all_to_all | solution.py:67
  135.9 7.2 %attend.1 = bf16[128,1024]{1,0:T(8,128)(2,1)S(1)} custom-call(s32[1]{0:T(128)} %bitcast.1.first_ref, bf16[128,1024]{1,0:T(8,128)(2,1)S(1)} %copy.229.query_ref, bf16[1024,1024]{1,0:T(8,128)(2,1)S(1)} %bitcast.316, bf16[1024,1024]{1,0:T(8,128)(2,1)S(1)} %bitcast.317), custom_call_target="tpu_custom_call" | custom-call | flops 536870912 | bytes 4194304 | tf_op jit(solution)/shard_map/attend/pallas_call | solution.py:442
  151.0 4.0 convolution_convert_fusion
  155.0 6.6 %all-to-all-start.1 = ((bf16[16,96,1152]{2,1,0:T(8,128)(2,1)}), bf16[16,96,1152]{2,1,0:T(8,128)(2,1)}, u32[]{:S(2)}, u32[]{:S(2)}) async-start(bf16[16,96,1152]{2,1,0:T(8,128)(2,1)} %bitcast.327), calls=%async_computation.1 | async-start | bytes 7077888 | tf_op jit(solution)/shard_map/all_to_all | solution.py:67
  164.6 41.8 %all-to-all-done.1 = bf16[16,96,1152]{2,1,0:T(8,128)(2,1)} async-done(((bf16[16,96,1152]{2,1,0:T(8,128)(2,1)}), bf16[16,96,1152]{2,1,0:T(8,128)(2,1)}, u32[]{:S(2)}, u32[]{:S(2)}) %all-to-all-start.1) | async-done | bytes 3538976 | tf_op jit(solution)/shard_map/all_to_all | solution.py:67
  207.1 26.3 %experts.1 = (bf16[16,2,48,1024]{3,2,1,0:T(8,128)(2,1)}, bf16[16,2,48,1152]{3,2,1,0:T(8,128)(2,1)}, bf16[2,3,2,128,512]{4,3,2,1,0:T(8,128)(2,1)}, bf16[2,3,2,128...) custom-call(s32[3]{0:T(128)} %pad_add_fusion.own_ref, ...), custom_call_target="tpu_custom_call" | custom-call | flops 14495514624 | bytes 31457280 | tf_op jit(solution)/shard_map/experts/pallas_call | solution.py:284
  233.4 4.5 all-to-all-start.2
  238.2 3.2 collective-permute-start.14
  245.6 30.5 %collective-permute-done.13 = bf16[2,3,2,128,512]{4,3,2,1,0:T(8,128)(2,1)} collective-permute-done((bf16[2,3,2,128,512]{4,3,2,1,0:T(8,128)(2,1)}, bf16[2,3,2,128,512]{4,3,2,1,0:T(8,128)(2,1)}, u32[]{:S(2)}, u32[]{:S(2)}) %collective-permute-start.13) | collective-permute-done | bytes 1572896 | tf_op jit(solution)/shard_map/ppermute | solution.py:88
  276.1 13.4 %all-to-all-done.2 = bf16[16,96,1152]{2,1,0:T(8,128)(2,1)} async-done(((bf16[16,96,1152]{2,1,0:T(8,128)(2,1)}), bf16[16,96,1152]{2,1,0:T(8,128)(2,1)}, u32[]{:S(2)}, u32[]{:S(2)}) %all-to-all-start.2) | async-done | bytes 3538976 | tf_op jit(solution)/shard_map/all_to_all | solution.py:67
  289.5 4.1 pad_maximum_fusion
  293.6 4.6 all-to-all-start.3
  303.2 3.2 collective-permute-start.15
  314.6 11.2 %attend_back.1 = (f32[128,1024]{1,0:T(8,128)S(1)}, bf16[1024,512]{1,0:T(8,128)(2,1)S(1)}, bf16[1024,512]{1,0:T(8,128)(2,1)S(1)}) custom-call(s32[1]{0:T(128)} %bitcast.1.first_ref, bf16[128,1024]{1,0:T(8,128)(2,1)S(1)} %copy.229.query_ref, bf16[1024,1024]{1,0:T(8,128)(2,1)S(1)} %bitcast.318, bf16[1024,1024]{1,0:T(8,128)(2,1)S(1)} %bitcast.319, ...), custom_call_target="tpu_custom_call" | custom-call | flops 1342177280 | bytes 4194304 | tf_op jit(solution)/shard_map/attend_back/pallas_call | solution.py:442
  333.9 7.8 %collective-permute-done.15 = bf16[2,3,2,128,512]{4,3,2,1,0:T(8,128)(2,1)} collective-permute-done((bf16[2,3,2,128,512]{4,3,2,1,0:T(8,128)(2,1)}, bf16[2,3,2,128,512]{4,3,2,1,0:T(8,128)(2,1)}, u32[]{:S(2)}, u32[]{:S(2)}) %collective-permute-start.15) | collective-permute-done | bytes 1572896 | tf_op jit(solution)/shard_map/ppermute | solution.py:88
  341.7 4.4 all-to-all-start.4
  346.1 3.2 convert_add_fusion
  366.8 33.1 %collective-permute-done.16 = bf16[3,2,128,512]{3,2,1,0:T(8,128)(2,1)} collective-permute-done((bf16[3,2,128,512]{3,2,1,0:T(8,128)(2,1)}, bf16[3,2,128,512]{3,2,1,0:T(8,128)(2,1)}, u32[]{:S(2)}, u32[]{:S(2)}) %collective-permute-start.16) | collective-permute-done | bytes 786464 | tf_op jit(solution)/shard_map/ppermute | solution.py:88
  399.9 3.7 fusion.135
  431.5 7.4 %all-to-all-start.5 = ((bf16[16,152,128]{2,1,0:T(8,128)(2,1)}), bf16[16,152,128]{2,1,0:T(8,128)(2,1)S(1)}, u32[]{:S(2)}, u32[]{:S(2)}) async-start(bf16[16,152,128]{2,1,0:T(8,128)(2,1)} %copy.244), calls=%async_computation.5 | async-start | bytes 1245184 | tf_op jit(solution)/shard_map/all_to_all | solution.py:67
  443.7 19.5 %owner.1 = bf16[1024,512]{1,0:T(8,128)(2,1)S(1)} custom-call(bf16[1024,512]{1,0:T(8,128)(2,1)S(1)} %bitcast.320), custom_call_target="tpu_custom_call" | custom-call | flops 20937965568 | bytes 2097152 | tf_op jit(solution)/shard_map/owner/pallas_call | solution.py:352
  474.4 3.5 all-to-all-start.6
  477.9 4.1 collective-permute-start.26
  491.4 3.5 collective-permute-done.28
  494.9 3.4 collective-permute-done.29
  503.1 3.7 all-to-all-start.7
  (376 shorter events, 174.8 us)
Async XLA Ops:
  7.2 135.9 %all-gather.6.cloned.1.call-start = ((), (), s32[]{:S(2)}) async-start(), calls=%async_computation.8 | async-start | bytes 2228224 | tf_op jit(solution)/shard_map/all_gather | solution.py:539
  7.9 199.1 %all-gather.12.cloned.1.call-start = ((), (), s32[]{:S(2)}) async-start(), calls=%async_computation.11 | async-start | bytes 5013504 | tf_op jit(solution)/shard_map/all_gather | solution.py:556
  15.0 24.1 %collective-permute-start.3 = (bf16[3,2,128,512]{3,2,1,0:T(8,128)(2,1)S(1)}, bf16[3,2,128,512]{3,2,1,0:T(8,128)(2,1)}, u32[]{:S(2)}, u32[]{:S(2)}) collective-permute-start(bf16[3,2,128,512]{3,2,1,0:T(8,128)(2,1)S(1)} %pad_maximum_fusion.3.refs_in_order_0_), channel_id=1, source_target_pairs={{0,16},{16,0},{32,48},{48,32},{64,80},{80,64},{96,112},{112,96},{1... | collective-permute-start | bytes 2359304 | tf_op jit(solution)/shard_map/ppermute | solution.py:88
  15.7 23.4 %collective-permute-start.4 = (bf16[3,2,128,512]{3,2,1,0:T(8,128)(2,1)S(1)}, bf16[3,2,128,512]{3,2,1,0:T(8,128)(2,1)}, u32[]{:S(2)}, u32[]{:S(2)}) collective-permute-start(bf16[3,2,128,512]{3,2,1,0:T(8,128)(2,1)S(1)} %pad_maximum_fusion.3.refs_in_order_0_), channel_id=1, source_target_pairs={{0,32},{16,48},{32,64},{48,80},{64,96},{80,112},{96,0},{112,16},{1... | collective-permute-start | bytes 2359304 | tf_op jit(solution)/shard_map/ppermute | solution.py:88
  17.6 21.5 %collective-permute-start.5 = (bf16[3,2,128,512]{3,2,1,0:T(8,128)(2,1)S(1)}, bf16[3,2,128,512]{3,2,1,0:T(8,128)(2,1)}, u32[]{:S(2)}, u32[]{:S(2)}) collective-permute-start(bf16[3,2,128,512]{3,2,1,0:T(8,128)(2,1)S(1)} %pad_maximum_fusion.3.refs_in_order_0_), channel_id=1, source_target_pairs={{0,96},{16,112},{32,0},{48,16},{64,32},{80,48},{96,64},{112,80},{1... | collective-permute-start | bytes 2359304 | tf_op jit(solution)/shard_map/ppermute | solution.py:88
  22.1 17.1 %collective-permute-start.1 = (bf16[2,136,1024]{2,1,0:T(8,128)(2,1)S(1)}, bf16[2,136,1024]{2,1,0:T(8,128)(2,1)S(1)}, u32[]{:S(2)}, u32[]{:S(2)}) collective-permute-start(bf16[2,136,1024]{2,1,0:T(8,128)(2,1)S(1)} %get-tuple-element.177), channel_id=1, source_target_pairs={{0,4},{1,5},{2,6},{3,7},{4,8},{5,9},{6,10},{7,11},{8,12},{9,13},{1... | collective-permute-start | bytes 1671176 | tf_op jit(solution)/shard_map/ppermute | solution.py:98
  23.8 15.4 %collective-permute-start.2 = (bf16[2,136,1024]{2,1,0:T(8,128)(2,1)S(1)}, bf16[2,136,1024]{2,1,0:T(8,128)(2,1)S(1)}, u32[]{:S(2)}, u32[]{:S(2)}) collective-permute-start(bf16[2,136,1024]{2,1,0:T(8,128)(2,1)S(1)} %get-tuple-element.177), channel_id=1, source_target_pairs={{0,12},{1,13},{2,14},{3,15},{4,0},{5,1},{6,2},{7,3},{8,4},{9,5},{1... | collective-permute-start | bytes 1671176 | tf_op jit(solution)/shard_map/ppermute | solution.py:98
  53.0 21.7 %collective-permute-start.10 = (bf16[3,2,128,512]{3,2,1,0:T(8,128)(2,1)}, bf16[3,2,128,512]{3,2,1,0:T(8,128)(2,1)}, u32[]{:S(2)}, u32[]{:S(2)}) collective-permute-start(bf16[3,2,128,512]{3,2,1,0:T(8,128)(2,1)} %collective-permute-done.3.refs_in_order_1_), channel_id=1, source_target_pairs={{0,96},{16,112},{32,0},{48,16},{64,32},{80,48},{96,64},{112,80},{1... | collective-permute-start | bytes 2359304 | tf_op jit(solution)/shard_map/ppermute | solution.py:88
  57.2 37.8 %collective-permute-start.9 = (bf16[3,2,128,512]{3,2,1,0:T(8,128)(2,1)}, bf16[3,2,128,512]{3,2,1,0:T(8,128)(2,1)}, u32[]{:S(2)}, u32[]{:S(2)}) collective-permute-start(bf16[3,2,128,512]{3,2,1,0:T(8,128)(2,1)} %collective-permute-done.3.refs_in_order_1_), channel_id=1, source_target_pairs={{0,32},{16,48},{32,64},{48,80},{64,96},{80,112},{96,0},{112,16},{1... | collective-permute-start | bytes 2359304 | tf_op jit(solution)/shard_map/ppermute | solution.py:88
  57.2 37.8 %collective-permute-start.11 = (bf16[3,2,128,512]{3,2,1,0:T(8,128)(2,1)}, bf16[3,2,128,512]{3,2,1,0:T(8,128)(2,1)}, u32[]{:S(2)}, u32[]{:S(2)}) collective-permute-start(bf16[3,2,128,512]{3,2,1,0:T(8,128)(2,1)} %collective-permute-done.4.refs_in_order_2_), channel_id=1, source_target_pairs={{0,32},{16,48},{32,64},{48,80},{64,96},{80,112},{96,0},{112,16},{1... | collective-permute-start | bytes 2359304 | tf_op jit(solution)/shard_map/ppermute | solution.py:88
  96.8 39.1 %all-to-all-start = ((bf16[8,128,1024]{2,1,0:T(8,128)(2,1)}), bf16[8,128,1024]{2,1,0:T(8,128)(2,1)S(1)}, u32[]{:S(2)}, u32[]{:S(2)}) async-start(bf16[8,128,1024]{2,1,0:T(8,128)(2,1)} %broadcast_in_dim.42), calls=%async_computation | async-start | bytes 4194304 | tf_op jit(solution)/shard_map/all_to_all | solution.py:67
  155.0 51.4 %all-to-all-start.1 = ((bf16[16,96,1152]{2,1,0:T(8,128)(2,1)}), bf16[16,96,1152]{2,1,0:T(8,128)(2,1)}, u32[]{:S(2)}, u32[]{:S(2)}) async-start(bf16[16,96,1152]{2,1,0:T(8,128)(2,1)} %bitcast.327), calls=%async_computation.1 | async-start | bytes 7077888 | tf_op jit(solution)/shard_map/all_to_all | solution.py:67
  161.6 301.7 %all-gather.8.cloned.1.call-start = ((), (), s32[]{:S(2)}) async-start(), calls=%async_computation.9 | async-start | bytes 4456448 | tf_op jit(solution)/shard_map/all_gather | solution.py:599
  161.6 45.4 %collective-permute-start.12 = (bf16[3,2,128,512]{3,2,1,0:T(8,128)(2,1)}, bf16[3,2,128,512]{3,2,1,0:T(8,128)(2,1)}, u32[]{:S(2)}, u32[]{:S(2)}) collective-permute-start(bf16[3,2,128,512]{3,2,1,0:T(8,128)(2,1)} %collective-permute-done.10.refs_in_order_5_), channel_id=1, source_target_pairs={{0,96},{16,112},{32,0},{48,16},{64,32},{80,48},{96,64},{112,80},{1... | collective-permute-start | bytes 2359304 | tf_op jit(solution)/shard_map/ppermute | solution.py:88
  233.4 56.1 %all-to-all-start.2 = ((bf16[16,96,1152]{2,1,0:T(8,128)(2,1)}), bf16[16,96,1152]{2,1,0:T(8,128)(2,1)}, u32[]{:S(2)}, u32[]{:S(2)}) async-start(bf16[16,96,1152]{2,1,0:T(8,128)(2,1)} %bitcast.330), calls=%async_computation.2 | async-start | bytes 7077888 | tf_op jit(solution)/shard_map/all_to_all | solution.py:67
  237.9 38.3 %collective-permute-start.13 = (bf16[2,3,2,128,512]{4,3,2,1,0:T(8,128)(2,1)}, bf16[2,3,2,128,512]{4,3,2,1,0:T(8,128)(2,1)}, u32[]{:S(2)}, u32[]{:S(2)}) collective-permute-start(bf16[2,3,2,128,512]{4,3,2,1,0:T(8,128)(2,1)} %get-tuple-element.78), channel_id=1, source_target_pairs={{0,32},{16,48},{32,64},{48,80},{64,96},{80,112},{96,0},{112,16},{1... | collective-permute-start | bytes 4718600 | tf_op jit(solution)/shard_map/ppermute | solution.py:88
  238.2 38.0 %collective-permute-start.14 = (bf16[2,3,2,128,512]{4,3,2,1,0:T(8,128)(2,1)}, bf16[2,3,2,128,512]{4,3,2,1,0:T(8,128)(2,1)}, u32[]{:S(2)}, u32[]{:S(2)}) collective-permute-start(bf16[2,3,2,128,512]{4,3,2,1,0:T(8,128)(2,1)} %get-tuple-element.79), channel_id=1, source_target_pairs={{0,96},{16,112},{32,0},{48,16},{64,32},{80,48},{96,64},{112,80},{1... | collective-permute-start | bytes 4718600 | tf_op jit(solution)/shard_map/ppermute | solution.py:88
  293.6 48.1 %all-to-all-start.3 = ((bf16[16,104,1024]{2,1,0:T(8,128)(2,1)}), bf16[16,104,1024]{2,1,0:T(8,128)(2,1)}, u32[]{:S(2)}, u32[]{:S(2)}) async-start(bf16[16,104,1024]{2,1,0:T(8,128)(2,1)} %pad_maximum_fusion), calls=%async_computation.3 | async-start | bytes 6815744 | tf_op jit(solution)/shard_map/all_to_all | solution.py:67
  298.2 172.2 %all-gather.10.cloned.1.call-start = ((), (), s32[]{:S(2)}) async-start(), calls=%async_computation.10 | async-start | bytes 4456448 | tf_op jit(solution)/shard_map/all_gather | solution.py:634
  303.2 38.4 %collective-permute-start.15 = (bf16[2,3,2,128,512]{4,3,2,1,0:T(8,128)(2,1)}, bf16[2,3,2,128,512]{4,3,2,1,0:T(8,128)(2,1)}, u32[]{:S(2)}, u32[]{:S(2)}) collective-permute-start(bf16[2,3,2,128,512]{4,3,2,1,0:T(8,128)(2,1)} %get-tuple-element.85), channel_id=1, source_target_pairs={{0,64},{16,80},{32,96},{48,112},{64,0},{80,16},{96,32},{112,48},{1... | collective-permute-start | bytes 4718600 | tf_op jit(solution)/shard_map/ppermute | solution.py:88
  341.7 70.1 %all-to-all-start.4 = ((bf16[8,128,1024]{2,1,0:T(8,128)(2,1)}), bf16[8,128,1024]{2,1,0:T(8,128)(2,1)}, u32[]{:S(2)}, u32[]{:S(2)}) async-start(bf16[8,128,1024]{2,1,0:T(8,128)(2,1)} %bitcast.328), calls=%async_computation.4 | async-start | bytes 4194304 | tf_op jit(solution)/shard_map/all_to_all | solution.py:67
  350.4 49.5 %collective-permute-start.16 = (bf16[3,2,128,512]{3,2,1,0:T(8,128)(2,1)}, bf16[3,2,128,512]{3,2,1,0:T(8,128)(2,1)}, u32[]{:S(2)}, u32[]{:S(2)}) collective-permute-start(bf16[3,2,128,512]{3,2,1,0:T(8,128)(2,1)} %fusion.28), channel_id=1, source_target_pairs={{0,16},{16,0},{32,48},{48,32},{64,80},{80,64},{96,112},{112,96},{1... | collective-permute-start | bytes 2359304 | tf_op jit(solution)/shard_map/ppermute | solution.py:88
  404.6 17.8 %collective-permute-start.17 = (bf16[128,512]{1,0:T(8,128)(2,1)}, bf16[128,512]{1,0:T(8,128)(2,1)}, u32[]{:S(2)}, u32[]{:S(2)}) collective-permute-start(bf16[128,512]{1,0:T(8,128)(2,1)} %get-tuple-element.163), channel_id=1, source_target_pairs={{0,16},{16,0},{32,48},{48,32},{64,80},{80,64},{96,112},{112,96},{1... | collective-permute-start | bytes 393224 | tf_op jit(solution)/shard_map/ppermute | solution.py:88
  404.6 19.6 %collective-permute-start.18 = (bf16[128,512]{1,0:T(8,128)(2,1)}, bf16[128,512]{1,0:T(8,128)(2,1)}, u32[]{:S(2)}, u32[]{:S(2)}) collective-permute-start(bf16[128,512]{1,0:T(8,128)(2,1)} %get-tuple-element.164), channel_id=1, source_target_pairs={{0,32},{16,48},{32,64},{48,80},{64,96},{80,112},{96,0},{112,16},{1... | collective-permute-start | bytes 393224 | tf_op jit(solution)/shard_map/ppermute | solution.py:88
  405.8 21.2 %collective-permute-start.19 = (bf16[128,512]{1,0:T(8,128)(2,1)}, bf16[128,512]{1,0:T(8,128)(2,1)}, u32[]{:S(2)}, u32[]{:S(2)}) collective-permute-start(bf16[128,512]{1,0:T(8,128)(2,1)} %get-tuple-element.165), channel_id=1, source_target_pairs={{0,48},{16,32},{32,80},{48,64},{64,112},{80,96},{96,16},{112,0},{1... | collective-permute-start | bytes 393224 | tf_op jit(solution)/shard_map/ppermute | solution.py:88
  408.8 18.2 %collective-permute-start.20 = (bf16[128,512]{1,0:T(8,128)(2,1)}, bf16[128,512]{1,0:T(8,128)(2,1)}, u32[]{:S(2)}, u32[]{:S(2)}) collective-permute-start(bf16[128,512]{1,0:T(8,128)(2,1)} %get-tuple-element.166), channel_id=1, source_target_pairs={{0,64},{16,80},{32,96},{48,112},{64,0},{80,16},{96,32},{112,48},{1... | collective-permute-start | bytes 393224 | tf_op jit(solution)/shard_map/ppermute | solution.py:88
  410.8 16.2 %collective-permute-start.21 = (bf16[128,512]{1,0:T(8,128)(2,1)}, bf16[128,512]{1,0:T(8,128)(2,1)}, u32[]{:S(2)}, u32[]{:S(2)}) collective-permute-start(bf16[128,512]{1,0:T(8,128)(2,1)} %get-tuple-element.167), channel_id=1, source_target_pairs={{0,80},{16,64},{32,112},{48,96},{64,16},{80,0},{96,48},{112,32},{1... | collective-permute-start | bytes 393224 | tf_op jit(solution)/shard_map/ppermute | solution.py:88
  431.5 31.6 %all-to-all-start.5 = ((bf16[16,152,128]{2,1,0:T(8,128)(2,1)}), bf16[16,152,128]{2,1,0:T(8,128)(2,1)S(1)}, u32[]{:S(2)}, u32[]{:S(2)}) async-start(bf16[16,152,128]{2,1,0:T(8,128)(2,1)} %copy.244), calls=%async_computation.5 | async-start | bytes 1245184 | tf_op jit(solution)/shard_map/all_to_all | solution.py:67
  467.0 18.5 %collective-permute-start.24 = (bf16[128,512]{1,0:T(8,128)(2,1)}, bf16[128,512]{1,0:T(8,128)(2,1)}, u32[]{:S(2)}, u32[]{:S(2)}) collective-permute-start(bf16[128,512]{1,0:T(8,128)(2,1)} %get-tuple-element.148), channel_id=1, source_target_pairs={{0,16},{16,0},{32,48},{48,32},{64,80},{80,64},{96,112},{112,96},{1... | collective-permute-start | bytes 393224 | tf_op jit(solution)/shard_map/ppermute | solution.py:88
  467.8 17.7 %collective-permute-start.25 = (bf16[128,512]{1,0:T(8,128)(2,1)S(1)}, bf16[128,512]{1,0:T(8,128)(2,1)}, u32[]{:S(2)}, u32[]{:S(2)}) collective-permute-start(bf16[128,512]{1,0:T(8,128)(2,1)S(1)} %get-tuple-element.147), channel_id=1, source_target_pairs={{0,96},{16,112},{32,0},{48,16},{64,32},{80,48},{96,64},{112,80},{1... | collective-permute-start | bytes 393224 | tf_op jit(solution)/shard_map/ppermute | solution.py:88
  474.4 23.9 %all-to-all-start.6 = ((bf16[8,216,128]{2,1,0:T(8,128)(2,1)}), bf16[8,216,128]{2,1,0:T(8,128)(2,1)S(1)}, u32[]{:S(2)}, u32[]{:S(2)}) async-start(bf16[8,216,128]{2,1,0:T(8,128)(2,1)} %pad_maximum_fusion.5), calls=%async_computation.6 | async-start | bytes 884736 | tf_op jit(solution)/shard_map/all_to_all | solution.py:67
  485.5 12.8 %collective-permute-start.29 = (bf16[128,512]{1,0:T(8,128)(2,1)S(1)}, bf16[128,512]{1,0:T(8,128)(2,1)S(1)}, u32[]{:S(2)}, u32[]{:S(2)}) collective-permute-start(bf16[128,512]{1,0:T(8,128)(2,1)S(1)} %get-tuple-element.143), channel_id=1, source_target_pairs={{0,32},{16,48},{32,64},{48,80},{64,96},{80,112},{96,0},{112,16},{1... | collective-permute-start | bytes 393224 | tf_op jit(solution)/shard_map/ppermute | solution.py:88
  (75 other events, 656.5 us)
Sparse Core Ops, SparseCore 0:
  10.5 51.6 all-gather.5
  65.3 65.2 all-gather.11
  206.6 72.4 all-gather.7
  331.6 66.2 all-gather.9

commit v5 on v4

--- a/solution.py
+++ b/solution.py
@@ -88,6 +88,17 @@
     return lax.ppermute(block, "ctx", pairs)
 
 
+def plus(left, right):
+    return (left.astype(jnp.float32) + right.astype(jnp.float32)).astype(jnp.bfloat16)
+
+
+def owner_move(block, up):
+    pairs = [
+        (2 * z + x, 2 * ((z + up) % 4) + x) for z in range(4) for x in range(2) if (z + up) % 4 < 3
+    ]
+    return lax.ppermute(block, "ctx", pairs)
+
+
 def exp_move(block, up, far, core):
     pairs = [
         (4 * y + 2 * h + c, 4 * ((y + up) % 4) + 2 * (h ^ far) + (c ^ core))
@@ -183,12 +194,11 @@
 
 
 def expert_kernel(own_ref, arrived_ref, grads_ref, *refs_in_order):
-    blocks, refs = refs_in_order[:8], refs_in_order[8:]
-    expert_steps(own_ref, arrived_ref, grads_ref, blocks, *refs)
-
-
-def expert_steps(own_ref, arrived_ref, grads_ref, blocks,
-                  made_ref, back_ref, sums_ref, sums_up_ref, sums_down_ref, sums_far_ref,
+    blocks, momenta, refs = refs_in_order[:8], refs_in_order[8:11], refs_in_order[11:]
+    expert_steps(own_ref, arrived_ref, grads_ref, blocks, momenta, *refs)
+
+
+def expert_steps(own_ref, arrived_ref, grads_ref, blocks, momenta, made_ref, back_ref, sums_ref,
                   weight_ref, rows_ref, hidden_ref, dgate_ref, dup_ref, dy_ref):
     expert = own_ref[0] + pl.program_id(0)
     level, side = own_ref[1], own_ref[2]
@@ -258,18 +268,20 @@
         return carry
 
     lax.fori_loop(0, CHUNKS, forward, 0)
-    for up, ref in ((0, sums_ref), (1, sums_up_ref), (3, sums_down_ref), (2, sums_far_ref)):
-        for other in range(2):
-            columns = part(up, other)
-            rows = rows_ref[:, columns]
-            ref[other, 0, 0] = contract_rows(rows, dgate_ref[...]).astype(jnp.bfloat16)
-            ref[other, 1, 0] = contract_rows(rows, dup_ref[...]).astype(jnp.bfloat16)
-            ref[other, 2, 0] = contract_rows(dy_ref[:, columns], hidden_ref[...]).astype(
-                jnp.bfloat16
-            )
-
-
-def expert_math(arrived, all_grads, weights):
+    own_part = 2 * level + side
+    pairs = ((rows_ref, dgate_ref), (rows_ref, dup_ref), (dy_ref, hidden_ref))
+    for kind in range(3):
+        slot = lax.rem(kind - level + 4, 4)
+        left, right = pairs[kind]
+        for index in range(D // width):
+            rows = slice(index * width, (index + 1) * width)
+            added = jnp.where(index == own_part, mom_rate, 0.0) * momenta[kind][0]
+            total = contract_rows(left[:, rows], right[...]) + added
+            sums_ref[slot, 0, rows] = total.astype(jnp.bfloat16)
+    sums_ref[lax.rem(7 - level, 4), 0] = jnp.zeros((D, FF), jnp.bfloat16)
+
+
+def expert_math(arrived, all_grads, weights, momenta):
     seqs, per_group = arrived.shape[:2]
     place = lax.axis_index("ctx")
     own = jnp.stack([lax.axis_index("exp") * per_group, place // 2, place % 2]).astype(jnp.int32)
@@ -278,7 +290,10 @@
     def rows_spec(width):
         return pl.BlockSpec((seqs, 1, CAP, width), lambda e, own: (0, e, 0, 0))
 
-    two = pl.BlockSpec((2, 3, 1, rows_each, FF), lambda e, own: (0, 0, e, 0, 0))
+    summed = pl.BlockSpec(
+        (4, 1, D, FF), lambda e, own: (0, e + own[2] - 2 * e * own[2], 0, 0)
+    )
+    momentum = pl.BlockSpec((1, rows_each, FF), lambda e, own: (e, 0, 0))
     one = pl.BlockSpec((3, 1, rows_each, FF), lambda e, own: (0, e, 0, 0))
     whole = pl.BlockSpec(all_grads.shape, lambda e, own: (0, 0, 0))
     return pl.pallas_call(
@@ -286,8 +301,8 @@
         grid_spec=pltpu.PrefetchScalarGridSpec(
             num_scalar_prefetch=1,
             grid=(per_group,),
-            in_specs=[rows_spec(D + WIDE), whole] + [one] * 8,
-            out_specs=[rows_spec(D), rows_spec(D + WIDE), two, two, two, two],
+            in_specs=[rows_spec(D + WIDE), whole] + [one] * 8 + [momentum] * 3,
+            out_specs=[rows_spec(D), rows_spec(D + WIDE), summed],
             scratch_shapes=[
                 pltpu.VMEM((3, D, FF), jnp.bfloat16),
                 pltpu.VMEM((ROWS, D), jnp.bfloat16),
@@ -300,8 +315,8 @@
         out_shape=[
             jax.ShapeDtypeStruct((seqs, per_group, CAP, D), jnp.bfloat16),
             jax.ShapeDtypeStruct((seqs, per_group, CAP, D + WIDE), jnp.bfloat16),
-        ]
-        + [jax.ShapeDtypeStruct((2, 3, per_group, rows_each, FF), jnp.bfloat16)] * 4,
+            jax.ShapeDtypeStruct((4, per_group, D, FF), jnp.bfloat16),
+        ],
         compiler_params=pltpu.CompilerParams(vmem_limit_bytes=56 * 2**20),
         cost_estimate=pl.CostEstimate(
             flops=18 * ROWS * per_group * D * FF,
@@ -309,7 +324,7 @@
             transcendentals=ROWS * per_group * FF,
         ),
         name="experts",
-    )(own, arrived, all_grads, *weights)
+    )(own, arrived, all_grads, *weights, *momenta)
 
 
 def split_two(value):
@@ -321,7 +336,7 @@
     return mat(left[0], right[0]) + (mat(left[0], right[1]) + mat(left[1], right[0]))
 
 
-def owner_kernel(matrix_ref, out_ref, gram_ref, total_ref):
+def owner_kernel(place_ref, matrix_ref, keep_ref, cross_ref, gram_ref, total_ref, ortho_ref):
     gram = contract_rows(matrix_ref[...], matrix_ref[...])
     width = gram_ref.shape[0]
     row = lax.broadcasted_iota(jnp.int32, (width, width), 0)
@@ -344,28 +359,39 @@
     lax.fori_loop(0, 5, step, 0)
     high, low = split_two(total_ref[...])
     matrix = matrix_ref[...]
-    out_ref[...] = ((mat(matrix, high) + mat(matrix, low)) * scale).astype(out_ref.dtype)
-
-
-def owner_orthogonal(stacked):
-    rows, width = stacked.shape
+    ortho_ref[...] = ((mat(matrix, high) + mat(matrix, low)) * scale).astype(ortho_ref.dtype)
+    level, side = place_ref[0], place_ref[1]
+    rows = keep_ref.shape[2]
+    for up in range(4):
+        for ref, column in ((keep_ref, side), (cross_ref, 1 - side)):
+            index = 2 * lax.rem(level + up, 4) + column
+            where = pl.ds(pl.multiple_of(index * rows, rows), rows)
+            ref[up, 0] = matrix_ref[where]
+            ref[up, 1] = ortho_ref[where]
+
+
+def owner_orthogonal(matrix, place):
+    rows, width = matrix.shape
+    whole = pl.BlockSpec(memory_space=pltpu.VMEM)
+    sent = jax.ShapeDtypeStruct((4, 2, rows // 8, width), jnp.bfloat16)
     return pl.pallas_call(
         owner_kernel,
-        out_shape=jax.ShapeDtypeStruct(stacked.shape, jnp.bfloat16),
-        in_specs=[pl.BlockSpec(memory_space=pltpu.VMEM)],
-        out_specs=pl.BlockSpec(memory_space=pltpu.VMEM),
+        out_shape=[sent, sent],
+        in_specs=[pl.BlockSpec(memory_space=pltpu.SMEM), whole],
+        out_specs=[whole, whole],
         scratch_shapes=[
             pltpu.VMEM((width, width), jnp.float32),
             pltpu.VMEM((width, width), jnp.float32),
+            pltpu.VMEM((rows, width), jnp.bfloat16),
         ],
         compiler_params=pltpu.CompilerParams(vmem_limit_bytes=48 * 2**20),
         cost_estimate=pl.CostEstimate(
             flops=6 * (22 * width**3 + 2 * rows * width**2),
-            bytes_accessed=4 * rows * width,
+            bytes_accessed=6 * rows * width,
             transcendentals=0,
         ),
         name="owner",
-    )(stacked)
+    )(place, matrix)
 
 
 def probabilities(queries, keys, first):
@@ -570,18 +596,11 @@
     keys = rotate(kv_raw[:, :KV], cosine, sine).astype(bf16)
     values = kv_raw[:, KV:].astype(bf16)
     sent_kv = jnp.concatenate([keys, values], axis=1).reshape(row_count, 2 * KV * HD)
-    sent_kv, below_other, above_other, far = lax.optimization_barrier(
-        (sent_kv, below_other, above_other, far)
-    )
-    far_other = ctx_move(above_other, 3, 0)
-    full_experts = (
-        own_experts, other_experts, below, below_other, above, above_other, far, far_other
-    )
     all_kv = spread(sent_kv, "ctx", None, ctx_count).reshape(ctx_count * row_count, 2 * KV * HD)
     flat_queries = queries.reshape(row_count, HEADS * HD)
     mixed_low = attention_call(attend_kernel, (flat_queries, all_kv), None, first_row, "attend")
     sent_mixed = mixed_low.reshape(row_count, exp_count, HD).transpose(1, 0, 2)
-    sent_mixed = sent_mixed.reshape(exp_count, row_count * HD // D, D)
+    sent_mixed = sent_mixed.reshape(exp_count, row_count // 2, 2 * HD)
     attended = mat(mixed_low, full_output)
     residual = inputs + attended
     inv_two = lax.rsqrt(jnp.mean(residual * residual, axis=-1, keepdims=True) + eps_norm)
@@ -594,26 +613,34 @@
         [normed_two, *gate_parts, jnp.zeros((row_count, WIDE - 3 * EXPERTS), bf16)], axis=1
     )
     sent_rows = contract_rows(select, extended).astype(bf16)
+    sent_rows, below_other, above_other, far = lax.optimization_barrier(
+        (sent_rows, below_other, above_other, far)
+    )
+    far_other = ctx_move(above_other, 3, 0)
     arrived = exchange(sent_rows.reshape(exp_count, per_group * CAP, D + WIDE), "exp")
-    later_normed, arrived = lax.optimization_barrier((normed_one, arrived))
+    later_normed, arrived, far_other = lax.optimization_barrier((normed_one, arrived, far_other))
+    full_experts = (
+        own_experts, other_experts, below, below_other, above, above_other, far, far_other
+    )
     all_normed = lax.all_gather(later_normed, "exp", axis=0, tiled=True)
-    produced, back, *expert_grads = expert_math(
-        arrived.reshape(exp_count, per_group, CAP, D + WIDE), all_grads, full_experts
-    )
+    produced, back, expert_grads = expert_math(
+        arrived.reshape(exp_count, per_group, CAP, D + WIDE),
+        all_grads,
+        full_experts,
+        (gate_momentum, up_momentum, down_momentum),
+    )
+    head_mixed = exchange(after(sent_mixed, arrived), "exp")
+    back, head_mixed = lax.optimization_barrier((back, head_mixed))
+    head_mixed = head_mixed.reshape(exp_count * row_count, HD)
     returned = exchange(back.reshape(exp_count, per_group * CAP, D + WIDE), "exp")
     returned = returned.reshape(EXPERTS * CAP, D + WIDE)
-    sum_same, sum_up, sum_down, sum_far = expert_grads
-    sum_up, sum_down, sum_far = (
-        ctx_move(sum_up, 1, 0),
-        ctx_move(sum_down, 3, 0),
-        ctx_move(sum_far, 2, 0),
-    )
-    returned, sum_up, sum_down = lax.optimization_barrier((returned, sum_up, sum_down))
+    far_up, far_down = ctx_move(expert_grads[2, 0], 1, 0), ctx_move(expert_grads[2, 1], 3, 0)
+    sum_up = jnp.stack([plus(expert_grads[1, 0], far_up), expert_grads[1, 1]])
+    sum_down = jnp.stack([expert_grads[3, 0], plus(expert_grads[3, 1], far_down)])
+    returned = after(returned, sum_up, sum_down)
+    sum_up, sum_down = owner_move(sum_up, 1), owner_move(sum_down, 3)
     produced = after(produced, returned)
-    route_values = exchange(
-        jnp.concatenate([produced.reshape(exp_count, per_group * CAP, D), sent_mixed], axis=1),
-        "exp",
-    )
+    route_values = exchange(produced.reshape(exp_count, per_group * CAP, D), "exp")
     summed_back = mat(select, returned)
     tail = summed_back[:, D:]
     grad_gates = (
@@ -632,41 +659,23 @@
     )
     grad_attended = grad_residual.astype(bf16)
     all_attended = lax.all_gather(grad_attended, "exp", axis=0, tiled=True)
+    grad_attended = after(grad_attended, sum_up, sum_down)
+    both_sums = (
+        expert_grads[0].astype(jnp.float32)
+        + sum_up.astype(jnp.float32)
+        + sum_down.astype(jnp.float32)
+    )
+    other_sums = ctx_move(both_sums[1].astype(bf16), 0, 1)
     grad_mixed = contract_cols(grad_attended, full_output).astype(bf16)
     grad_queries, key_terms, value_terms = attention_call(
         attend_back_kernel, (flat_queries, all_kv), grad_mixed, first_row, "attend_back"
     )
     kv_terms = jnp.concatenate([key_terms, value_terms], axis=1)
-    kv_terms, route_values, sum_far = lax.optimization_barrier(
-        (kv_terms, route_values, sum_far)
-    )
-    both_sums = (
-        sum_same.astype(jnp.float32)
-        + sum_up.astype(jnp.float32)
-        + sum_down.astype(jnp.float32)
-        + sum_far.astype(jnp.float32)
-    )
-    other_sums = ctx_move(both_sums[1].astype(bf16), 0, 1)
+    kv_terms, route_values = lax.optimization_barrier((kv_terms, route_values))
     kv_terms = exchange(kv_terms.reshape(ctx_count, row_count, 2 * KV * HD), "ctx")
     grad_query_raw = rotate(
         grad_queries.reshape(row_count, HEADS, HD), cosine, -sine
     ).astype(bf16)
-    expert_sums = both_sums[0] + other_sums.astype(jnp.float32)
-    momenta = jnp.stack([gate_momentum, up_momentum, down_momentum])
-    fresh = mom_rate * momenta + expert_sums
-    matrix_count = 3 * per_group
-    rows_each = fresh.shape[2]
-    sent_fresh = jnp.pad(
-        fresh.astype(bf16).reshape(matrix_count, rows_each, -1),
-        ((0, ctx_count - matrix_count), (0, 0), (0, 0)),
-    )
-    level, side = lax.axis_index("ctx") // 2, lax.axis_index("ctx") % 2
-    moves = [(up, other) for up in range(4) for other in range(2)]
-    owned = []
-    for up, other in moves:
-        owner = 2 * ((level + up) % 4) + (side + other) % 2
-        block = lax.dynamic_index_in_dim(sent_fresh, owner, 0, keepdims=False)
-        owned.append(ctx_move(block, up, other) if up or other else block)
     kv_sums = jnp.sum(kv_terms.astype(jnp.float32), axis=0).reshape(row_count, 2 * KV, HD)
     grad_key_raw = rotate(kv_sums[:, :KV], cosine, -sine).astype(bf16)
     grad_kv_raw = jnp.concatenate([grad_key_raw, kv_sums[:, KV:].astype(bf16)], axis=1)
@@ -697,18 +706,15 @@
         ],
         axis=1,
     ).astype(bf16)
-    head_mixed = route_values[:, per_group * CAP :].reshape(exp_count * row_count, HD)
-    route_values = route_values[:, : per_group * CAP].reshape(EXPERTS * CAP, D)
+    route_values = route_values.reshape(EXPERTS * CAP, D)
     head_send = jnp.concatenate([jnp.transpose(grad_projected, (1, 0, 2)), small], axis=1)
+    level, side = lax.axis_index("ctx") // 2, lax.axis_index("ctx") % 2
+    owned = (both_sums[0] + other_sums.astype(jnp.float32)).astype(bf16)
     head_send, owned = lax.optimization_barrier((head_send, owned))
     head_grads = exchange(head_send, "exp")
-    ortho = owner_orthogonal(jnp.stack(owned).reshape(ctx_count * rows_each, -1))
-    head_grads, ortho = lax.optimization_barrier((head_grads, ortho))
-    ortho = ortho.reshape(ctx_count, rows_each, -1)
-    returned_rows = [
-        ctx_move(ortho[index], (4 - up) % 4, other) if up or other else ortho[index]
-        for index, (up, other) in enumerate(moves)
-    ]
+    keep, cross = owner_orthogonal(owned, jnp.stack([level, side]).astype(jnp.int32))
+    head_grads = after(head_grads, keep, cross)
+    crossed = ctx_move(cross, 0, 1)
     small = jnp.sum(head_grads[:, row_count : row_count + small_rows].astype(jnp.float32), axis=0)
     head_grads = head_grads[:, :row_count].reshape(exp_count * row_count, 2 * HD)
 
@@ -729,7 +735,11 @@
         ],
         axis=1,
     )
-    part, *returned_rows = lax.optimization_barrier((exchange(part, "ctx"), *returned_rows))
+    part, crossed = lax.optimization_barrier((exchange(part, "ctx"), crossed))
+    returned_rows = [
+        ctx_move(jnp.stack([keep[up], crossed[up]]), up, 0) if up else jnp.stack([keep[0], crossed[0]])
+        for up in range(4)
+    ]
     part = jnp.sum(part.astype(jnp.float32), axis=0)
     sums = spread(part[: 3 * HD].astype(bf16), "ctx", None, ctx_count)
     sums = jnp.transpose(sums, (0, 2, 1)).reshape(D, 3 * HD).astype(jnp.float32)
@@ -749,20 +759,24 @@
         jnp.concatenate([query_weight, kv_weight, output_weight], axis=1),
     )
 
-    returned_rows = jnp.stack(returned_rows)
-    ortho = jnp.stack(
-        [
+    returned_rows = jnp.stack(returned_rows).reshape(8, 2, D // ctx_count, -1)
+    fresh, ortho = [], []
+    for kind in range(3):
+        picked = [
             lax.dynamic_index_in_dim(
                 returned_rows,
-                2 * ((matrix // 2 - level) % 4) + (matrix + side) % 2,
+                2 * ((level + 4 - kind) % 4) + (expert + side) % 2,
                 0,
                 keepdims=False,
-            )
-            for matrix in range(matrix_count)
+            ).astype(jnp.float32)
+            for expert in range(per_group)
         ]
-    )
-    ortho = ortho.reshape(fresh.shape).astype(jnp.float32)
-    new = step_weight(jnp.stack([gate_weight, up_weight, down_weight]), ortho)
+        fresh.append(jnp.stack([rows[0] for rows in picked]))
+        ortho.append(jnp.stack([rows[1] for rows in picked]))
+    new = [
+        step_weight(weight, factor)
+        for weight, factor in zip((gate_weight, up_weight, down_weight), ortho)
+    ]
 
     gates_wide = [mat(part, widen) for part in gate_parts]
     block_value = residual

time: 542 us -> 505 us (0.932)
  local copies, waits for them, and re-layouts: 55.7 us -> 35.9 us
  waiting for transfers between devices: 225 us -> 211 us
  starting transfers between devices: 92.1 us -> 80.4 us
  other arithmetic: 37.9 us -> 44 us
    ppermute x0 -> x2, waiting for transfers between devices: none -> 28.7 us  [owner_move(): return lax.ppermute(block, 'ctx', pairs)]
    ppermute x25 -> x14, waiting for transfers between devices: 130 us -> 104 us  [ctx_move(): return lax.ppermute(block, 'ctx', pairs)]
    ppermute x25 -> x14, starting transfers between devices: 43.5 us -> 19.1 us  [ctx_move(): return lax.ppermute(block, 'ctx', pairs)]
    all_to_all x8 -> x9, waiting for transfers between devices: 84.7 us -> 64.1 us  [exchange(): lax.all_to_all(blocks, axis, split_axis=0, concat_axis=0, tiled=True, axi...]
    all_to_all x8 -> x9, starting transfers between devices: 38.5 us -> 48.1 us  [exchange(): lax.all_to_all(blocks, axis, split_axis=0, concat_axis=0, tiled=True, axi...]
    another operation x4 -> x16, other arithmetic: 1.91 us -> 10.6 us  [the longest x2 3.68 us: body(): jnp.stack([expert_grads[3, 0], plus(expert_grads[3, 1], far_down)])]
    unnamed x150 -> x159, local copies, waits for them, and re-layouts: 14.7 us -> 6.7 us
  transfers between devices with their start and end apart: 43 -> 35, of which waited for: 19 -> 20; matrix products, arithmetic and copies ran while one was open for 22% -> 22% of each run, Pallas kernels for 12% -> 13%
where the time goes in v5:
time: 505 us; the launch traced here: 496 us
  waiting for transfers between devices  211 us (42%)
  starting transfers between devices  80.4 us (16%)
  Pallas kernels  65.3 us (13%)
  other arithmetic  44 us (9%)
  matrix products  42.9 us (8%)
  local copies, waits for them, and re-layouts  35.9 us (7%)
  between operations  16.1 us (3%)
    ppermute x14, waiting for transfers between devices, ctx_move(): return lax.ppermute(block, 'ctx', pairs)  104 us
    all_to_all x9, waiting for transfers between devices, exchange(): lax.all_to_all(blocks, axis, split_axis=0, concat_axis=0, tiled=True, axi...  64.1 us
    all_to_all x9, starting transfers between devices, exchange(): lax.all_to_all(blocks, axis, split_axis=0, concat_axis=0, tiled=True, axi...  48.1 us
    ppermute x2, waiting for transfers between devices, owner_move(): return lax.ppermute(block, 'ctx', pairs)  28.7 us
    pallas_call x1, Pallas kernels, expert_math(): pl.pallas_call(expert_kernel, grid_spec=pltpu.PrefetchScalarGridSpec(num_...  26.8 us
    dot_general x12, matrix products, mat(): return jnp.dot(left, right, preferred_element_type=jnp.float32)  25.5 us
    pallas_call x1, Pallas kernels, owner_orthogonal(): pl.pallas_call(owner_kernel, out_shape=[sent, sent], in_specs=[pl.BlockSp...  20.1 us
    ppermute x14, starting transfers between devices, ctx_move(): return lax.ppermute(block, 'ctx', pairs)  19.1 us
  transfers between devices with their start and end apart: 35, of which 20 were waited for; matrix products, arithmetic and copies ran while one was open for 22% of the time, Pallas kernels for 13%

profile of v5, /device:TPU:0, one launch (start us, length us, event | category | flops | bytes accessed | tf_op | source)
XLA Modules:
  0.0 495.6 jit_solution(8962696946693208638)
XLA Ops:
  25.4 13.8 %collective-permute-done.3.refs_in_order_1_ = bf16[3,2,128,512]{3,2,1,0:T(8,128)(2,1)} collective-permute-done((bf16[3,2,128,512]{3,2,1,0:T(8,128)(2,1)S(1)}, bf16[3,2,128,512]{3,2,1,0:T(8,128)(2,1)}, u32[]{:S(2)}, u32[]{:S(2)}) %collective-permute-start.3) | collective-permute-done | bytes 786464 | tf_op jit(solution)/shard_map/ppermute | solution.py:88
  42.4 6.3 %collective-permute-done.7 = bf16[136,1024]{1,0:T(8,128)(2,1)S(1)} collective-permute-done((bf16[136,1024]{1,0:T(8,128)(2,1)S(1)}, bf16[136,1024]{1,0:T(8,128)(2,1)S(1)}, u32[]{:S(2)}, u32[]{:S(2)}) %collective-permute-start.7) | collective-permute-done | bytes 278560 | tf_op jit(solution)/shard_map/ppermute | solution.py:109
  48.7 3.9 collective-permute-done.6
  65.6 6.5 %all-to-all-start = ((bf16[8,128,1024]{2,1,0:T(8,128)(2,1)}), bf16[8,128,1024]{2,1,0:T(8,128)(2,1)S(1)}, u32[]{:S(2)}, u32[]{:S(2)}) async-start(bf16[8,128,1024]{2,1,0:T(8,128)(2,1)} %broadcast_in_dim.45), calls=%async_computation | async-start | bytes 4194304 | tf_op jit(solution)/shard_map/all_to_all | solution.py:67
  84.3 18.2 %all-to-all-done = bf16[8,128,1024]{2,1,0:T(8,128)(2,1)S(1)} async-done(((bf16[8,128,1024]{2,1,0:T(8,128)(2,1)}), bf16[8,128,1024]{2,1,0:T(8,128)(2,1)S(1)}, u32[]{:S(2)}, u32[]{:S(2)}) %all-to-all-start) | async-done | bytes 2097184 | tf_op jit(solution)/shard_map/all_to_all | solution.py:67
  102.5 7.2 %attend.1 = bf16[128,1024]{1,0:T(8,128)(2,1)S(1)} custom-call(s32[1]{0:T(128)} %bitcast.1.first_ref, bf16[128,1024]{1,0:T(8,128)(2,1)S(1)} %copy.228.query_ref, bf16[1024,1024]{1,0:T(8,128)(2,1)S(1)} %bitcast.300, bf16[1024,1024]{1,0:T(8,128)(2,1)S(1)} %bitcast.301), custom_call_target="tpu_custom_call" | custom-call | flops 536870912 | bytes 4194304 | tf_op jit(solution)/shard_map/attend/pallas_call | solution.py:468
  117.7 4.0 convolution_convert_fusion
  121.6 10.6 %collective-permute-done.11.refs_in_order_6_ = bf16[3,2,128,512]{3,2,1,0:T(8,128)(2,1)} collective-permute-done((bf16[3,2,128,512]{3,2,1,0:T(8,128)(2,1)}, bf16[3,2,128,512]{3,2,1,0:T(8,128)(2,1)}, u32[]{:S(2)}, u32[]{:S(2)}) %collective-permute-start.11) | collective-permute-done | bytes 786464 | tf_op jit(solution)/shard_map/ppermute | solution.py:88
  132.2 4.5 all-to-all-start.1
  139.3 17.6 %collective-permute-done.12.refs_in_order_7_ = bf16[3,2,128,512]{3,2,1,0:T(8,128)(2,1)} collective-permute-done((bf16[3,2,128,512]{3,2,1,0:T(8,128)(2,1)}, bf16[3,2,128,512]{3,2,1,0:T(8,128)(2,1)}, u32[]{:S(2)}, u32[]{:S(2)}) %collective-permute-start.12) | collective-permute-done | bytes 786464 | tf_op jit(solution)/shard_map/ppermute | solution.py:88
  156.8 24.7 %all-to-all-done.1 = bf16[16,96,1152]{2,1,0:T(8,128)(2,1)} async-done(((bf16[16,96,1152]{2,1,0:T(8,128)(2,1)}), bf16[16,96,1152]{2,1,0:T(8,128)(2,1)}, u32[]{:S(2)}, u32[]{:S(2)}) %all-to-all-start.1) | async-done | bytes 3538976 | tf_op jit(solution)/shard_map/all_to_all | solution.py:67
  185.2 3.9 all-to-all-start.2
  189.2 26.8 %experts.1 = (bf16[16,2,48,1024]{3,2,1,0:T(8,128)(2,1)}, bf16[16,2,48,1152]{3,2,1,0:T(8,128)(2,1)}, bf16[4,2,1024,512]{3,2,1,0:T(8,128)(2,1)}) custom-call(s32[3]{0:T(128)} %pad_add_fusion.own_ref, bf16[16,2,48,1152]{3,2,1,0:T(8,128)(2,1)} %bitcast.38.arrived_ref, bf16[16,128,1152]{2,1,0:T(8,128)(2,1)} %bitcast.335, bf16[3,2,128,512]{3,2,1,0:T(8,128)(2,1)} %copy-done.31, ...), custom_call_target="tpu_custom_call" | custom-call | flops 14495514624 | bytes 31457280 | tf_op jit(solution)/shard_map/experts/pallas_call | solution.py:299
  216.6 7.3 %all-to-all-start.3 = ((bf16[16,96,1152]{2,1,0:T(8,128)(2,1)}), bf16[16,96,1152]{2,1,0:T(8,128)(2,1)}, u32[]{:S(2)}, u32[]{:S(2)}) async-start(bf16[16,96,1152]{2,1,0:T(8,128)(2,1)} %bitcast.309), calls=%async_computation.3 | async-start | bytes 7077888 | tf_op jit(solution)/shard_map/all_to_all | solution.py:67
  228.6 23.4 %collective-permute-done.14 = bf16[1024,512]{1,0:T(8,128)(2,1)S(1)} collective-permute-done((bf16[1024,512]{1,0:T(8,128)(2,1)S(1)}, bf16[1024,512]{1,0:T(8,128)(2,1)S(1)}, u32[]{:S(2)}, u32[]{:S(2)}) %collective-permute-start.14) | collective-permute-done | bytes 1048608 | tf_op jit(solution)/shard_map/ppermute | solution.py:88
  264.4 5.4 %all-to-all-done.3 = bf16[16,96,1152]{2,1,0:T(8,128)(2,1)} async-done(((bf16[16,96,1152]{2,1,0:T(8,128)(2,1)}), bf16[16,96,1152]{2,1,0:T(8,128)(2,1)}, u32[]{:S(2)}, u32[]{:S(2)}) %all-to-all-start.3) | async-done | bytes 3538976 | tf_op jit(solution)/shard_map/all_to_all | solution.py:67
  269.8 4.6 all-to-all-start.4
  281.3 26.5 %collective-permute-done.15 = bf16[2,1024,512]{2,1,0:T(8,128)(2,1)} collective-permute-done((bf16[2,1024,512]{2,1,0:T(8,128)(2,1)}, bf16[2,1024,512]{2,1,0:T(8,128)(2,1)}, u32[]{:S(2)}, u32[]{:S(2)}) %collective-permute-start.15) | collective-permute-done | bytes 2097184 | tf_op jit(solution)/shard_map/ppermute | solution.py:99
  310.0 3.8 fusion
  317.8 11.2 %attend_back.1 = (f32[128,1024]{1,0:T(8,128)S(1)}, bf16[1024,512]{1,0:T(8,128)(2,1)S(1)}, bf16[1024,512]{1,0:T(8,128)(2,1)S(1)}) custom-call(s32[1]{0:T(128)} %bitcast.1.first_ref, bf16[128,1024]{1,0:T(8,128)(2,1)S(1)} %copy.228.query_ref, bf16[1024,1024]{1,0:T(8,128)(2,1)S(1)} %bitcast.302, bf16[1024,1024]{1,0:T(8,128)(2,1)S(1)} %bitcast.303, ...), custom_call_target="tpu_custom_call" | custom-call | flops 1342177280 | bytes 4194304 | tf_op jit(solution)/shard_map/attend_back/pallas_call | solution.py:468
  330.7 5.9 %all-to-all-start.5 = ((bf16[8,128,1024]{2,1,0:T(8,128)(2,1)}), bf16[8,128,1024]{2,1,0:T(8,128)(2,1)}, u32[]{:S(2)}, u32[]{:S(2)}) async-start(bf16[8,128,1024]{2,1,0:T(8,128)(2,1)} %bitcast.58), calls=%async_computation.5 | async-start | bytes 4194304 | tf_op jit(solution)/shard_map/all_to_all | solution.py:67
  339.9 12.8 %collective-permute-done.17 = bf16[1024,512]{1,0:T(8,128)(2,1)} collective-permute-done((bf16[1024,512]{1,0:T(8,128)(2,1)}, bf16[1024,512]{1,0:T(8,128)(2,1)}, u32[]{:S(2)}, u32[]{:S(2)}) %collective-permute-start.17) | collective-permute-done | bytes 1048608 | tf_op jit(solution)/shard_map/ppermute | solution.py:88
  360.4 3.3 fusion.16
  363.7 10.1 %all-to-all-done.5 = bf16[8,128,1024]{2,1,0:T(8,128)(2,1)} async-done(((bf16[8,128,1024]{2,1,0:T(8,128)(2,1)}), bf16[8,128,1024]{2,1,0:T(8,128)(2,1)}, u32[]{:S(2)}, u32[]{:S(2)}) %all-to-all-start.5) | async-done | bytes 2097184 | tf_op jit(solution)/shard_map/all_to_all | solution.py:67
  378.4 3.6 fusion.54
  385.9 7.1 %all-to-all-start.6 = ((bf16[16,152,128]{2,1,0:T(8,128)(2,1)}), bf16[16,152,128]{2,1,0:T(8,128)(2,1)S(1)}, u32[]{:S(2)}, u32[]{:S(2)}) async-start(bf16[16,152,128]{2,1,0:T(8,128)(2,1)} %copy.243), calls=%async_computation.6 | async-start | bytes 1245184 | tf_op jit(solution)/shard_map/all_to_all | solution.py:67
  393.1 20.1 %owner.1 = (bf16[4,2,128,512]{3,2,1,0:T(8,128)(2,1)S(1)}, bf16[4,2,128,512]{3,2,1,0:T(8,128)(2,1)S(1)}) custom-call(s32[2]{0:T(128)S(1)} %pad_add_fusion.1.place_ref, bf16[1024,512]{1,0:T(8,128)(2,1)S(1)} %fusion.5.matrix_ref), custom_call_target="tpu_custom_call" | custom-call | flops 20937965568 | bytes 3145728 | tf_op jit(solution)/shard_map/owner/pallas_call | solution.py:377
  421.4 4.8 all-to-all-start.7
  427.2 12.2 %collective-permute-done.18 = bf16[4,2,128,512]{3,2,1,0:T(8,128)(2,1)} collective-permute-done((bf16[4,2,128,512]{3,2,1,0:T(8,128)(2,1)S(1)}, bf16[4,2,128,512]{3,2,1,0:T(8,128)(2,1)}, u32[]{:S(2)}, u32[]{:S(2)}) %collective-permute-start.18) | collective-permute-done | bytes 1048608 | tf_op jit(solution)/shard_map/ppermute | solution.py:88
  439.4 5.7 %all-to-all-done.7 = bf16[8,216,128]{2,1,0:T(8,128)(2,1)S(1)} async-done(((bf16[8,216,128]{2,1,0:T(8,128)(2,1)}), bf16[8,216,128]{2,1,0:T(8,128)(2,1)S(1)}, u32[]{:S(2)}, u32[]{:S(2)}) %all-to-all-start.7) | async-done | bytes 442400 | tf_op jit(solution)/shard_map/all_to_all | solution.py:67
  446.0 3.5 all-to-all-start.8
  471.7 9.4 %collective-permute-done.19 = bf16[2,2,128,512]{3,2,1,0:T(8,128)(2,1)} collective-permute-done((bf16[2,2,128,512]{3,2,1,0:T(8,128)(2,1)S(1)}, bf16[2,2,128,512]{3,2,1,0:T(8,128)(2,1)}, u32[]{:S(2)}, u32[]{:S(2)}) %collective-permute-start.19) | collective-permute-done | bytes 524320 | tf_op jit(solution)/shard_map/ppermute | solution.py:88
  (379 shorter events, 150.9 us)
Async XLA Ops:
  7.2 102.6 %all-gather.6.cloned.1.call-start = ((), (), s32[]{:S(2)}) async-start(), calls=%async_computation.9 | async-start | bytes 2228224 | tf_op jit(solution)/shard_map/all_gather | solution.py:565
  7.9 181.2 %all-gather.12.cloned.1.call-start = ((), (), s32[]{:S(2)}) async-start(), calls=%async_computation.12 | async-start | bytes 5013504 | tf_op jit(solution)/shard_map/all_gather | solution.py:582
  10.6 11.1 %collective-permute-start = (bf16[136,1024]{1,0:T(8,128)(2,1)S(1)}, bf16[136,1024]{1,0:T(8,128)(2,1)S(1)}, u32[]{:S(2)}, u32[]{:S(2)}) collective-permute-start(bf16[136,1024]{1,0:T(8,128)(2,1)S(1)} %fusion.71), channel_id=1, source_target_pairs={{0,2},{1,3},{2,0},{3,1},{4,6},{5,7},{6,4},{7,5},{8,10},{9,11},{10,... | collective-permute-start | bytes 835592 | tf_op jit(solution)/shard_map/ppermute | solution.py:109
  15.0 24.1 %collective-permute-start.3 = (bf16[3,2,128,512]{3,2,1,0:T(8,128)(2,1)S(1)}, bf16[3,2,128,512]{3,2,1,0:T(8,128)(2,1)}, u32[]{:S(2)}, u32[]{:S(2)}) collective-permute-start(bf16[3,2,128,512]{3,2,1,0:T(8,128)(2,1)S(1)} %pad_maximum_fusion.5.refs_in_order_0_), channel_id=1, source_target_pairs={{0,16},{16,0},{32,48},{48,32},{64,80},{80,64},{96,112},{112,96},{1... | collective-permute-start | bytes 2359304 | tf_op jit(solution)/shard_map/ppermute | solution.py:88
  15.7 23.4 %collective-permute-start.4 = (bf16[3,2,128,512]{3,2,1,0:T(8,128)(2,1)S(1)}, bf16[3,2,128,512]{3,2,1,0:T(8,128)(2,1)}, u32[]{:S(2)}, u32[]{:S(2)}) collective-permute-start(bf16[3,2,128,512]{3,2,1,0:T(8,128)(2,1)S(1)} %pad_maximum_fusion.5.refs_in_order_0_), channel_id=1, source_target_pairs={{0,32},{16,48},{32,64},{48,80},{64,96},{80,112},{96,0},{112,16},{1... | collective-permute-start | bytes 2359304 | tf_op jit(solution)/shard_map/ppermute | solution.py:88
  17.6 21.5 %collective-permute-start.5 = (bf16[3,2,128,512]{3,2,1,0:T(8,128)(2,1)S(1)}, bf16[3,2,128,512]{3,2,1,0:T(8,128)(2,1)}, u32[]{:S(2)}, u32[]{:S(2)}) collective-permute-start(bf16[3,2,128,512]{3,2,1,0:T(8,128)(2,1)S(1)} %pad_maximum_fusion.5.refs_in_order_0_), channel_id=1, source_target_pairs={{0,96},{16,112},{32,0},{48,16},{64,32},{80,48},{96,64},{112,80},{1... | collective-permute-start | bytes 2359304 | tf_op jit(solution)/shard_map/ppermute | solution.py:88
  22.1 17.1 %collective-permute-start.1 = (bf16[2,136,1024]{2,1,0:T(8,128)(2,1)S(1)}, bf16[2,136,1024]{2,1,0:T(8,128)(2,1)S(1)}, u32[]{:S(2)}, u32[]{:S(2)}) collective-permute-start(bf16[2,136,1024]{2,1,0:T(8,128)(2,1)S(1)} %get-tuple-element.145), channel_id=1, source_target_pairs={{0,4},{1,5},{2,6},{3,7},{4,8},{5,9},{6,10},{7,11},{8,12},{9,13},{1... | collective-permute-start | bytes 1671176 | tf_op jit(solution)/shard_map/ppermute | solution.py:109
  23.8 15.4 %collective-permute-start.2 = (bf16[2,136,1024]{2,1,0:T(8,128)(2,1)S(1)}, bf16[2,136,1024]{2,1,0:T(8,128)(2,1)S(1)}, u32[]{:S(2)}, u32[]{:S(2)}) collective-permute-start(bf16[2,136,1024]{2,1,0:T(8,128)(2,1)S(1)} %get-tuple-element.145), channel_id=1, source_target_pairs={{0,12},{1,13},{2,14},{3,15},{4,0},{5,1},{6,2},{7,3},{8,4},{9,5},{1... | collective-permute-start | bytes 1671176 | tf_op jit(solution)/shard_map/ppermute | solution.py:109
  65.6 37.0 %all-to-all-start = ((bf16[8,128,1024]{2,1,0:T(8,128)(2,1)}), bf16[8,128,1024]{2,1,0:T(8,128)(2,1)S(1)}, u32[]{:S(2)}, u32[]{:S(2)}) async-start(bf16[8,128,1024]{2,1,0:T(8,128)(2,1)} %broadcast_in_dim.45), calls=%async_computation | async-start | bytes 4194304 | tf_op jit(solution)/shard_map/all_to_all | solution.py:67
  73.0 48.6 %collective-permute-start.9 = (bf16[3,2,128,512]{3,2,1,0:T(8,128)(2,1)}, bf16[3,2,128,512]{3,2,1,0:T(8,128)(2,1)}, u32[]{:S(2)}, u32[]{:S(2)}) collective-permute-start(bf16[3,2,128,512]{3,2,1,0:T(8,128)(2,1)} %collective-permute-done.3.refs_in_order_1_), channel_id=1, source_target_pairs={{0,32},{16,48},{32,64},{48,80},{64,96},{80,112},{96,0},{112,16},{1... | collective-permute-start | bytes 2359304 | tf_op jit(solution)/shard_map/ppermute | solution.py:88
  75.1 46.6 %collective-permute-start.10 = (bf16[3,2,128,512]{3,2,1,0:T(8,128)(2,1)}, bf16[3,2,128,512]{3,2,1,0:T(8,128)(2,1)}, u32[]{:S(2)}, u32[]{:S(2)}) collective-permute-start(bf16[3,2,128,512]{3,2,1,0:T(8,128)(2,1)} %collective-permute-done.3.refs_in_order_1_), channel_id=1, source_target_pairs={{0,96},{16,112},{32,0},{48,16},{64,32},{80,48},{96,64},{112,80},{1... | collective-permute-start | bytes 2359304 | tf_op jit(solution)/shard_map/ppermute | solution.py:88
  76.3 55.9 %collective-permute-start.11 = (bf16[3,2,128,512]{3,2,1,0:T(8,128)(2,1)}, bf16[3,2,128,512]{3,2,1,0:T(8,128)(2,1)}, u32[]{:S(2)}, u32[]{:S(2)}) collective-permute-start(bf16[3,2,128,512]{3,2,1,0:T(8,128)(2,1)} %collective-permute-done.4.refs_in_order_2_), channel_id=1, source_target_pairs={{0,32},{16,48},{32,64},{48,80},{64,96},{80,112},{96,0},{112,16},{1... | collective-permute-start | bytes 2359304 | tf_op jit(solution)/shard_map/ppermute | solution.py:88
  132.2 49.3 %all-to-all-start.1 = ((bf16[16,96,1152]{2,1,0:T(8,128)(2,1)}), bf16[16,96,1152]{2,1,0:T(8,128)(2,1)}, u32[]{:S(2)}, u32[]{:S(2)}) async-start(bf16[16,96,1152]{2,1,0:T(8,128)(2,1)} %bitcast.307), calls=%async_computation.1 | async-start | bytes 7077888 | tf_op jit(solution)/shard_map/all_to_all | solution.py:67
  136.7 277.6 %all-gather.8.cloned.1.call-start = ((), (), s32[]{:S(2)}) async-start(), calls=%async_computation.10 | async-start | bytes 4456448 | tf_op jit(solution)/shard_map/all_gather | solution.py:625
  136.8 20.1 %collective-permute-start.12 = (bf16[3,2,128,512]{3,2,1,0:T(8,128)(2,1)}, bf16[3,2,128,512]{3,2,1,0:T(8,128)(2,1)}, u32[]{:S(2)}, u32[]{:S(2)}) collective-permute-start(bf16[3,2,128,512]{3,2,1,0:T(8,128)(2,1)} %collective-permute-done.10.refs_in_order_5_), channel_id=1, source_target_pairs={{0,96},{16,112},{32,0},{48,16},{64,32},{80,48},{96,64},{112,80},{1... | collective-permute-start | bytes 2359304 | tf_op jit(solution)/shard_map/ppermute | solution.py:88
  185.2 30.7 %all-to-all-start.2 = ((bf16[16,64,128]{2,1,0:T(8,128)(2,1)}), bf16[16,64,128]{2,1,0:T(8,128)(2,1)S(1)}, u32[]{:S(2)}, u32[]{:S(2)}) async-start(bf16[16,64,128]{2,1,0:T(8,128)(2,1)} %reshape.437), calls=%async_computation.2 | async-start | bytes 524288 | tf_op jit(solution)/shard_map/all_to_all | solution.py:67
  216.6 53.2 %all-to-all-start.3 = ((bf16[16,96,1152]{2,1,0:T(8,128)(2,1)}), bf16[16,96,1152]{2,1,0:T(8,128)(2,1)}, u32[]{:S(2)}, u32[]{:S(2)}) async-start(bf16[16,96,1152]{2,1,0:T(8,128)(2,1)} %bitcast.309), calls=%async_computation.3 | async-start | bytes 7077888 | tf_op jit(solution)/shard_map/all_to_all | solution.py:67
  226.5 25.5 %collective-permute-start.14 = (bf16[1024,512]{1,0:T(8,128)(2,1)S(1)}, bf16[1024,512]{1,0:T(8,128)(2,1)S(1)}, u32[]{:S(2)}, u32[]{:S(2)}) collective-permute-start(bf16[1024,512]{1,0:T(8,128)(2,1)S(1)} %get-tuple-element.103), channel_id=1, source_target_pairs={{0,96},{16,112},{32,0},{48,16},{64,32},{80,48},{96,64},{112,80},{1... | collective-permute-start | bytes 3145736 | tf_op jit(solution)/shard_map/ppermute | solution.py:88
  227.4 26.4 %collective-permute-start.13 = (bf16[1024,512]{1,0:T(8,128)(2,1)S(1)}, bf16[1024,512]{1,0:T(8,128)(2,1)S(1)}, u32[]{:S(2)}, u32[]{:S(2)}) collective-permute-start(bf16[1024,512]{1,0:T(8,128)(2,1)S(1)} %get-tuple-element.105), channel_id=1, source_target_pairs={{0,32},{16,48},{32,64},{48,80},{64,96},{80,112},{96,0},{112,16},{1... | collective-permute-start | bytes 3145736 | tf_op jit(solution)/shard_map/ppermute | solution.py:88
  257.4 50.4 %collective-permute-start.15 = (bf16[2,1024,512]{2,1,0:T(8,128)(2,1)}, bf16[2,1024,512]{2,1,0:T(8,128)(2,1)}, u32[]{:S(2)}, u32[]{:S(2)}) collective-permute-start(bf16[2,1024,512]{2,1,0:T(8,128)(2,1)} %pad_maximum_fusion.1), channel_id=1, source_target_pairs={{0,32},{16,48},{32,64},{48,80},{96,0},{112,16},{1,33},{17,49},{33,... | collective-permute-start | bytes 6291464 | tf_op jit(solution)/shard_map/ppermute | solution.py:99
  260.9 49.1 %collective-permute-start.16 = (bf16[2,1024,512]{2,1,0:T(8,128)(2,1)}, bf16[2,1024,512]{2,1,0:T(8,128)(2,1)}, u32[]{:S(2)}, u32[]{:S(2)}) collective-permute-start(bf16[2,1024,512]{2,1,0:T(8,128)(2,1)} %pad_maximum_fusion.2), channel_id=1, source_target_pairs={{32,0},{48,16},{64,32},{80,48},{96,64},{112,80},{33,1},{49,17},{65... | collective-permute-start | bytes 6291464 | tf_op jit(solution)/shard_map/ppermute | solution.py:99
  269.8 60.9 %all-to-all-start.4 = ((bf16[16,96,1024]{2,1,0:T(8,128)(2,1)}), bf16[16,96,1024]{2,1,0:T(8,128)(2,1)}, u32[]{:S(2)}, u32[]{:S(2)}) async-start(bf16[16,96,1024]{2,1,0:T(8,128)(2,1)} %bitcast.310), calls=%async_computation.4 | async-start | bytes 6291456 | tf_op jit(solution)/shard_map/all_to_all | solution.py:67
  274.4 143.0 %all-gather.10.cloned.1.call-start = ((), (), s32[]{:S(2)}) async-start(), calls=%async_computation.11 | async-start | bytes 4456448 | tf_op jit(solution)/shard_map/all_gather | solution.py:661
  315.0 37.8 %collective-permute-start.17 = (bf16[1024,512]{1,0:T(8,128)(2,1)}, bf16[1024,512]{1,0:T(8,128)(2,1)}, u32[]{:S(2)}, u32[]{:S(2)}) collective-permute-start(bf16[1024,512]{1,0:T(8,128)(2,1)} %fusion.31), channel_id=1, source_target_pairs={{0,16},{16,0},{32,48},{48,32},{64,80},{80,64},{96,112},{112,96},{1... | collective-permute-start | bytes 3145736 | tf_op jit(solution)/shard_map/ppermute | solution.py:88
  330.7 43.2 %all-to-all-start.5 = ((bf16[8,128,1024]{2,1,0:T(8,128)(2,1)}), bf16[8,128,1024]{2,1,0:T(8,128)(2,1)}, u32[]{:S(2)}, u32[]{:S(2)}) async-start(bf16[8,128,1024]{2,1,0:T(8,128)(2,1)} %bitcast.58), calls=%async_computation.5 | async-start | bytes 4194304 | tf_op jit(solution)/shard_map/all_to_all | solution.py:67
  385.9 28.2 %all-to-all-start.6 = ((bf16[16,152,128]{2,1,0:T(8,128)(2,1)}), bf16[16,152,128]{2,1,0:T(8,128)(2,1)S(1)}, u32[]{:S(2)}, u32[]{:S(2)}) async-start(bf16[16,152,128]{2,1,0:T(8,128)(2,1)} %copy.243), calls=%async_computation.6 | async-start | bytes 1245184 | tf_op jit(solution)/shard_map/all_to_all | solution.py:67
  413.2 26.1 %collective-permute-start.18 = (bf16[4,2,128,512]{3,2,1,0:T(8,128)(2,1)S(1)}, bf16[4,2,128,512]{3,2,1,0:T(8,128)(2,1)}, u32[]{:S(2)}, u32[]{:S(2)}) collective-permute-start(bf16[4,2,128,512]{3,2,1,0:T(8,128)(2,1)S(1)} %get-tuple-element.80), channel_id=1, source_target_pairs={{0,16},{16,0},{32,48},{48,32},{64,80},{80,64},{96,112},{112,96},{1... | collective-permute-start | bytes 3145736 | tf_op jit(solution)/shard_map/ppermute | solution.py:88
  421.4 23.7 %all-to-all-start.7 = ((bf16[8,216,128]{2,1,0:T(8,128)(2,1)}), bf16[8,216,128]{2,1,0:T(8,128)(2,1)S(1)}, u32[]{:S(2)}, u32[]{:S(2)}) async-start(bf16[8,216,128]{2,1,0:T(8,128)(2,1)} %pad_maximum_fusion.13), calls=%async_computation.7 | async-start | bytes 884736 | tf_op jit(solution)/shard_map/all_to_all | solution.py:67
  446.0 12.5 %all-to-all-start.8 = ((bf16[8,192,128]{2,1,0:T(8,128)(2,1)}), bf16[8,192,128]{2,1,0:T(8,128)(2,1)S(1)}, u32[]{:S(2)}, u32[]{:S(2)}) async-start(bf16[8,192,128]{2,1,0:T(8,128)(2,1)} %broadcast_in_dim.108), calls=%async_computation.8 | async-start | bytes 786432 | tf_op jit(solution)/shard_map/all_to_all | solution.py:67
  451.0 18.7 %collective-permute-start.21 = (bf16[2,2,128,512]{3,2,1,0:T(8,128)(2,1)S(1)}, bf16[2,2,128,512]{3,2,1,0:T(8,128)(2,1)}, u32[]{:S(2)}, u32[]{:S(2)}) collective-permute-start(bf16[2,2,128,512]{3,2,1,0:T(8,128)(2,1)S(1)} %pad_maximum_fusion.9), channel_id=1, source_target_pairs={{0,96},{16,112},{32,0},{48,16},{64,32},{80,48},{96,64},{112,80},{1... | collective-permute-start | bytes 1572872 | tf_op jit(solution)/shard_map/ppermute | solution.py:88
  455.0 16.7 %collective-permute-start.20 = (bf16[2,2,128,512]{3,2,1,0:T(8,128)(2,1)}, bf16[2,2,128,512]{3,2,1,0:T(8,128)(2,1)}, u32[]{:S(2)}, u32[]{:S(2)}) collective-permute-start(bf16[2,2,128,512]{3,2,1,0:T(8,128)(2,1)} %pad_maximum_fusion.8), channel_id=1, source_target_pairs={{0,64},{16,80},{32,96},{48,112},{64,0},{80,16},{96,32},{112,48},{1... | collective-permute-start | bytes 1572872 | tf_op jit(solution)/shard_map/ppermute | solution.py:88
  455.9 25.2 %collective-permute-start.19 = (bf16[2,2,128,512]{3,2,1,0:T(8,128)(2,1)S(1)}, bf16[2,2,128,512]{3,2,1,0:T(8,128)(2,1)}, u32[]{:S(2)}, u32[]{:S(2)}) collective-permute-start(bf16[2,2,128,512]{3,2,1,0:T(8,128)(2,1)S(1)} %pad_maximum_fusion.7), channel_id=1, source_target_pairs={{0,32},{16,48},{32,64},{48,80},{64,96},{80,112},{96,0},{112,16},{1... | collective-permute-start | bytes 1572872 | tf_op jit(solution)/shard_map/ppermute | solution.py:88
  (80 other events, 785.6 us)
Sparse Core Ops, SparseCore 0:
  10.5 51.7 all-gather.5
  65.3 59.3 all-gather.11
  181.7 64.9 all-gather.7
  279.7 81.5 all-gather.9

commit v6 on v5

--- a/solution.py
+++ b/solution.py
@@ -596,6 +596,7 @@
     keys = rotate(kv_raw[:, :KV], cosine, sine).astype(bf16)
     values = kv_raw[:, KV:].astype(bf16)
     sent_kv = jnp.concatenate([keys, values], axis=1).reshape(row_count, 2 * KV * HD)
+    sent_kv = after(sent_kv, far)
     all_kv = spread(sent_kv, "ctx", None, ctx_count).reshape(ctx_count * row_count, 2 * KV * HD)
     flat_queries = queries.reshape(row_count, HEADS * HD)
     mixed_low = attention_call(attend_kernel, (flat_queries, all_kv), None, first_row, "attend")
@@ -613,8 +614,8 @@
         [normed_two, *gate_parts, jnp.zeros((row_count, WIDE - 3 * EXPERTS), bf16)], axis=1
     )
     sent_rows = contract_rows(select, extended).astype(bf16)
-    sent_rows, below_other, above_other, far = lax.optimization_barrier(
-        (sent_rows, below_other, above_other, far)
+    sent_rows, below_other, above_other = lax.optimization_barrier(
+        (sent_rows, below_other, above_other)
     )
     far_other = ctx_move(above_other, 3, 0)
     arrived = exchange(sent_rows.reshape(exp_count, per_group * CAP, D + WIDE), "exp")
@@ -659,19 +660,20 @@
     )
     grad_attended = grad_residual.astype(bf16)
     all_attended = lax.all_gather(grad_attended, "exp", axis=0, tiled=True)
-    grad_attended = after(grad_attended, sum_up, sum_down)
+    grad_mixed = contract_cols(grad_attended, full_output).astype(bf16)
+    grad_queries, key_terms, value_terms = attention_call(
+        attend_back_kernel, (flat_queries, all_kv), grad_mixed, first_row, "attend_back"
+    )
+    kv_terms = jnp.concatenate([key_terms, value_terms], axis=1)
+    kv_terms, route_values, sum_up, sum_down = lax.optimization_barrier(
+        (kv_terms, route_values, sum_up, sum_down)
+    )
     both_sums = (
         expert_grads[0].astype(jnp.float32)
         + sum_up.astype(jnp.float32)
         + sum_down.astype(jnp.float32)
     )
     other_sums = ctx_move(both_sums[1].astype(bf16), 0, 1)
-    grad_mixed = contract_cols(grad_attended, full_output).astype(bf16)
-    grad_queries, key_terms, value_terms = attention_call(
-        attend_back_kernel, (flat_queries, all_kv), grad_mixed, first_row, "attend_back"
-    )
-    kv_terms = jnp.concatenate([key_terms, value_terms], axis=1)
-    kv_terms, route_values = lax.optimization_barrier((kv_terms, route_values))
     kv_terms = exchange(kv_terms.reshape(ctx_count, row_count, 2 * KV * HD), "ctx")
     grad_query_raw = rotate(
         grad_queries.reshape(row_count, HEADS, HD), cosine, -sine

time: 505 us -> 529 us (1.048)
  waiting for transfers between devices: 211 us -> 223 us
  local copies, waits for them, and re-layouts: 35.9 us -> 43.5 us
    all_to_all x9, waiting for transfers between devices: 64.1 us -> 81.6 us  [exchange(): lax.all_to_all(blocks, axis, split_axis=0, concat_axis=0, tiled=True, axi...]
    ppermute x2, waiting for transfers between devices: 28.7 us -> 18.5 us  [owner_move(): return lax.ppermute(block, 'ctx', pairs)]
    ppermute x14, waiting for transfers between devices: 104 us -> 113 us  [ctx_move(): return lax.ppermute(block, 'ctx', pairs)]
    unnamed x159 -> x125, local copies, waits for them, and re-layouts: 6.7 us -> 11.3 us
  transfers between devices with their start and end apart: 35 -> 35, of which waited for: 20 -> 16; matrix products, arithmetic and copies ran while one was open for 22% -> 22% of each run, Pallas kernels for 13% -> 13%
where the time goes in v6:
time: 529 us; the launch traced here: 521 us
  waiting for transfers between devices  223 us (42%)
  starting transfers between devices  83.1 us (16%)
  Pallas kernels  65.4 us (12%)
  other arithmetic  46.9 us (9%)
  matrix products  43.6 us (8%)
  local copies, waits for them, and re-layouts  43.5 us (8%)
  between operations  15.5 us (3%)
    ppermute x14, waiting for transfers between devices, ctx_move(): return lax.ppermute(block, 'ctx', pairs)  113 us
    all_to_all x9, waiting for transfers between devices, exchange(): lax.all_to_all(blocks, axis, split_axis=0, concat_axis=0, tiled=True, axi...  81.6 us
    all_to_all x9, starting transfers between devices, exchange(): lax.all_to_all(blocks, axis, split_axis=0, concat_axis=0, tiled=True, axi...  44.8 us
    pallas_call x1, Pallas kernels, expert_math(): pl.pallas_call(expert_kernel, grid_spec=pltpu.PrefetchScalarGridSpec(num_...  26.9 us
    dot_general x12, matrix products, mat(): return jnp.dot(left, right, preferred_element_type=jnp.float32)  24.9 us
    ppermute x14, starting transfers between devices, ctx_move(): return lax.ppermute(block, 'ctx', pairs)  22 us
    pallas_call x1, Pallas kernels, owner_orthogonal(): pl.pallas_call(owner_kernel, out_shape=[sent, sent], in_specs=[pl.BlockSp...  20.1 us
    ppermute x2, waiting for transfers between devices, owner_move(): return lax.ppermute(block, 'ctx', pairs)  18.5 us
  transfers between devices with their start and end apart: 35, of which 16 were waited for; matrix products, arithmetic and copies ran while one was open for 22% of the time, Pallas kernels for 13%

profile of v6, /device:TPU:0, one launch (start us, length us, event | category | flops | bytes accessed | tf_op | source)
XLA Modules:
  0.0 521.1 jit_solution(9117239692835050959)
XLA Ops:
  10.6 3.2 collective-permute-start
  25.4 13.8 %collective-permute-done.3.refs_in_order_1_ = bf16[3,2,128,512]{3,2,1,0:T(8,128)(2,1)} collective-permute-done((bf16[3,2,128,512]{3,2,1,0:T(8,128)(2,1)S(1)}, bf16[3,2,128,512]{3,2,1,0:T(8,128)(2,1)}, u32[]{:S(2)}, u32[]{:S(2)}) %collective-permute-start.3) | collective-permute-done | bytes 786464 | tf_op jit(solution)/shard_map/ppermute | solution.py:88
  42.6 5.5 %collective-permute-done.6 = bf16[136,1024]{1,0:T(8,128)(2,1)S(1)} collective-permute-done((bf16[136,1024]{1,0:T(8,128)(2,1)S(1)}, bf16[136,1024]{1,0:T(8,128)(2,1)S(1)}, u32[]{:S(2)}, u32[]{:S(2)}) %collective-permute-start.6) | collective-permute-done | bytes 278560 | tf_op jit(solution)/shard_map/ppermute | solution.py:109
  61.2 14.3 %collective-permute-done.9.refs_in_order_6_ = bf16[3,2,128,512]{3,2,1,0:T(8,128)(2,1)} collective-permute-done((bf16[3,2,128,512]{3,2,1,0:T(8,128)(2,1)}, bf16[3,2,128,512]{3,2,1,0:T(8,128)(2,1)}, u32[]{:S(2)}, u32[]{:S(2)}) %collective-permute-start.9) | collective-permute-done | bytes 786464 | tf_op jit(solution)/shard_map/ppermute | solution.py:88
  77.2 3.9 all-to-all-start
  93.7 22.8 %all-to-all-done = bf16[8,128,1024]{2,1,0:T(8,128)(2,1)S(1)} async-done(((bf16[8,128,1024]{2,1,0:T(8,128)(2,1)}), bf16[8,128,1024]{2,1,0:T(8,128)(2,1)S(1)}, u32[]{:S(2)}, u32[]{:S(2)}) %all-to-all-start) | async-done | bytes 2097184 | tf_op jit(solution)/shard_map/all_to_all | solution.py:67
  116.5 7.2 %attend.1 = bf16[128,1024]{1,0:T(8,128)(2,1)S(1)} custom-call(s32[1]{0:T(128)} %bitcast.1.first_ref, bf16[128,1024]{1,0:T(8,128)(2,1)S(1)} %copy.228.query_ref, bf16[1024,1024]{1,0:T(8,128)(2,1)S(1)} %bitcast.300, bf16[1024,1024]{1,0:T(8,128)(2,1)S(1)} %bitcast.301), custom_call_target="tpu_custom_call" | custom-call | flops 536870912 | bytes 4194304 | tf_op jit(solution)/shard_map/attend/pallas_call | solution.py:468
  132.2 4.0 convolution_convert_fusion
  136.2 4.7 all-to-all-start.1
  144.8 16.4 %collective-permute-done.12.refs_in_order_7_ = bf16[3,2,128,512]{3,2,1,0:T(8,128)(2,1)} collective-permute-done((bf16[3,2,128,512]{3,2,1,0:T(8,128)(2,1)}, bf16[3,2,128,512]{3,2,1,0:T(8,128)(2,1)}, u32[]{:S(2)}, u32[]{:S(2)}) %collective-permute-start.12) | collective-permute-done | bytes 786464 | tf_op jit(solution)/shard_map/ppermute | solution.py:88
  161.2 24.6 %all-to-all-done.1 = bf16[16,96,1152]{2,1,0:T(8,128)(2,1)} async-done(((bf16[16,96,1152]{2,1,0:T(8,128)(2,1)}), bf16[16,96,1152]{2,1,0:T(8,128)(2,1)}, u32[]{:S(2)}, u32[]{:S(2)}) %all-to-all-start.1) | async-done | bytes 3538976 | tf_op jit(solution)/shard_map/all_to_all | solution.py:67
  189.5 3.7 all-to-all-start.2
  193.2 26.9 %experts.1 = (bf16[16,2,48,1024]{3,2,1,0:T(8,128)(2,1)}, bf16[16,2,48,1152]{3,2,1,0:T(8,128)(2,1)}, bf16[4,2,1024,512]{3,2,1,0:T(8,128)(2,1)}) custom-call(s32[3]{0:T(128)} %pad_add_fusion.own_ref, bf16[16,2,48,1152]{3,2,1,0:T(8,128)(2,1)} %bitcast.38.arrived_ref, bf16[16,128,1152]{2,1,0:T(8,128)(2,1)} %bitcast.336, bf16[3,2,128,512]{3,2,1,0:T(8,128)(2,1)} %copy-done.33, ...), custom_call_target="tpu_custom_call" | custom-call | flops 14495514624 | bytes 31457280 | tf_op jit(solution)/shard_map/experts/pallas_call | solution.py:299
  220.8 7.3 %all-to-all-start.3 = ((bf16[16,96,1152]{2,1,0:T(8,128)(2,1)}), bf16[16,96,1152]{2,1,0:T(8,128)(2,1)}, u32[]{:S(2)}, u32[]{:S(2)}) async-start(bf16[16,96,1152]{2,1,0:T(8,128)(2,1)} %bitcast.309), calls=%async_computation.3 | async-start | bytes 7077888 | tf_op jit(solution)/shard_map/all_to_all | solution.py:67
  228.1 4.4 slice_bitcast_fusion.2
  236.4 23.1 %collective-permute-done.13 = bf16[1024,512]{1,0:T(8,128)(2,1)} collective-permute-done((bf16[1024,512]{1,0:T(8,128)(2,1)}, bf16[1024,512]{1,0:T(8,128)(2,1)}, u32[]{:S(2)}, u32[]{:S(2)}) %collective-permute-start.13) | collective-permute-done | bytes 1048608 | tf_op jit(solution)/shard_map/ppermute | solution.py:88
  265.3 8.8 %all-to-all-done.3 = bf16[16,96,1152]{2,1,0:T(8,128)(2,1)} async-done(((bf16[16,96,1152]{2,1,0:T(8,128)(2,1)}), bf16[16,96,1152]{2,1,0:T(8,128)(2,1)}, u32[]{:S(2)}, u32[]{:S(2)}) %all-to-all-start.3) | async-done | bytes 3538976 | tf_op jit(solution)/shard_map/all_to_all | solution.py:67
  274.1 4.6 all-to-all-start.4
  281.5 4.8 collective-permute-start.15
  297.7 11.2 %attend_back.1 = (f32[128,1024]{1,0:T(8,128)S(1)}, bf16[1024,512]{1,0:T(8,128)(2,1)S(1)}, bf16[1024,512]{1,0:T(8,128)(2,1)S(1)}) custom-call(s32[1]{0:T(128)} %bitcast.1.first_ref, bf16[128,1024]{1,0:T(8,128)(2,1)S(1)} %copy.228.query_ref, bf16[1024,1024]{1,0:T(8,128)(2,1)S(1)} %bitcast.302, bf16[1024,1024]{1,0:T(8,128)(2,1)S(1)} %bitcast.303, ...), custom_call_target="tpu_custom_call" | custom-call | flops 1342177280 | bytes 4194304 | tf_op jit(solution)/shard_map/attend_back/pallas_call | solution.py:468
  314.4 15.8 %collective-permute-done.16 = bf16[2,1024,512]{2,1,0:T(8,128)(2,1)} collective-permute-done((bf16[2,1024,512]{2,1,0:T(8,128)(2,1)}, bf16[2,1024,512]{2,1,0:T(8,128)(2,1)}, u32[]{:S(2)}, u32[]{:S(2)}) %collective-permute-start.16) | collective-permute-done | bytes 2097184 | tf_op jit(solution)/shard_map/ppermute | solution.py:99
  333.0 4.4 all-to-all-start.5
  337.4 3.8 fusion
  352.2 3.3 fusion.16
  355.4 34.9 %collective-permute-done.17 = bf16[1024,512]{1,0:T(8,128)(2,1)} collective-permute-done((bf16[1024,512]{1,0:T(8,128)(2,1)S(1)}, bf16[1024,512]{1,0:T(8,128)(2,1)}, u32[]{:S(2)}, u32[]{:S(2)}) %collective-permute-start.17) | collective-permute-done | bytes 1048608 | tf_op jit(solution)/shard_map/ppermute | solution.py:88
  403.0 6.6 %all-to-all-start.6 = ((bf16[16,152,128]{2,1,0:T(8,128)(2,1)}), bf16[16,152,128]{2,1,0:T(8,128)(2,1)S(1)}, u32[]{:S(2)}, u32[]{:S(2)}) async-start(bf16[16,152,128]{2,1,0:T(8,128)(2,1)} %copy.243), calls=%async_computation.6 | async-start | bytes 1245184 | tf_op jit(solution)/shard_map/all_to_all | solution.py:67
  409.6 20.1 %owner.1 = (bf16[4,2,128,512]{3,2,1,0:T(8,128)(2,1)S(1)}, bf16[4,2,128,512]{3,2,1,0:T(8,128)(2,1)S(1)}) custom-call(s32[2]{0:T(128)S(1)} %pad_add_fusion.1.place_ref, bf16[1024,512]{1,0:T(8,128)(2,1)S(1)} %fusion.5.matrix_ref), custom_call_target="tpu_custom_call" | custom-call | flops 20937965568 | bytes 3145728 | tf_op jit(solution)/shard_map/owner/pallas_call | solution.py:377
  438.9 5.5 %all-to-all-start.7 = ((bf16[8,216,128]{2,1,0:T(8,128)(2,1)}), bf16[8,216,128]{2,1,0:T(8,128)(2,1)S(1)}, u32[]{:S(2)}, u32[]{:S(2)}) async-start(bf16[8,216,128]{2,1,0:T(8,128)(2,1)} %pad_maximum_fusion.13), calls=%async_computation.7 | async-start | bytes 884736 | tf_op jit(solution)/shard_map/all_to_all | solution.py:67
  445.5 10.6 %collective-permute-done.18 = bf16[4,2,128,512]{3,2,1,0:T(8,128)(2,1)} collective-permute-done((bf16[4,2,128,512]{3,2,1,0:T(8,128)(2,1)S(1)}, bf16[4,2,128,512]{3,2,1,0:T(8,128)(2,1)}, u32[]{:S(2)}, u32[]{:S(2)}) %collective-permute-start.18) | collective-permute-done | bytes 1048608 | tf_op jit(solution)/shard_map/ppermute | solution.py:88
  456.1 5.5 %all-to-all-done.7 = bf16[8,216,128]{2,1,0:T(8,128)(2,1)S(1)} async-done(((bf16[8,216,128]{2,1,0:T(8,128)(2,1)}), bf16[8,216,128]{2,1,0:T(8,128)(2,1)S(1)}, u32[]{:S(2)}, u32[]{:S(2)}) %all-to-all-start.7) | async-done | bytes 442400 | tf_op jit(solution)/shard_map/all_to_all | solution.py:67
  468.4 4.1 all-to-all-start.8
  474.6 19.8 %all-to-all-done.8 = bf16[8,192,128]{2,1,0:T(8,128)(2,1)S(1)} async-done(((bf16[8,192,128]{2,1,0:T(8,128)(2,1)}), bf16[8,192,128]{2,1,0:T(8,128)(2,1)S(1)}, u32[]{:S(2)}, u32[]{:S(2)}) %all-to-all-start.8) | async-done | bytes 393248 | tf_op jit(solution)/shard_map/all_to_all | solution.py:67
  (345 shorter events, 156.1 us)
Async XLA Ops:
  7.2 116.6 %all-gather.6.cloned.1.call-start = ((), (), s32[]{:S(2)}) async-start(), calls=%async_computation.9 | async-start | bytes 2228224 | tf_op jit(solution)/shard_map/all_gather | solution.py:565
  7.9 185.3 %all-gather.12.cloned.1.call-start = ((), (), s32[]{:S(2)}) async-start(), calls=%async_computation.12 | async-start | bytes 5013504 | tf_op jit(solution)/shard_map/all_gather | solution.py:582
  10.6 11.1 %collective-permute-start = (bf16[136,1024]{1,0:T(8,128)(2,1)S(1)}, bf16[136,1024]{1,0:T(8,128)(2,1)S(1)}, u32[]{:S(2)}, u32[]{:S(2)}) collective-permute-start(bf16[136,1024]{1,0:T(8,128)(2,1)S(1)} %fusion.71), channel_id=1, source_target_pairs={{0,2},{1,3},{2,0},{3,1},{4,6},{5,7},{6,4},{7,5},{8,10},{9,11},{10,... | collective-permute-start | bytes 835592 | tf_op jit(solution)/shard_map/ppermute | solution.py:109
  15.0 24.1 %collective-permute-start.3 = (bf16[3,2,128,512]{3,2,1,0:T(8,128)(2,1)S(1)}, bf16[3,2,128,512]{3,2,1,0:T(8,128)(2,1)}, u32[]{:S(2)}, u32[]{:S(2)}) collective-permute-start(bf16[3,2,128,512]{3,2,1,0:T(8,128)(2,1)S(1)} %pad_maximum_fusion.5.refs_in_order_0_), channel_id=1, source_target_pairs={{0,16},{16,0},{32,48},{48,32},{64,80},{80,64},{96,112},{112,96},{1... | collective-permute-start | bytes 2359304 | tf_op jit(solution)/shard_map/ppermute | solution.py:88
  15.7 23.4 %collective-permute-start.4 = (bf16[3,2,128,512]{3,2,1,0:T(8,128)(2,1)S(1)}, bf16[3,2,128,512]{3,2,1,0:T(8,128)(2,1)}, u32[]{:S(2)}, u32[]{:S(2)}) collective-permute-start(bf16[3,2,128,512]{3,2,1,0:T(8,128)(2,1)S(1)} %pad_maximum_fusion.5.refs_in_order_0_), channel_id=1, source_target_pairs={{0,32},{16,48},{32,64},{48,80},{64,96},{80,112},{96,0},{112,16},{1... | collective-permute-start | bytes 2359304 | tf_op jit(solution)/shard_map/ppermute | solution.py:88
  17.6 21.5 %collective-permute-start.5 = (bf16[3,2,128,512]{3,2,1,0:T(8,128)(2,1)S(1)}, bf16[3,2,128,512]{3,2,1,0:T(8,128)(2,1)}, u32[]{:S(2)}, u32[]{:S(2)}) collective-permute-start(bf16[3,2,128,512]{3,2,1,0:T(8,128)(2,1)S(1)} %pad_maximum_fusion.5.refs_in_order_0_), channel_id=1, source_target_pairs={{0,96},{16,112},{32,0},{48,16},{64,32},{80,48},{96,64},{112,80},{1... | collective-permute-start | bytes 2359304 | tf_op jit(solution)/shard_map/ppermute | solution.py:88
  22.1 17.1 %collective-permute-start.1 = (bf16[2,136,1024]{2,1,0:T(8,128)(2,1)S(1)}, bf16[2,136,1024]{2,1,0:T(8,128)(2,1)S(1)}, u32[]{:S(2)}, u32[]{:S(2)}) collective-permute-start(bf16[2,136,1024]{2,1,0:T(8,128)(2,1)S(1)} %get-tuple-element.147), channel_id=1, source_target_pairs={{0,4},{1,5},{2,6},{3,7},{4,8},{5,9},{6,10},{7,11},{8,12},{9,13},{1... | collective-permute-start | bytes 1671176 | tf_op jit(solution)/shard_map/ppermute | solution.py:109
  23.8 15.4 %collective-permute-start.2 = (bf16[2,136,1024]{2,1,0:T(8,128)(2,1)S(1)}, bf16[2,136,1024]{2,1,0:T(8,128)(2,1)S(1)}, u32[]{:S(2)}, u32[]{:S(2)}) collective-permute-start(bf16[2,136,1024]{2,1,0:T(8,128)(2,1)S(1)} %get-tuple-element.147), channel_id=1, source_target_pairs={{0,12},{1,13},{2,14},{3,15},{4,0},{5,1},{6,2},{7,3},{8,4},{9,5},{1... | collective-permute-start | bytes 1671176 | tf_op jit(solution)/shard_map/ppermute | solution.py:109
  53.0 22.4 %collective-permute-start.9 = (bf16[3,2,128,512]{3,2,1,0:T(8,128)(2,1)}, bf16[3,2,128,512]{3,2,1,0:T(8,128)(2,1)}, u32[]{:S(2)}, u32[]{:S(2)}) collective-permute-start(bf16[3,2,128,512]{3,2,1,0:T(8,128)(2,1)} %collective-permute-done.4.refs_in_order_2_), channel_id=1, source_target_pairs={{0,32},{16,48},{32,64},{48,80},{64,96},{80,112},{96,0},{112,16},{1... | collective-permute-start | bytes 2359304 | tf_op jit(solution)/shard_map/ppermute | solution.py:88
  77.2 39.3 %all-to-all-start = ((bf16[8,128,1024]{2,1,0:T(8,128)(2,1)}), bf16[8,128,1024]{2,1,0:T(8,128)(2,1)S(1)}, u32[]{:S(2)}, u32[]{:S(2)}) async-start(bf16[8,128,1024]{2,1,0:T(8,128)(2,1)} %broadcast_in_dim.42), calls=%async_computation | async-start | bytes 4194304 | tf_op jit(solution)/shard_map/all_to_all | solution.py:67
  82.0 54.2 %collective-permute-start.10 = (bf16[3,2,128,512]{3,2,1,0:T(8,128)(2,1)}, bf16[3,2,128,512]{3,2,1,0:T(8,128)(2,1)}, u32[]{:S(2)}, u32[]{:S(2)}) collective-permute-start(bf16[3,2,128,512]{3,2,1,0:T(8,128)(2,1)} %collective-permute-done.3.refs_in_order_1_), channel_id=1, source_target_pairs={{0,32},{16,48},{32,64},{48,80},{64,96},{80,112},{96,0},{112,16},{1... | collective-permute-start | bytes 2359304 | tf_op jit(solution)/shard_map/ppermute | solution.py:88
  84.1 52.2 %collective-permute-start.11 = (bf16[3,2,128,512]{3,2,1,0:T(8,128)(2,1)}, bf16[3,2,128,512]{3,2,1,0:T(8,128)(2,1)}, u32[]{:S(2)}, u32[]{:S(2)}) collective-permute-start(bf16[3,2,128,512]{3,2,1,0:T(8,128)(2,1)} %collective-permute-done.3.refs_in_order_1_), channel_id=1, source_target_pairs={{0,96},{16,112},{32,0},{48,16},{64,32},{80,48},{96,64},{112,80},{1... | collective-permute-start | bytes 2359304 | tf_op jit(solution)/shard_map/ppermute | solution.py:88
  136.2 49.6 %all-to-all-start.1 = ((bf16[16,96,1152]{2,1,0:T(8,128)(2,1)}), bf16[16,96,1152]{2,1,0:T(8,128)(2,1)}, u32[]{:S(2)}, u32[]{:S(2)}) async-start(bf16[16,96,1152]{2,1,0:T(8,128)(2,1)} %bitcast.307), calls=%async_computation.1 | async-start | bytes 7077888 | tf_op jit(solution)/shard_map/all_to_all | solution.py:67
  140.9 290.1 %all-gather.8.cloned.1.call-start = ((), (), s32[]{:S(2)}) async-start(), calls=%async_computation.10 | async-start | bytes 4456448 | tf_op jit(solution)/shard_map/all_gather | solution.py:626
  141.0 20.2 %collective-permute-start.12 = (bf16[3,2,128,512]{3,2,1,0:T(8,128)(2,1)}, bf16[3,2,128,512]{3,2,1,0:T(8,128)(2,1)}, u32[]{:S(2)}, u32[]{:S(2)}) collective-permute-start(bf16[3,2,128,512]{3,2,1,0:T(8,128)(2,1)} %collective-permute-done.11.refs_in_order_5_), channel_id=1, source_target_pairs={{0,96},{16,112},{32,0},{48,16},{64,32},{80,48},{96,64},{112,80},{1... | collective-permute-start | bytes 2359304 | tf_op jit(solution)/shard_map/ppermute | solution.py:88
  189.5 30.6 %all-to-all-start.2 = ((bf16[16,64,128]{2,1,0:T(8,128)(2,1)}), bf16[16,64,128]{2,1,0:T(8,128)(2,1)S(1)}, u32[]{:S(2)}, u32[]{:S(2)}) async-start(bf16[16,64,128]{2,1,0:T(8,128)(2,1)} %reshape.441), calls=%async_computation.2 | async-start | bytes 524288 | tf_op jit(solution)/shard_map/all_to_all | solution.py:67
  220.8 53.3 %all-to-all-start.3 = ((bf16[16,96,1152]{2,1,0:T(8,128)(2,1)}), bf16[16,96,1152]{2,1,0:T(8,128)(2,1)}, u32[]{:S(2)}, u32[]{:S(2)}) async-start(bf16[16,96,1152]{2,1,0:T(8,128)(2,1)} %bitcast.309), calls=%async_computation.3 | async-start | bytes 7077888 | tf_op jit(solution)/shard_map/all_to_all | solution.py:67
  232.5 27.0 %collective-permute-start.13 = (bf16[1024,512]{1,0:T(8,128)(2,1)}, bf16[1024,512]{1,0:T(8,128)(2,1)}, u32[]{:S(2)}, u32[]{:S(2)}) collective-permute-start(bf16[1024,512]{1,0:T(8,128)(2,1)} %get-tuple-element.107), channel_id=1, source_target_pairs={{0,32},{16,48},{32,64},{48,80},{64,96},{80,112},{96,0},{112,16},{1... | collective-permute-start | bytes 3145736 | tf_op jit(solution)/shard_map/ppermute | solution.py:88
  233.9 25.6 %collective-permute-start.14 = (bf16[1024,512]{1,0:T(8,128)(2,1)}, bf16[1024,512]{1,0:T(8,128)(2,1)}, u32[]{:S(2)}, u32[]{:S(2)}) collective-permute-start(bf16[1024,512]{1,0:T(8,128)(2,1)} %get-tuple-element.105), channel_id=1, source_target_pairs={{0,96},{16,112},{32,0},{48,16},{64,32},{80,48},{96,64},{112,80},{1... | collective-permute-start | bytes 3145736 | tf_op jit(solution)/shard_map/ppermute | solution.py:88
  274.1 58.8 %all-to-all-start.4 = ((bf16[16,96,1024]{2,1,0:T(8,128)(2,1)}), bf16[16,96,1024]{2,1,0:T(8,128)(2,1)}, u32[]{:S(2)}, u32[]{:S(2)}) async-start(bf16[16,96,1024]{2,1,0:T(8,128)(2,1)} %bitcast.310), calls=%async_computation.4 | async-start | bytes 6291456 | tf_op jit(solution)/shard_map/all_to_all | solution.py:67
  278.7 156.2 %all-gather.10.cloned.1.call-start = ((), (), s32[]{:S(2)}) async-start(), calls=%async_computation.11 | async-start | bytes 4456448 | tf_op jit(solution)/shard_map/all_gather | solution.py:662
  280.1 50.1 %collective-permute-start.16 = (bf16[2,1024,512]{2,1,0:T(8,128)(2,1)}, bf16[2,1024,512]{2,1,0:T(8,128)(2,1)}, u32[]{:S(2)}, u32[]{:S(2)}) collective-permute-start(bf16[2,1024,512]{2,1,0:T(8,128)(2,1)} %pad_maximum_fusion.2), channel_id=1, source_target_pairs={{32,0},{48,16},{64,32},{80,48},{96,64},{112,80},{33,1},{49,17},{65... | collective-permute-start | bytes 6291464 | tf_op jit(solution)/shard_map/ppermute | solution.py:99
  281.5 51.4 %collective-permute-start.15 = (bf16[2,1024,512]{2,1,0:T(8,128)(2,1)}, bf16[2,1024,512]{2,1,0:T(8,128)(2,1)}, u32[]{:S(2)}, u32[]{:S(2)}) collective-permute-start(bf16[2,1024,512]{2,1,0:T(8,128)(2,1)} %pad_maximum_fusion.1), channel_id=1, source_target_pairs={{0,32},{16,48},{32,64},{48,80},{96,0},{112,16},{1,33},{17,49},{33,... | collective-permute-start | bytes 6291464 | tf_op jit(solution)/shard_map/ppermute | solution.py:99
  333.0 59.6 %all-to-all-start.5 = ((bf16[8,128,1024]{2,1,0:T(8,128)(2,1)}), bf16[8,128,1024]{2,1,0:T(8,128)(2,1)}, u32[]{:S(2)}, u32[]{:S(2)}) async-start(bf16[8,128,1024]{2,1,0:T(8,128)(2,1)} %bitcast.58), calls=%async_computation.5 | async-start | bytes 4194304 | tf_op jit(solution)/shard_map/all_to_all | solution.py:67
  343.3 47.0 %collective-permute-start.17 = (bf16[1024,512]{1,0:T(8,128)(2,1)S(1)}, bf16[1024,512]{1,0:T(8,128)(2,1)}, u32[]{:S(2)}, u32[]{:S(2)}) collective-permute-start(bf16[1024,512]{1,0:T(8,128)(2,1)S(1)} %fusion.31), channel_id=1, source_target_pairs={{0,16},{16,0},{32,48},{48,32},{64,80},{80,64},{96,112},{112,96},{1... | collective-permute-start | bytes 3145736 | tf_op jit(solution)/shard_map/ppermute | solution.py:88
  403.0 28.0 %all-to-all-start.6 = ((bf16[16,152,128]{2,1,0:T(8,128)(2,1)}), bf16[16,152,128]{2,1,0:T(8,128)(2,1)S(1)}, u32[]{:S(2)}, u32[]{:S(2)}) async-start(bf16[16,152,128]{2,1,0:T(8,128)(2,1)} %copy.243), calls=%async_computation.6 | async-start | bytes 1245184 | tf_op jit(solution)/shard_map/all_to_all | solution.py:67
  429.7 26.3 %collective-permute-start.18 = (bf16[4,2,128,512]{3,2,1,0:T(8,128)(2,1)S(1)}, bf16[4,2,128,512]{3,2,1,0:T(8,128)(2,1)}, u32[]{:S(2)}, u32[]{:S(2)}) collective-permute-start(bf16[4,2,128,512]{3,2,1,0:T(8,128)(2,1)S(1)} %get-tuple-element.82), channel_id=1, source_target_pairs={{0,16},{16,0},{32,48},{48,32},{64,80},{80,64},{96,112},{112,96},{1... | collective-permute-start | bytes 3145736 | tf_op jit(solution)/shard_map/ppermute | solution.py:88
  438.9 22.6 %all-to-all-start.7 = ((bf16[8,216,128]{2,1,0:T(8,128)(2,1)}), bf16[8,216,128]{2,1,0:T(8,128)(2,1)S(1)}, u32[]{:S(2)}, u32[]{:S(2)}) async-start(bf16[8,216,128]{2,1,0:T(8,128)(2,1)} %pad_maximum_fusion.13), calls=%async_computation.7 | async-start | bytes 884736 | tf_op jit(solution)/shard_map/all_to_all | solution.py:67
  463.9 42.2 %collective-permute-start.19 = (bf16[2,2,128,512]{3,2,1,0:T(8,128)(2,1)}, bf16[2,2,128,512]{3,2,1,0:T(8,128)(2,1)}, u32[]{:S(2)}, u32[]{:S(2)}) collective-permute-start(bf16[2,2,128,512]{3,2,1,0:T(8,128)(2,1)} %pad_maximum_fusion.7), channel_id=1, source_target_pairs={{0,32},{16,48},{32,64},{48,80},{64,96},{80,112},{96,0},{112,16},{1... | collective-permute-start | bytes 1572872 | tf_op jit(solution)/shard_map/ppermute | solution.py:88
  464.1 42.0 %collective-permute-start.20 = (bf16[2,2,128,512]{3,2,1,0:T(8,128)(2,1)S(1)}, bf16[2,2,128,512]{3,2,1,0:T(8,128)(2,1)}, u32[]{:S(2)}, u32[]{:S(2)}) collective-permute-start(bf16[2,2,128,512]{3,2,1,0:T(8,128)(2,1)S(1)} %pad_maximum_fusion.8), channel_id=1, source_target_pairs={{0,64},{16,80},{32,96},{48,112},{64,0},{80,16},{96,32},{112,48},{1... | collective-permute-start | bytes 1572872 | tf_op jit(solution)/shard_map/ppermute | solution.py:88
  467.0 39.2 %collective-permute-start.21 = (bf16[2,2,128,512]{3,2,1,0:T(8,128)(2,1)S(1)}, bf16[2,2,128,512]{3,2,1,0:T(8,128)(2,1)S(1)}, u32[]{:S(2)}, u32[]{:S(2)}) collective-permute-start(bf16[2,2,128,512]{3,2,1,0:T(8,128)(2,1)S(1)} %pad_maximum_fusion.9), channel_id=1, source_target_pairs={{0,96},{16,112},{32,0},{48,16},{64,32},{80,48},{96,64},{112,80},{1... | collective-permute-start | bytes 1572872 | tf_op jit(solution)/shard_map/ppermute | solution.py:88
  468.4 26.0 %all-to-all-start.8 = ((bf16[8,192,128]{2,1,0:T(8,128)(2,1)}), bf16[8,192,128]{2,1,0:T(8,128)(2,1)S(1)}, u32[]{:S(2)}, u32[]{:S(2)}) async-start(bf16[8,192,128]{2,1,0:T(8,128)(2,1)} %broadcast_in_dim.57), calls=%async_computation.8 | async-start | bytes 786432 | tf_op jit(solution)/shard_map/all_to_all | solution.py:67
  (63 other events, 526.4 us)
Sparse Core Ops, SparseCore 0:
  10.5 51.6 all-gather.5
  65.3 62.8 all-gather.11
  185.9 65.6 all-gather.7
  291.5 67.1 all-gather.9

commit v7 on v6

--- a/solution.py
+++ b/solution.py
@@ -596,7 +596,6 @@
     keys = rotate(kv_raw[:, :KV], cosine, sine).astype(bf16)
     values = kv_raw[:, KV:].astype(bf16)
     sent_kv = jnp.concatenate([keys, values], axis=1).reshape(row_count, 2 * KV * HD)
-    sent_kv = after(sent_kv, far)
     all_kv = spread(sent_kv, "ctx", None, ctx_count).reshape(ctx_count * row_count, 2 * KV * HD)
     flat_queries = queries.reshape(row_count, HEADS * HD)
     mixed_low = attention_call(attend_kernel, (flat_queries, all_kv), None, first_row, "attend")
@@ -619,7 +618,9 @@
     )
     far_other = ctx_move(above_other, 3, 0)
     arrived = exchange(sent_rows.reshape(exp_count, per_group * CAP, D + WIDE), "exp")
-    later_normed, arrived, far_other = lax.optimization_barrier((normed_one, arrived, far_other))
+    later_normed, arrived, far, far_other = lax.optimization_barrier(
+        (normed_one, arrived, far, far_other)
+    )
     full_experts = (
         own_experts, other_experts, below, below_other, above, above_other, far, far_other
     )
@@ -636,10 +637,11 @@
     returned = exchange(back.reshape(exp_count, per_group * CAP, D + WIDE), "exp")
     returned = returned.reshape(EXPERTS * CAP, D + WIDE)
     far_up, far_down = ctx_move(expert_grads[2, 0], 1, 0), ctx_move(expert_grads[2, 1], 3, 0)
-    sum_up = jnp.stack([plus(expert_grads[1, 0], far_up), expert_grads[1, 1]])
-    sum_down = jnp.stack([expert_grads[3, 0], plus(expert_grads[3, 1], far_down)])
-    returned = after(returned, sum_up, sum_down)
-    sum_up, sum_down = owner_move(sum_up, 1), owner_move(sum_down, 3)
+    added_up = plus(expert_grads[1, 0], far_up)
+    added_down = plus(expert_grads[3, 1], far_down)
+    returned = after(returned, added_up, added_down)
+    sum_up, sum_down = owner_move(expert_grads[1, 1], 1), owner_move(expert_grads[3, 0], 3)
+    added_up, added_down = owner_move(added_up, 1), owner_move(added_down, 3)
     produced = after(produced, returned)
     route_values = exchange(produced.reshape(exp_count, per_group * CAP, D), "exp")
     summed_back = mat(select, returned)
@@ -660,20 +662,20 @@
     )
     grad_attended = grad_residual.astype(bf16)
     all_attended = lax.all_gather(grad_attended, "exp", axis=0, tiled=True)
+    grad_attended = after(grad_attended, sum_up, sum_down)
     grad_mixed = contract_cols(grad_attended, full_output).astype(bf16)
     grad_queries, key_terms, value_terms = attention_call(
         attend_back_kernel, (flat_queries, all_kv), grad_mixed, first_row, "attend_back"
     )
     kv_terms = jnp.concatenate([key_terms, value_terms], axis=1)
-    kv_terms, route_values, sum_up, sum_down = lax.optimization_barrier(
-        (kv_terms, route_values, sum_up, sum_down)
-    )
-    both_sums = (
-        expert_grads[0].astype(jnp.float32)
-        + sum_up.astype(jnp.float32)
-        + sum_down.astype(jnp.float32)
-    )
-    other_sums = ctx_move(both_sums[1].astype(bf16), 0, 1)
+    kv_terms, added_up, added_down = lax.optimization_barrier((kv_terms, added_up, added_down))
+    both_sums = [
+        sum((part.astype(jnp.float32) for part in parts), expert_grads[0, slot].astype(jnp.float32))
+        for slot, parts in enumerate(((added_up, sum_down), (sum_up, added_down)))
+    ]
+    other_sums = both_sums[1].astype(bf16)
+    kv_terms = after(kv_terms, route_values, other_sums)
+    other_sums = ctx_move(other_sums, 0, 1)
     kv_terms = exchange(kv_terms.reshape(ctx_count, row_count, 2 * KV * HD), "ctx")
     grad_query_raw = rotate(
         grad_queries.reshape(row_count, HEADS, HD), cosine, -sine

time: 529 us -> 495 us (0.936)
  waiting for transfers between devices: 223 us -> 202 us
  local copies, waits for them, and re-layouts: 43.5 us -> 35.1 us
  other arithmetic: 46.9 us -> 41.2 us
    ppermute x14, waiting for transfers between devices: 113 us -> 83.8 us  [ctx_move(): return lax.ppermute(block, 'ctx', pairs)]
    all_to_all x9, waiting for transfers between devices: 81.6 us -> 103 us  [exchange(): lax.all_to_all(blocks, axis, split_axis=0, concat_axis=0, tiled=True, axi...]
    ppermute x2 -> x4, waiting for transfers between devices: 18.5 us -> 3.63 us  [owner_move(): return lax.ppermute(block, 'ctx', pairs)]
    convert_element_type x0 -> x2, other arithmetic: none -> 6.78 us  [the longest x1 3.49 us: plus(): (left.astype(jnp.float32) + right.astype(jnp.float32)).astype(jnp.bfloat16)]
    another operation x7 -> x4, other arithmetic: 6.01 us -> 0.24 us  [the longest x2 4.29 us: body(): jnp.stack([expert_grads[3, 0], plus(expert_grads[3, 1], far_down)])]
    unnamed x125 -> x147, local copies, waits for them, and re-layouts: 11.3 us -> 7.3 us
  transfers between devices with their start and end apart: 35 -> 37, of which waited for: 16 -> 17; matrix products, arithmetic and copies ran while one was open for 22% -> 22% of each run, Pallas kernels for 13% -> 13%
where the time goes in v7:
time: 495 us; the launch traced here: 487 us
  waiting for transfers between devices  202 us (41%)
  starting transfers between devices  82.4 us (17%)
  Pallas kernels  65.4 us (13%)
  matrix products  44.5 us (9%)
  other arithmetic  41.2 us (8%)
  local copies, waits for them, and re-layouts  35.1 us (7%)
  between operations  15.8 us (3%)
    all_to_all x9, waiting for transfers between devices, exchange(): lax.all_to_all(blocks, axis, split_axis=0, concat_axis=0, tiled=True, axi...  103 us
    ppermute x14, waiting for transfers between devices, ctx_move(): return lax.ppermute(block, 'ctx', pairs)  83.8 us
    all_to_all x9, starting transfers between devices, exchange(): lax.all_to_all(blocks, axis, split_axis=0, concat_axis=0, tiled=True, axi...  46.7 us
    pallas_call x1, Pallas kernels, expert_math(): pl.pallas_call(expert_kernel, grid_spec=pltpu.PrefetchScalarGridSpec(num_...  26.8 us
    dot_general x12, matrix products, mat(): return jnp.dot(left, right, preferred_element_type=jnp.float32)  25.5 us
    pallas_call x1, Pallas kernels, owner_orthogonal(): pl.pallas_call(owner_kernel, out_shape=[sent, sent], in_specs=[pl.BlockSp...  20.1 us
    ppermute x14, starting transfers between devices, ctx_move(): return lax.ppermute(block, 'ctx', pairs)  19 us
    pallas_call x2, Pallas kernels, attention_call(): pl.pallas_call(kernel, grid_spec=pltpu.PrefetchScalarGridSpec(num_scalar_...  18.4 us
  transfers between devices with their start and end apart: 37, of which 17 were waited for; matrix products, arithmetic and copies ran while one was open for 22% of the time, Pallas kernels for 13%

profile of v7, /device:TPU:0, one launch (start us, length us, event | category | flops | bytes accessed | tf_op | source)
XLA Modules:
  0.0 486.6 jit_solution(6639915295792455445)
XLA Ops:
  25.4 13.7 %collective-permute-done.3.refs_in_order_1_ = bf16[3,2,128,512]{3,2,1,0:T(8,128)(2,1)S(1)} collective-permute-done((bf16[3,2,128,512]{3,2,1,0:T(8,128)(2,1)S(1)}, bf16[3,2,128,512]{3,2,1,0:T(8,128)(2,1)S(1)}, u32[]{:S(2)}, u32[]{:S(2)}) %collective-permute-start.3) | collective-permute-done | bytes 786464 | tf_op jit(solution)/shard_map/ppermute | solution.py:88
  42.5 5.5 %collective-permute-done.6 = bf16[136,1024]{1,0:T(8,128)(2,1)S(1)} collective-permute-done((bf16[136,1024]{1,0:T(8,128)(2,1)S(1)}, bf16[136,1024]{1,0:T(8,128)(2,1)S(1)}, u32[]{:S(2)}, u32[]{:S(2)}) %collective-permute-start.6) | collective-permute-done | bytes 278560 | tf_op jit(solution)/shard_map/ppermute | solution.py:109
  61.9 6.5 %all-to-all-start = ((bf16[8,128,1024]{2,1,0:T(8,128)(2,1)}), bf16[8,128,1024]{2,1,0:T(8,128)(2,1)S(1)}, u32[]{:S(2)}, u32[]{:S(2)}) async-start(bf16[8,128,1024]{2,1,0:T(8,128)(2,1)} %broadcast_in_dim.45), calls=%async_computation | async-start | bytes 4194304 | tf_op jit(solution)/shard_map/all_to_all | solution.py:67
  79.6 19.4 %all-to-all-done = bf16[8,128,1024]{2,1,0:T(8,128)(2,1)S(1)} async-done(((bf16[8,128,1024]{2,1,0:T(8,128)(2,1)}), bf16[8,128,1024]{2,1,0:T(8,128)(2,1)S(1)}, u32[]{:S(2)}, u32[]{:S(2)}) %all-to-all-start) | async-done | bytes 2097184 | tf_op jit(solution)/shard_map/all_to_all | solution.py:67
  99.0 7.2 %attend.1 = bf16[128,1024]{1,0:T(8,128)(2,1)S(1)} custom-call(s32[1]{0:T(128)} %bitcast.1.first_ref, bf16[128,1024]{1,0:T(8,128)(2,1)S(1)} %copy.228.query_ref, bf16[1024,1024]{1,0:T(8,128)(2,1)S(1)} %bitcast.291, bf16[1024,1024]{1,0:T(8,128)(2,1)S(1)} %bitcast.292), custom_call_target="tpu_custom_call" | custom-call | flops 536870912 | bytes 4194304 | tf_op jit(solution)/shard_map/attend/pallas_call | solution.py:468
  114.7 4.0 convolution_convert_fusion
  118.7 4.7 all-to-all-start.1
  128.3 16.6 %collective-permute-done.11.refs_in_order_6_ = bf16[3,2,128,512]{3,2,1,0:T(8,128)(2,1)} collective-permute-done((bf16[3,2,128,512]{3,2,1,0:T(8,128)(2,1)}, bf16[3,2,128,512]{3,2,1,0:T(8,128)(2,1)}, u32[]{:S(2)}, u32[]{:S(2)}) %collective-permute-start.11) | collective-permute-done | bytes 786464 | tf_op jit(solution)/shard_map/ppermute | solution.py:88
  144.9 23.4 %all-to-all-done.1 = bf16[16,96,1152]{2,1,0:T(8,128)(2,1)} async-done(((bf16[16,96,1152]{2,1,0:T(8,128)(2,1)}), bf16[16,96,1152]{2,1,0:T(8,128)(2,1)}, u32[]{:S(2)}, u32[]{:S(2)}) %all-to-all-start.1) | async-done | bytes 3538976 | tf_op jit(solution)/shard_map/all_to_all | solution.py:67
  171.9 3.7 all-to-all-start.2
  175.7 26.8 %experts.1 = (bf16[16,2,48,1024]{3,2,1,0:T(8,128)(2,1)}, bf16[16,2,48,1152]{3,2,1,0:T(8,128)(2,1)}, bf16[4,2,1024,512]{3,2,1,0:T(8,128)(2,1)}) custom-call(s32[3]{0:T(128)} %pad_add_fusion.own_ref, bf16[16,2,48,1152]{3,2,1,0:T(8,128)(2,1)} %bitcast.37.arrived_ref, bf16[16,128,1152]{2,1,0:T(8,128)(2,1)} %bitcast.326, bf16[3,2,128,512]{3,2,1,0:T(8,128)(2,1)} %copy-done.31, ...), custom_call_target="tpu_custom_call" | custom-call | flops 14495514624 | bytes 31457280 | tf_op jit(solution)/shard_map/experts/pallas_call | solution.py:299
  203.2 7.3 %all-to-all-start.3 = ((bf16[16,96,1152]{2,1,0:T(8,128)(2,1)}), bf16[16,96,1152]{2,1,0:T(8,128)(2,1)}, u32[]{:S(2)}, u32[]{:S(2)}) async-start(bf16[16,96,1152]{2,1,0:T(8,128)(2,1)} %bitcast.300), calls=%async_computation.3 | async-start | bytes 7077888 | tf_op jit(solution)/shard_map/all_to_all | solution.py:67
  210.6 3.8 slice_bitcast_fusion
  220.8 20.7 %collective-permute-done.13 = bf16[1024,512]{1,0:T(8,128)(2,1)S(1)} collective-permute-done((bf16[1024,512]{1,0:T(8,128)(2,1)S(1)}, bf16[1024,512]{1,0:T(8,128)(2,1)S(1)}, u32[]{:S(2)}, u32[]{:S(2)}) %collective-permute-start.13) | collective-permute-done | bytes 1048608 | tf_op jit(solution)/shard_map/ppermute | solution.py:88
  241.6 3.5 fusion.12
  248.3 8.1 %all-to-all-done.3 = bf16[16,96,1152]{2,1,0:T(8,128)(2,1)} async-done(((bf16[16,96,1152]{2,1,0:T(8,128)(2,1)}), bf16[16,96,1152]{2,1,0:T(8,128)(2,1)}, u32[]{:S(2)}, u32[]{:S(2)}) %all-to-all-start.3) | async-done | bytes 3538976 | tf_op jit(solution)/shard_map/all_to_all | solution.py:67
  256.4 4.6 all-to-all-start.4
  269.5 11.2 %attend_back.1 = (f32[128,1024]{1,0:T(8,128)S(1)}, bf16[1024,512]{1,0:T(8,128)(2,1)S(1)}, bf16[1024,512]{1,0:T(8,128)(2,1)S(1)}) custom-call(s32[1]{0:T(128)} %bitcast.1.first_ref, bf16[128,1024]{1,0:T(8,128)(2,1)S(1)} %copy.228.query_ref, bf16[1024,1024]{1,0:T(8,128)(2,1)S(1)} %bitcast.293, bf16[1024,1024]{1,0:T(8,128)(2,1)S(1)} %bitcast.294, ...), custom_call_target="tpu_custom_call" | custom-call | flops 1342177280 | bytes 4194304 | tf_op jit(solution)/shard_map/attend_back/pallas_call | solution.py:468
  282.4 3.6 collective-permute-done.17
  290.9 13.9 %all-to-all-done.4 = bf16[16,96,1024]{2,1,0:T(8,128)(2,1)} async-done(((bf16[16,96,1024]{2,1,0:T(8,128)(2,1)}), bf16[16,96,1024]{2,1,0:T(8,128)(2,1)}, u32[]{:S(2)}, u32[]{:S(2)}) %all-to-all-start.4) | async-done | bytes 3145760 | tf_op jit(solution)/shard_map/all_to_all | solution.py:67
  304.8 4.9 %all-to-all-start.5 = ((bf16[8,128,1024]{2,1,0:T(8,128)(2,1)}), bf16[8,128,1024]{2,1,0:T(8,128)(2,1)}, u32[]{:S(2)}, u32[]{:S(2)}) async-start(bf16[8,128,1024]{2,1,0:T(8,128)(2,1)} %bitcast.57), calls=%async_computation.5 | async-start | bytes 4194304 | tf_op jit(solution)/shard_map/all_to_all | solution.py:67
  313.8 20.0 %collective-permute-done.19 = bf16[1024,512]{1,0:T(8,128)(2,1)S(1)} collective-permute-done((bf16[1024,512]{1,0:T(8,128)(2,1)}, bf16[1024,512]{1,0:T(8,128)(2,1)S(1)}, u32[]{:S(2)}, u32[]{:S(2)}) %collective-permute-start.19) | collective-permute-done | bytes 1048608 | tf_op jit(solution)/shard_map/ppermute | solution.py:88
  341.5 3.4 fusion.18
  344.8 13.0 %all-to-all-done.5 = bf16[8,128,1024]{2,1,0:T(8,128)(2,1)} async-done(((bf16[8,128,1024]{2,1,0:T(8,128)(2,1)}), bf16[8,128,1024]{2,1,0:T(8,128)(2,1)}, u32[]{:S(2)}, u32[]{:S(2)}) %all-to-all-start.5) | async-done | bytes 2097184 | tf_op jit(solution)/shard_map/all_to_all | solution.py:67
  362.3 3.6 fusion.53
  369.9 6.9 %all-to-all-start.6 = ((bf16[16,152,128]{2,1,0:T(8,128)(2,1)}), bf16[16,152,128]{2,1,0:T(8,128)(2,1)S(1)}, u32[]{:S(2)}, u32[]{:S(2)}) async-start(bf16[16,152,128]{2,1,0:T(8,128)(2,1)} %copy.243), calls=%async_computation.6 | async-start | bytes 1245184 | tf_op jit(solution)/shard_map/all_to_all | solution.py:67
  376.8 20.1 %owner.1 = (bf16[4,2,128,512]{3,2,1,0:T(8,128)(2,1)S(1)}, bf16[4,2,128,512]{3,2,1,0:T(8,128)(2,1)S(1)}) custom-call(s32[2]{0:T(128)S(1)} %pad_add_fusion.1.place_ref, bf16[1024,512]{1,0:T(8,128)(2,1)S(1)} %fusion.9.matrix_ref), custom_call_target="tpu_custom_call" | custom-call | flops 20937965568 | bytes 3145728 | tf_op jit(solution)/shard_map/owner/pallas_call | solution.py:377
  405.3 4.1 all-to-all-start.7
  410.5 12.8 %collective-permute-done.20 = bf16[4,2,128,512]{3,2,1,0:T(8,128)(2,1)} collective-permute-done((bf16[4,2,128,512]{3,2,1,0:T(8,128)(2,1)S(1)}, bf16[4,2,128,512]{3,2,1,0:T(8,128)(2,1)}, u32[]{:S(2)}, u32[]{:S(2)}) %collective-permute-start.20) | collective-permute-done | bytes 1048608 | tf_op jit(solution)/shard_map/ppermute | solution.py:88
  423.3 5.0 %all-to-all-done.7 = bf16[8,216,128]{2,1,0:T(8,128)(2,1)S(1)} async-done(((bf16[8,216,128]{2,1,0:T(8,128)(2,1)}), bf16[8,216,128]{2,1,0:T(8,128)(2,1)S(1)}, u32[]{:S(2)}, u32[]{:S(2)}) %all-to-all-start.7) | async-done | bytes 442400 | tf_op jit(solution)/shard_map/all_to_all | solution.py:67
  434.6 3.9 all-to-all-start.8
  439.8 20.5 %all-to-all-done.8 = bf16[8,192,128]{2,1,0:T(8,128)(2,1)S(1)} async-done(((bf16[8,192,128]{2,1,0:T(8,128)(2,1)}), bf16[8,192,128]{2,1,0:T(8,128)(2,1)S(1)}, u32[]{:S(2)}, u32[]{:S(2)}) %all-to-all-start.8) | async-done | bytes 393248 | tf_op jit(solution)/shard_map/all_to_all | solution.py:67
  (368 shorter events, 144.3 us)
Async XLA Ops:
  7.2 99.0 %all-gather.6.cloned.1.call-start = ((), (), s32[]{:S(2)}) async-start(), calls=%async_computation.9 | async-start | bytes 2228224 | tf_op jit(solution)/shard_map/all_gather | solution.py:565
  7.9 167.7 %all-gather.12.cloned.1.call-start = ((), (), s32[]{:S(2)}) async-start(), calls=%async_computation.12 | async-start | bytes 5013504 | tf_op jit(solution)/shard_map/all_gather | solution.py:582
  15.0 24.0 %collective-permute-start.3 = (bf16[3,2,128,512]{3,2,1,0:T(8,128)(2,1)S(1)}, bf16[3,2,128,512]{3,2,1,0:T(8,128)(2,1)S(1)}, u32[]{:S(2)}, u32[]{:S(2)}) collective-permute-start(bf16[3,2,128,512]{3,2,1,0:T(8,128)(2,1)S(1)} %pad_maximum_fusion.3.refs_in_order_0_), channel_id=1, source_target_pairs={{0,16},{16,0},{32,48},{48,32},{64,80},{80,64},{96,112},{112,96},{1... | collective-permute-start | bytes 2359304 | tf_op jit(solution)/shard_map/ppermute | solution.py:88
  15.7 23.3 %collective-permute-start.4 = (bf16[3,2,128,512]{3,2,1,0:T(8,128)(2,1)S(1)}, bf16[3,2,128,512]{3,2,1,0:T(8,128)(2,1)S(1)}, u32[]{:S(2)}, u32[]{:S(2)}) collective-permute-start(bf16[3,2,128,512]{3,2,1,0:T(8,128)(2,1)S(1)} %pad_maximum_fusion.3.refs_in_order_0_), channel_id=1, source_target_pairs={{0,32},{16,48},{32,64},{48,80},{64,96},{80,112},{96,0},{112,16},{1... | collective-permute-start | bytes 2359304 | tf_op jit(solution)/shard_map/ppermute | solution.py:88
  17.6 21.4 %collective-permute-start.5 = (bf16[3,2,128,512]{3,2,1,0:T(8,128)(2,1)S(1)}, bf16[3,2,128,512]{3,2,1,0:T(8,128)(2,1)}, u32[]{:S(2)}, u32[]{:S(2)}) collective-permute-start(bf16[3,2,128,512]{3,2,1,0:T(8,128)(2,1)S(1)} %pad_maximum_fusion.3.refs_in_order_0_), channel_id=1, source_target_pairs={{0,96},{16,112},{32,0},{48,16},{64,32},{80,48},{96,64},{112,80},{1... | collective-permute-start | bytes 2359304 | tf_op jit(solution)/shard_map/ppermute | solution.py:88
  22.1 17.0 %collective-permute-start.1 = (bf16[2,136,1024]{2,1,0:T(8,128)(2,1)S(1)}, bf16[2,136,1024]{2,1,0:T(8,128)(2,1)S(1)}, u32[]{:S(2)}, u32[]{:S(2)}) collective-permute-start(bf16[2,136,1024]{2,1,0:T(8,128)(2,1)S(1)} %get-tuple-element.149), channel_id=1, source_target_pairs={{0,4},{1,5},{2,6},{3,7},{4,8},{5,9},{6,10},{7,11},{8,12},{9,13},{1... | collective-permute-start | bytes 1671176 | tf_op jit(solution)/shard_map/ppermute | solution.py:109
  61.9 37.0 %all-to-all-start = ((bf16[8,128,1024]{2,1,0:T(8,128)(2,1)}), bf16[8,128,1024]{2,1,0:T(8,128)(2,1)S(1)}, u32[]{:S(2)}, u32[]{:S(2)}) async-start(bf16[8,128,1024]{2,1,0:T(8,128)(2,1)} %broadcast_in_dim.45), calls=%async_computation | async-start | bytes 4194304 | tf_op jit(solution)/shard_map/all_to_all | solution.py:67
  69.4 49.3 %collective-permute-start.10 = (bf16[3,2,128,512]{3,2,1,0:T(8,128)(2,1)}, bf16[3,2,128,512]{3,2,1,0:T(8,128)(2,1)}, u32[]{:S(2)}, u32[]{:S(2)}) collective-permute-start(bf16[3,2,128,512]{3,2,1,0:T(8,128)(2,1)} %copy-done.69), channel_id=1, source_target_pairs={{0,96},{16,112},{32,0},{48,16},{64,32},{80,48},{96,64},{112,80},{1... | collective-permute-start | bytes 2359304 | tf_op jit(solution)/shard_map/ppermute | solution.py:88
  72.6 46.0 %collective-permute-start.9 = (bf16[3,2,128,512]{3,2,1,0:T(8,128)(2,1)}, bf16[3,2,128,512]{3,2,1,0:T(8,128)(2,1)}, u32[]{:S(2)}, u32[]{:S(2)}) collective-permute-start(bf16[3,2,128,512]{3,2,1,0:T(8,128)(2,1)} %copy-done.69), channel_id=1, source_target_pairs={{0,32},{16,48},{32,64},{48,80},{64,96},{80,112},{96,0},{112,16},{1... | collective-permute-start | bytes 2359304 | tf_op jit(solution)/shard_map/ppermute | solution.py:88
  118.7 49.6 %all-to-all-start.1 = ((bf16[16,96,1152]{2,1,0:T(8,128)(2,1)}), bf16[16,96,1152]{2,1,0:T(8,128)(2,1)}, u32[]{:S(2)}, u32[]{:S(2)}) async-start(bf16[16,96,1152]{2,1,0:T(8,128)(2,1)} %bitcast.298), calls=%async_computation.1 | async-start | bytes 7077888 | tf_op jit(solution)/shard_map/all_to_all | solution.py:67
  123.4 274.8 %all-gather.8.cloned.1.call-start = ((), (), s32[]{:S(2)}) async-start(), calls=%async_computation.10 | async-start | bytes 4456448 | tf_op jit(solution)/shard_map/all_gather | solution.py:627
  123.5 21.4 %collective-permute-start.11 = (bf16[3,2,128,512]{3,2,1,0:T(8,128)(2,1)}, bf16[3,2,128,512]{3,2,1,0:T(8,128)(2,1)}, u32[]{:S(2)}, u32[]{:S(2)}) collective-permute-start(bf16[3,2,128,512]{3,2,1,0:T(8,128)(2,1)} %copy-done.70), channel_id=1, source_target_pairs={{0,32},{16,48},{32,64},{48,80},{64,96},{80,112},{96,0},{112,16},{1... | collective-permute-start | bytes 2359304 | tf_op jit(solution)/shard_map/ppermute | solution.py:88
  123.8 21.1 %collective-permute-start.12 = (bf16[3,2,128,512]{3,2,1,0:T(8,128)(2,1)}, bf16[3,2,128,512]{3,2,1,0:T(8,128)(2,1)}, u32[]{:S(2)}, u32[]{:S(2)}) collective-permute-start(bf16[3,2,128,512]{3,2,1,0:T(8,128)(2,1)} %collective-permute-done.10.refs_in_order_5_), channel_id=1, source_target_pairs={{0,96},{16,112},{32,0},{48,16},{64,32},{80,48},{96,64},{112,80},{1... | collective-permute-start | bytes 2359304 | tf_op jit(solution)/shard_map/ppermute | solution.py:88
  171.9 30.6 %all-to-all-start.2 = ((bf16[16,64,128]{2,1,0:T(8,128)(2,1)}), bf16[16,64,128]{2,1,0:T(8,128)(2,1)S(1)}, u32[]{:S(2)}, u32[]{:S(2)}) async-start(bf16[16,64,128]{2,1,0:T(8,128)(2,1)} %reshape.438), calls=%async_computation.2 | async-start | bytes 524288 | tf_op jit(solution)/shard_map/all_to_all | solution.py:67
  203.2 53.2 %all-to-all-start.3 = ((bf16[16,96,1152]{2,1,0:T(8,128)(2,1)}), bf16[16,96,1152]{2,1,0:T(8,128)(2,1)}, u32[]{:S(2)}, u32[]{:S(2)}) async-start(bf16[16,96,1152]{2,1,0:T(8,128)(2,1)} %bitcast.300), calls=%async_computation.3 | async-start | bytes 7077888 | tf_op jit(solution)/shard_map/all_to_all | solution.py:67
  214.4 27.2 %collective-permute-start.13 = (bf16[1024,512]{1,0:T(8,128)(2,1)S(1)}, bf16[1024,512]{1,0:T(8,128)(2,1)S(1)}, u32[]{:S(2)}, u32[]{:S(2)}) collective-permute-start(bf16[1024,512]{1,0:T(8,128)(2,1)S(1)} %get-tuple-element.109), channel_id=1, source_target_pairs={{0,32},{16,48},{32,64},{48,80},{64,96},{80,112},{96,0},{112,16},{1... | collective-permute-start | bytes 3145736 | tf_op jit(solution)/shard_map/ppermute | solution.py:88
  214.5 27.0 %collective-permute-start.14 = (bf16[1024,512]{1,0:T(8,128)(2,1)S(1)}, bf16[1024,512]{1,0:T(8,128)(2,1)S(1)}, u32[]{:S(2)}, u32[]{:S(2)}) collective-permute-start(bf16[1024,512]{1,0:T(8,128)(2,1)S(1)} %get-tuple-element.108), channel_id=1, source_target_pairs={{0,96},{16,112},{32,0},{48,16},{64,32},{80,48},{96,64},{112,80},{1... | collective-permute-start | bytes 3145736 | tf_op jit(solution)/shard_map/ppermute | solution.py:88
  217.6 49.3 %collective-permute-start.15 = (bf16[1024,512]{1,0:T(8,128)(2,1)}, bf16[1024,512]{1,0:T(8,128)(2,1)}, u32[]{:S(2)}, u32[]{:S(2)}) collective-permute-start(bf16[1024,512]{1,0:T(8,128)(2,1)} %get-tuple-element.107), channel_id=1, source_target_pairs={{0,32},{16,48},{32,64},{48,80},{96,0},{112,16},{1,33},{17,49},{33,... | collective-permute-start | bytes 3145736 | tf_op jit(solution)/shard_map/ppermute | solution.py:99
  219.5 47.4 %collective-permute-start.16 = (bf16[1024,512]{1,0:T(8,128)(2,1)}, bf16[1024,512]{1,0:T(8,128)(2,1)}, u32[]{:S(2)}, u32[]{:S(2)}) collective-permute-start(bf16[1024,512]{1,0:T(8,128)(2,1)} %get-tuple-element.106), channel_id=1, source_target_pairs={{32,0},{48,16},{64,32},{80,48},{96,64},{112,80},{33,1},{49,17},{65... | collective-permute-start | bytes 3145736 | tf_op jit(solution)/shard_map/ppermute | solution.py:99
  245.1 41.0 %collective-permute-start.17 = (bf16[1024,512]{1,0:T(8,128)(2,1)}, bf16[1024,512]{1,0:T(8,128)(2,1)}, u32[]{:S(2)}, u32[]{:S(2)}) collective-permute-start(bf16[1024,512]{1,0:T(8,128)(2,1)} %get-tuple-element.111), channel_id=1, source_target_pairs={{0,32},{16,48},{32,64},{48,80},{96,0},{112,16},{1,33},{17,49},{33,... | collective-permute-start | bytes 3145736 | tf_op jit(solution)/shard_map/ppermute | solution.py:99
  247.0 39.0 %collective-permute-start.18 = (bf16[1024,512]{1,0:T(8,128)(2,1)}, bf16[1024,512]{1,0:T(8,128)(2,1)}, u32[]{:S(2)}, u32[]{:S(2)}) collective-permute-start(bf16[1024,512]{1,0:T(8,128)(2,1)} %get-tuple-element.110), channel_id=1, source_target_pairs={{32,0},{48,16},{64,32},{80,48},{96,64},{112,80},{33,1},{49,17},{65... | collective-permute-start | bytes 3145736 | tf_op jit(solution)/shard_map/ppermute | solution.py:99
  256.4 48.4 %all-to-all-start.4 = ((bf16[16,96,1024]{2,1,0:T(8,128)(2,1)}), bf16[16,96,1024]{2,1,0:T(8,128)(2,1)}, u32[]{:S(2)}, u32[]{:S(2)}) async-start(bf16[16,96,1024]{2,1,0:T(8,128)(2,1)} %bitcast.301), calls=%async_computation.4 | async-start | bytes 6291456 | tf_op jit(solution)/shard_map/all_to_all | solution.py:67
  261.0 140.3 %all-gather.10.cloned.1.call-start = ((), (), s32[]{:S(2)}) async-start(), calls=%async_computation.11 | async-start | bytes 4456448 | tf_op jit(solution)/shard_map/all_gather | solution.py:664
  289.3 44.5 %collective-permute-start.19 = (bf16[1024,512]{1,0:T(8,128)(2,1)}, bf16[1024,512]{1,0:T(8,128)(2,1)S(1)}, u32[]{:S(2)}, u32[]{:S(2)}) collective-permute-start(bf16[1024,512]{1,0:T(8,128)(2,1)} %fusion.11), channel_id=1, source_target_pairs={{0,16},{16,0},{32,48},{48,32},{64,80},{80,64},{96,112},{112,96},{1... | collective-permute-start | bytes 3145736 | tf_op jit(solution)/shard_map/ppermute | solution.py:88
  304.8 53.0 %all-to-all-start.5 = ((bf16[8,128,1024]{2,1,0:T(8,128)(2,1)}), bf16[8,128,1024]{2,1,0:T(8,128)(2,1)}, u32[]{:S(2)}, u32[]{:S(2)}) async-start(bf16[8,128,1024]{2,1,0:T(8,128)(2,1)} %bitcast.57), calls=%async_computation.5 | async-start | bytes 4194304 | tf_op jit(solution)/shard_map/all_to_all | solution.py:67
  369.9 28.2 %all-to-all-start.6 = ((bf16[16,152,128]{2,1,0:T(8,128)(2,1)}), bf16[16,152,128]{2,1,0:T(8,128)(2,1)S(1)}, u32[]{:S(2)}, u32[]{:S(2)}) async-start(bf16[16,152,128]{2,1,0:T(8,128)(2,1)} %copy.243), calls=%async_computation.6 | async-start | bytes 1245184 | tf_op jit(solution)/shard_map/all_to_all | solution.py:67
  397.0 26.3 %collective-permute-start.20 = (bf16[4,2,128,512]{3,2,1,0:T(8,128)(2,1)S(1)}, bf16[4,2,128,512]{3,2,1,0:T(8,128)(2,1)}, u32[]{:S(2)}, u32[]{:S(2)}) collective-permute-start(bf16[4,2,128,512]{3,2,1,0:T(8,128)(2,1)S(1)} %get-tuple-element.84), channel_id=1, source_target_pairs={{0,16},{16,0},{32,48},{48,32},{64,80},{80,64},{96,112},{112,96},{1... | collective-permute-start | bytes 3145736 | tf_op jit(solution)/shard_map/ppermute | solution.py:88
  405.3 23.0 %all-to-all-start.7 = ((bf16[8,216,128]{2,1,0:T(8,128)(2,1)}), bf16[8,216,128]{2,1,0:T(8,128)(2,1)S(1)}, u32[]{:S(2)}, u32[]{:S(2)}) async-start(bf16[8,216,128]{2,1,0:T(8,128)(2,1)} %pad_maximum_fusion.11), calls=%async_computation.7 | async-start | bytes 884736 | tf_op jit(solution)/shard_map/all_to_all | solution.py:67
  429.8 41.7 %collective-permute-start.21 = (bf16[2,2,128,512]{3,2,1,0:T(8,128)(2,1)S(1)}, bf16[2,2,128,512]{3,2,1,0:T(8,128)(2,1)}, u32[]{:S(2)}, u32[]{:S(2)}) collective-permute-start(bf16[2,2,128,512]{3,2,1,0:T(8,128)(2,1)S(1)} %pad_maximum_fusion.5), channel_id=1, source_target_pairs={{0,32},{16,48},{32,64},{48,80},{64,96},{80,112},{96,0},{112,16},{1... | collective-permute-start | bytes 1572872 | tf_op jit(solution)/shard_map/ppermute | solution.py:88
  430.6 40.9 %collective-permute-start.22 = (bf16[2,2,128,512]{3,2,1,0:T(8,128)(2,1)S(1)}, bf16[2,2,128,512]{3,2,1,0:T(8,128)(2,1)}, u32[]{:S(2)}, u32[]{:S(2)}) collective-permute-start(bf16[2,2,128,512]{3,2,1,0:T(8,128)(2,1)S(1)} %pad_maximum_fusion.6), channel_id=1, source_target_pairs={{0,64},{16,80},{32,96},{48,112},{64,0},{80,16},{96,32},{112,48},{1... | collective-permute-start | bytes 1572872 | tf_op jit(solution)/shard_map/ppermute | solution.py:88
  432.7 38.8 %collective-permute-start.23 = (bf16[2,2,128,512]{3,2,1,0:T(8,128)(2,1)S(1)}, bf16[2,2,128,512]{3,2,1,0:T(8,128)(2,1)}, u32[]{:S(2)}, u32[]{:S(2)}) collective-permute-start(bf16[2,2,128,512]{3,2,1,0:T(8,128)(2,1)S(1)} %pad_maximum_fusion.7), channel_id=1, source_target_pairs={{0,96},{16,112},{32,0},{48,16},{64,32},{80,48},{96,64},{112,80},{1... | collective-permute-start | bytes 1572872 | tf_op jit(solution)/shard_map/ppermute | solution.py:88
  434.6 25.8 %all-to-all-start.8 = ((bf16[8,192,128]{2,1,0:T(8,128)(2,1)}), bf16[8,192,128]{2,1,0:T(8,128)(2,1)S(1)}, u32[]{:S(2)}, u32[]{:S(2)}) async-start(bf16[8,192,128]{2,1,0:T(8,128)(2,1)} %broadcast_in_dim.108), calls=%async_computation.8 | async-start | bytes 786432 | tf_op jit(solution)/shard_map/all_to_all | solution.py:67
  (76 other events, 955.2 us)
Sparse Core Ops, SparseCore 0:
  10.5 51.6 all-gather.5
  65.3 59.6 all-gather.11
  168.4 64.5 all-gather.7
  266.5 78.8 all-gather.9
